TPU v7x, 32 devices: a whole 2x2x4 slice. The times are simulated.
32 devices in a mesh: ctx: 8 (over z, x), rep: 4 (over y, core).
Axes of the slice: x: 2, y: 2, z: 4, core: 2. Of those that a mesh axis runs over, the one named last changes fastest.
Arguments:
- queries: bfloat16 [8, 2, 128, 192], P('rep', None, 'ctx'), parts along dimension 0, may hold values from -6 to 6
- key_absorb: bfloat16 [128, 128, 512], P('ctx'), may hold values from -0.5 to 0.5
- latent_cache: bfloat16 [8, 32768, 576], P('rep', 'ctx'), parts along dimension 0, may hold values from -600 to 600
- page_order: int32 [8, 256], P('rep', 'ctx'), parts along dimension 0, may hold values from 0 to 255, each once within a row
- lengths: int32 [8], P('rep'), parts along dimension 0, may hold values from 8192 to 32768
- kerple_scale: float32 [128], replicated, may hold values from 0.05 to 2
- kerple_rate: float32 [128], replicated, may hold values from 0.005 to 0.5
- value_up: bfloat16 [128, 512, 128], P('ctx'), may hold values from -0.25 to 0.25
- output_weight: bfloat16 [16384, 7168], P('ctx'), may hold values from -0.0625 to 0.0625
Outputs:
- attn_out: bfloat16 [8, 2, 7168], P('rep', None, 'ctx'), parts along dimension 0
There are 4 independent parts, one for each index of `rep`. A program takes and returns all parts, laid end to end along the dimension named above; an argument that names none is the same for every part. Nothing has to cross between parts.
All inputs are finite; a program needn't handle non-finite values.
Results may differ from a plain program's by a relative error of at most 0.015.
Values may be sent and summed in bfloat16 or wider, within the bound.
No kernel may reach another device: no remote copies, remote signals or barrier semaphores. Data moves between devices by JAX's collectives and lax.ppermute only.
A program may use at most 192 MiB of HBM per device.

v0:
```python
import jax
import jax.numpy as jnp
from jax import lax
from jax.sharding import PartitionSpec as P

NOPE = 128
ROPE = 64
LAT = 512
PAGE = 128


masked_score = -1e30


def block_terms(full_query, cache_block, key_pos, query_pos, kerple_scale, kerple_rate):
    distance = query_pos[:, :, None] - key_pos[:, None, :]
    visible = (distance >= 0)[:, :, None, :]
    spread = jnp.maximum(distance, 0).astype(jnp.float32)[:, :, None, :]
    log_bias = kerple_scale[:, None] * jnp.log1p(kerple_rate[:, None] * spread)
    softmax_scale = (NOPE + ROPE) ** (-0.5)
    scores = jnp.einsum(
        "bqhc,btc->bqht", full_query, cache_block, preferred_element_type=jnp.float32
    )
    scores = jnp.where(visible, scores * softmax_scale - log_bias, masked_score)
    row_max = jnp.max(scores, axis=-1)
    weights = jnp.where(visible, jnp.exp(scores - row_max[..., None]), 0.0)
    row_total = jnp.sum(weights, axis=-1)
    summed = jnp.einsum(
        "bqht,btc->bqhc",
        weights.astype(jnp.bfloat16),
        cache_block[..., :LAT],
        preferred_element_type=jnp.float32,
    )
    return (row_max, row_total, summed)


def per_device(
    queries,
    key_absorb,
    latent_cache,
    page_order,
    lengths,
    kerple_scale,
    kerple_rate,
    value_up,
    output_weight,
):
    requests, query_len, local_heads, _ = queries.shape
    keys_dev = latent_cache.shape[1]
    latent_query = jnp.einsum(
        "bqhn,hnc->bqhc", queries[..., :NOPE], key_absorb, preferred_element_type=jnp.float32
    ).astype(jnp.bfloat16)
    own_query = jnp.concatenate([latent_query, queries[..., NOPE:]], axis=-1)
    full_query = lax.all_gather(own_query, "ctx", axis=2, tiled=True)
    offsets = jnp.arange(PAGE, dtype=jnp.int32)
    key_pos = (page_order[:, :, None] * PAGE + offsets[None, None, :]).reshape(requests, keys_dev)
    query_pos = lengths[:, None] - query_len + jnp.arange(query_len, dtype=jnp.int32)[None, :]
    partial_terms = block_terms(
        full_query, latent_cache, key_pos, query_pos, kerple_scale, kerple_rate
    )
    row_max, row_total, summed = partial_terms
    global_max = lax.pmax(row_max, "ctx")
    factor = jnp.exp(row_max - global_max)
    shared_total, shared_sum = (
        lax.psum_scatter(row_total * factor, "ctx", scatter_dimension=2, tiled=True),
        lax.psum_scatter(summed * factor[..., None], "ctx", scatter_dimension=2, tiled=True),
    )
    attn_latent = (shared_sum / shared_total[..., None]).astype(jnp.bfloat16)
    up_values = jnp.einsum(
        "bqhc,hcv->bqhv", attn_latent, value_up, preferred_element_type=jnp.float32
    ).astype(jnp.bfloat16)
    flat_values = up_values.reshape(requests * query_len, local_heads * up_values.shape[-1])
    partial_out = jnp.dot(flat_values, output_weight, preferred_element_type=jnp.float32).reshape(
        requests, query_len, output_weight.shape[1]
    )
    return lax.psum_scatter(partial_out, "ctx", scatter_dimension=2, tiled=True).astype(
        jnp.bfloat16
    )


def solution(mesh):
    in_specs = (
        P("rep", None, "ctx", None),
        P("ctx", None, None),
        P("rep", "ctx", None),
        P("rep", "ctx"),
        P("rep"),
        P(),
        P(),
        P("ctx", None, None),
        P("ctx", None),
    )
    out_specs = P("rep", None, "ctx")
    return jax.shard_map(
        per_device, mesh=mesh, in_specs=in_specs, out_specs=out_specs, check_vma=False
    )
```

profile of v0, /device:TPU:0, one launch (start us, length us, event | category | flops | bytes accessed | tf_op | source)
XLA Modules:
  0.0 341.8 jit_solution(9713386593606058490)
XLA Ops:
  6.5 0.0 copy-start
  6.5 0.0 reduce-scatter.7.cloned.1.call-start
  6.5 0.9 slice.9
  7.4 0.7 slice.10
  8.1 0.7 broadcast_add_fusion
  8.8 0.1 iota_add_fusion
  8.9 0.7 broadcast_multiply_fusion
  9.5 0.1 broadcast_bitcast_fusion
  9.7 0.1 subtract_compare_fusion
  9.8 0.1 fusion.39
  9.9 0.0 copy-done
  9.9 0.4 fusion.27
  10.3 0.1 pad_maximum_fusion
  10.4 33.4 %all_gather.3 = bf16[2,2,128,576]{3,1,0,2:T(2,128)(2,1)S(1)} all-gather(bf16[2,2,16,576]{3,1,0,2:T(2,128)(2,1)S(1)} %pad_maximum_fusion), channel_id=1, replica_groups=mesh['ctx'=8,'rep'=4] {'ctx'}, dimensions={2}, use_global_device_ids=true | all-gather | bytes 663552 | tf_op jit(solution)/shard_map/all_gather | solution.py:54
  43.8 13.0 %fusion.47 = (f32[2,2,128]{2,1,0:T(2,128)S(1)}, f32[2,2,128,4096]{3,2,1,0:T(8,128)}) fusion(f32[2,2,4096]{2,1,0:T(2,128)S(1)} %fusion.39, f32[128]{0:T(128)} %param.15, f32[128]{0:T(128)} %param.14, bf16[2,4096,576]{1,2,0:T(8,128)(2,1)} %param.11, bf16[2,2,128,576]{3,1,0,2:T(2,128)(2,1)S(1)} %all_gather.3, pred[2,2,4096]{2,1,0:T(4,128)(4,1)S(1)} %subtract_compare_fusion), kind=kOutput, calls=%fused_computation.44 | convolution fusion | flops 2428501504 | bytes 18500608 | tf_op jit(solution)/shard_map/bqhc,btc->bqht/dot_general | solution.py:21
  56.9 21.4 %pmax.7 = f32[2,2,128]{2,1,0:T(2,128)S(1)} all-reduce(f32[2,2,128]{2,1,0:T(2,128)S(1)} %get-tuple-element.7), channel_id=1, replica_groups=mesh['ctx'=8,'rep'=4] {'ctx'}, use_global_device_ids=true, to_apply=%region_1.2 | all-reduce | flops 512 | bytes 4096 | tf_op jit(solution)/shard_map/pmax | solution.py:62
  78.2 5.1 %fusion.7 = f32[2,2,128]{2,1,0:T(2,128)S(1)} fusion(f32[2,2,128,4096]{3,2,1,0:T(8,128)} %get-tuple-element.8, f32[2,2,128]{2,1,0:T(2,128)S(1)} %get-tuple-element.7, pred[2,2,4096]{2,1,0:T(4,128)(4,1)S(1)} %subtract_compare_fusion), kind=kLoop, calls=%fused_computation.9 | loop fusion | flops 6290944 | bytes 8409088 | tf_op jit(solution)/shard_map/reduce_sum | solution.py:27
  83.4 0.2 copy.33
  83.5 0.8 reshape.56
  84.3 0.0 reduce-scatter.7.cloned.1.call-update
  84.3 0.0 all-reduce.3.cloned.1.call-start
  84.4 0.0 copy-start.2
  84.4 8.2 %fusion.19 = f32[2,2,128,512]{3,2,1,0:T(8,128)S(1)} fusion(bf16[2,4096,576]{1,2,0:T(8,128)(2,1)} %param.11, f32[2,2,128,4096]{3,2,1,0:T(8,128)} %get-tuple-element.8, f32[2,2,128]{2,1,0:T(2,128)S(1)} %get-tuple-element.7, pred[2,2,4096]{2,1,0:T(4,128)(4,1)S(1)} %subtract_compare_fusion, f32[2,2,128]{2,1,0:T(2,128)S(1)} %get-tuple-element.6), kind=kOutput, calls=%fused_computation.18 | convolution fusion | flops 2154037248 | bytes 17846272 | tf_op jit(solution)/shard_map/bqht,btc->bqhc/dot_general | solution.py:28
  92.6 1.8 copy.26
  94.4 0.0 all-reduce.3.cloned.1.call-update
  94.4 0.2 reduce-scatter.9.cloned.1.call-start
  94.7 0.0 copy-done.2
  94.7 0.6 dynamic-slice
  95.9 47.1 %reduce-scatter.7.cloned.1.call-done = f32[16,4]{1,0:T(8,128)} async-done(((f32[128,4]{1,0:T(8,128)}), f32[16,4]{1,0:T(8,128)}) %reduce-scatter.7.cloned.1.call-update) | async-done | bytes 272
  143.0 0.8 reshape.57
  143.8 79.8 %all-reduce.3.cloned.1.call-done = f32[2,2,128,512]{3,1,0,2:T(2,128)} async-done(((f32[2,2,128,512]{3,1,0,2:T(2,128)}), f32[2,2,128,512]{3,1,0,2:T(2,128)}) %all-reduce.3.cloned.1.call-update) | async-done | bytes 1048592
  223.6 2.1 fusion.33
  225.8 11.5 %fusion = f32[2,2,7168]{2,1,0:T(2,128)S(1)} fusion(bf16[2048,7168]{1,0:T(8,128)(2,1)} %param.17, bf16[16,2,1,2,128]{4,3,2,1,0:T(2,128)(2,1)S(1)} %fusion.33), kind=kOutput, calls=%fused_computation | convolution fusion | flops 117440512 | bytes 29491200 | tf_op jit(solution)/shard_map/dot_general | solution.py:73
  237.3 0.0 copy-start.1
  237.3 6.9 %copy.35 = f32[2,2,7168]{1,0,2:T(2,128)} copy(f32[2,2,7168]{2,1,0:T(2,128)S(1)} %fusion) | data formatting | bytes 229376
  244.2 7.9 %reshape.58 = f32[7168,4]{1,0:T(8,128)} reshape(f32[7168,2,2]{2,1,0:T(2,128)} %bitcast.57) | data formatting | bytes 229376
  252.1 0.0 reduce-scatter.9.cloned.1.call-update
  252.1 80.6 %reduce-scatter.9.cloned.1.call-done = f32[896,4]{1,0:T(8,128)} async-done(((f32[7168,4]{1,0:T(8,128)}), f32[896,4]{1,0:T(8,128)}) %reduce-scatter.9.cloned.1.call-update) | async-done | bytes 14352
  332.7 1.3 reshape.59
  334.0 1.2 copy.36
  335.2 0.0 copy-done.1
  (4 shorter events, 0.1 us)
Async XLA Ops:
  6.5 3.4 copy-start
  6.5 136.5 %reduce-scatter.7.cloned.1.call-start = ((), (), s32[]{:S(2)}) async-start(), calls=%async_computation.2 | async-start | bytes 73728
  84.3 139.3 %all-reduce.3.cloned.1.call-start = ((), (), s32[]{:S(2)}) async-start(), calls=%async_computation.4 | async-start | bytes 2097152
  84.4 10.3 %copy-start.2 = (u32[32]{0:T(128)S(1)}, u32[32]{0:T(128)}, u32[]{:S(2)}) copy-start(u32[32]{0:T(128)} %constant.21) | copy-start | bytes 388
  94.4 238.3 %reduce-scatter.9.cloned.1.call-start = ((), (), s32[]{:S(2)}) async-start(), calls=%async_computation.3 | async-start | bytes 4128768
  237.3 97.9 %copy-start.1 = (bf16[16,128,512]{2,1,0:T(8,128)(2,1)S(1)}, bf16[16,128,512]{2,1,0:T(8,128)(2,1)}, u32[]{:S(2)}) copy-start(bf16[16,128,512]{2,1,0:T(8,128)(2,1)} %param.10) | copy-start | bytes 6291460
Sparse Core Ops, SparseCore 0:
  84.4 58.5 reduce-scatter.6
  146.6 77.0 all-reduce.2
  252.2 80.4 reduce-scatter.8
where the time goes:
time: 342 us
  waiting for transfers between devices  208 us (61%)
  blocking collectives  54.8 us (16%)
  matrix products  35.2 us (10%)
  local copies, waits for them, and re-layouts  23.1 us (7%)
  between operations  13.9 us (4%)
  other arithmetic  6.88 us (2%)
    unnamed x6, waiting for transfers between devices  208 us
    all_gather x1, blocking collectives, per_device(): full_query = lax.all_gather(own_query, 'ctx', axis=2, tiled=True)  33.4 us
    pmax x1, blocking collectives, per_device(): global_max = lax.pmax(row_max, 'ctx')  21.4 us
    unnamed x16, local copies, waits for them, and re-layouts  19.7 us
    dot_general x1, matrix products, block_terms(): jnp.einsum('bqhc,btc->bqht', full_query, cache_block, preferred_element_t...  13 us
    dot_general x1, matrix products, per_device(): jnp.dot(flat_values, output_weight, preferred_element_type=jnp.float32)  11.5 us
    dot_general x1, matrix products, block_terms(): jnp.einsum('bqht,btc->bqhc', weights.astype(jnp.bfloat16), cache_block[.....  8.18 us
  transfers between devices with their start and end apart: 3, of which 3 were waited for; matrix products, arithmetic and copies ran while one was open for 3% of the time, Pallas kernels for 0%

commit v1 on v0

v1 whole, which is shorter than its diff:
```python
import functools

import jax
import jax.numpy as jnp
from jax import lax
from jax.experimental import pallas as pl
from jax.experimental.pallas import tpu as pltpu
from jax.sharding import PartitionSpec as P

NOPE = 128
ROPE = 64
LAT = 512
PAGE = 128
LANES = 128
LAT_TILES = LAT // LANES
LOG2E = 1.4426950408889634
SOFTMAX_SCALE = (NOPE + ROPE) ** (-0.5)
LOWEST = -1e30
STAT_ROWS = 16


def head_of_row(shape, heads):
    return lax.rem(lax.broadcasted_iota(jnp.int32, shape, 0), heads)


def query_kernel(queries_hbm, absorb_hbm, out_ref, again_ref, queries_ref, absorb_ref, sems):
    rows = queries_ref.shape[0]
    heads = absorb_ref.shape[0]
    half = rows // 2
    pieces = sems.shape[0] - 1
    group = heads // pieces
    copies = [pltpu.make_async_copy(queries_hbm, queries_ref, sems.at[pieces])] + [
        pltpu.make_async_copy(
            absorb_hbm.at[pl.ds(i * group, group)],
            absorb_ref.at[pl.ds(i * group, group)],
            sems.at[i],
        )
        for i in range(pieces)
    ]
    for copy in copies:
        copy.start()
    copies[0].wait()
    nope = queries_ref[:, :NOPE]
    owner = head_of_row((rows, NOPE), heads)
    latent = jnp.zeros((rows, LAT), jnp.float32)
    for i in range(pieces):
        spread = jnp.concatenate(
            [
                jnp.where(owner == h, nope, jnp.zeros_like(nope))
                for h in range(i * group, (i + 1) * group)
            ],
            axis=1,
        )
        copies[i + 1].wait()
        latent += jnp.dot(
            spread,
            absorb_ref[i * group : (i + 1) * group].reshape(group * NOPE, LAT),
            preferred_element_type=jnp.float32,
        )
    latent = latent.astype(jnp.bfloat16)
    rope = queries_ref[:, NOPE:]
    rope = jnp.concatenate([rope[:half], rope[half:]], axis=1)
    for b in range(2):
        for j in range(LAT_TILES):
            start = (b * LAT_TILES + j) * half
            out_ref[start : start + half, :] = latent[
                b * half : (b + 1) * half, j * LANES : (j + 1) * LANES
            ]
    out_ref[2 * LAT_TILES * half :, :] = rope
    again_ref[...] = out_ref[...]


def column_kernel(rate_ref, scale_ref, through_ref, inv_rate_ref, scales_ref, passed_ref):
    del through_ref, passed_ref
    ctx, heads, _ = inv_rate_ref.shape
    line = ctx // 2
    me = lax.axis_index("ctx")
    for source, target in ((1.0 / rate_ref[...], inv_rate_ref), (scale_ref[...], scales_ref)):
        size = source.shape[1]
        same = lax.broadcasted_iota(jnp.int32, (size, size), 0) == lax.broadcasted_iota(
            jnp.int32, (size, size), 1
        )
        column = jnp.sum(jnp.where(same, source, 0.0), axis=1, keepdims=True)
        column = jnp.broadcast_to(column, (size, LANES)).reshape(ctx, heads, LANES)
        for k in range(ctx):
            owner = me ^ (2 * (k % line) + k // line)
            picked = jnp.zeros((heads, LANES), jnp.float32)
            for device in range(ctx):
                picked = jnp.where(owner == device, column[device], picked)
            target[k] = picked


def attention_kernel(pages_ref, lengths_ref, *refs, ctx, b):
    query_refs, refs = refs[:ctx], refs[ctx:]
    cache_ref, inv_rate, scale, near_ref, far_ref, query, acc, total, *buffers = refs
    scores_of, weights_of, factor_of = buffers[:2], buffers[2:4], buffers[4:]
    rows, chunk = scores_of[0].shape
    half = rows // ctx
    heads = half // 2
    line = ctx // 2
    steps = cache_ref.shape[2] // chunk
    pair_width = 2 * PAGE
    pairs = chunk // pair_width
    request_rows = LAT_TILES * half
    start = b * request_rows

    for k, block in enumerate(query_refs):
        own = slice(k * half, (k + 1) * half)
        for j in range(LAT_TILES):
            query[own, j * LANES : (j + 1) * LANES] = block[
                start + j * half : start + (j + 1) * half, :
            ]
        query[own, LAT:] = block[2 * request_rows :, b * ROPE : (b + 1) * ROPE]

    lane = lax.broadcasted_iota(jnp.int32, (heads, LANES), 1)
    first_pos = lengths_ref[b] - 2

    def raw_scores(at):
        return jnp.dot(
            query[...],
            cache_ref[b, :, at * pair_width : (at + 1) * pair_width],
            preferred_element_type=jnp.float32,
        )

    def add_products(step):
        weights, factor = weights_of[step % 2], factor_of[step % 2]
        for columns in (slice(0, LAT // 2), slice(LAT // 2, LAT)):
            new = lax.dot_general(
                weights[...],
                cache_ref[b, columns, step * chunk : (step + 1) * chunk],
                (((1,), (1,)), ((), ())),
                preferred_element_type=jnp.float32,
            )
            for j in range(columns.start, columns.stop, LANES):
                part = new[:, j - columns.start : j - columns.start + LANES]
                at = slice(j, j + LANES)
                acc[:, at] = acc[:, at] * factor[...] + part if step else part

    top = jnp.full((rows, LANES), LOWEST, jnp.float32)
    ahead = raw_scores(0)
    for step in range(steps):
        scores, weights = scores_of[step % 2], weights_of[step % 2]
        tops = [None, None]
        for pair in range(pairs):
            raw = ahead
            at = step * pairs + pair
            if at + 1 < steps * pairs:
                ahead = raw_scores(at + 1)
            for side in range(2):
                page = pair * 2 + side
                columns = slice(page * PAGE, (page + 1) * PAGE)
                part = raw[:, side * PAGE : (side + 1) * PAGE].reshape(ctx, 2, heads, PAGE)
                base = first_pos - pages_ref[b, step * (chunk // PAGE) + page] * PAGE
                values = []
                for q in range(2):
                    distance = base + q - lane
                    spread = jnp.where(distance >= 0, distance.astype(jnp.float32), jnp.inf)
                    logs = jnp.log2(spread[None] + inv_rate[...])
                    value = part[:, q] * (SOFTMAX_SCALE * LOG2E) - scale[...] * logs
                    tops[q] = value if tops[q] is None else jnp.maximum(tops[q], value)
                    values.append(value)
                scores[:, columns] = jnp.stack(values, axis=1).reshape(rows, PAGE)
        lane_top = jnp.stack(tops, axis=1).reshape(rows, LANES)
        before = top
        top = jnp.maximum(before, jnp.max(lane_top, axis=1, keepdims=True))
        factor = jnp.exp2(before - top)
        factor_of[step % 2][...] = factor
        if step:
            add_products(step - 1)
        lane_total = total[...] * factor if step else jnp.zeros((rows, LANES), jnp.float32)
        for page in range(chunk // PAGE):
            columns = slice(page * PAGE, (page + 1) * PAGE)
            value = jnp.exp2(scores[:, columns] - top)
            lane_total += value
            weights[:, columns] = value.astype(jnp.bfloat16)
        total[...] = lane_total
    add_products(steps - 1)

    row_total = jnp.sum(total[...], axis=1, keepdims=True)
    row_total = jnp.broadcast_to(row_total, (rows, LANES))
    seen = row_total > 0.0
    safe = jnp.where(seen, row_total, 1.0)
    share = 1.0 / safe
    for j in range(LAT_TILES):
        columns = slice(j * LANES, (j + 1) * LANES)
        part = (acc[:, columns] * share).astype(jnp.bfloat16).reshape(ctx, half, LANES)
        near_ref[:, j * half : (j + 1) * half, :] = part[:line]
        far_ref[:, j * half : (j + 1) * half, :] = part[line:]
    log_total = jnp.where(seen, top + jnp.log2(safe), LOWEST).reshape(ctx, half, LANES)
    across = jnp.sum(jnp.where(diagonal(half), log_total, 0.0), axis=1, keepdims=True)
    packed = three_parts(across).astype(jnp.bfloat16)
    near_ref[:, request_rows:, :] = packed[:line]
    far_ref[:, request_rows:, :] = packed[line:]


def diagonal(half):
    return lax.broadcasted_iota(jnp.int32, (half, LANES), 0) == lax.broadcasted_iota(
        jnp.int32, (half, LANES), 1
    )


def three_parts(value):
    high = value.astype(jnp.bfloat16).astype(jnp.float32)
    middle = (value - high).astype(jnp.bfloat16).astype(jnp.float32)
    low = value - high - middle
    row = lax.broadcasted_iota(jnp.int32, (value.shape[0], STAT_ROWS, LANES), 1)
    return jnp.where(
        row == 0, high, jnp.where(row == 1, middle, jnp.where(row == 2, low, 0.0))
    )


def logs_of(stats):
    return jnp.sum(stats.astype(jnp.float32), axis=1, keepdims=True)


def as_column(across, half):
    return jnp.sum(jnp.where(diagonal(half), across, 0.0), axis=-1, keepdims=True)


def merge_kernel(own_ref, other_ref, *out_refs):
    request_rows = own_ref.shape[1] - STAT_ROWS
    half = request_rows // LAT_TILES
    own_log = logs_of(own_ref[:, request_rows:, :])
    other_log = logs_of(other_ref[:, request_rows:, :])
    high = jnp.maximum(own_log, other_log)
    own_factor = jnp.exp2(own_log - high)
    other_factor = jnp.exp2(other_log - high)
    both = own_factor + other_factor
    stats = three_parts(high + jnp.log2(both)).astype(jnp.bfloat16)
    own_factor = as_column(own_factor / both, half)
    other_factor = as_column(other_factor / both, half)
    for j in range(LAT_TILES):
        at = slice(j * half, (j + 1) * half)
        merged = (
            own_ref[:, at, :].astype(jnp.float32) * own_factor
            + other_ref[:, at, :].astype(jnp.float32) * other_factor
        ).astype(jnp.bfloat16)
        for k, out_ref in enumerate(out_refs):
            out_ref[at, :] = merged[k]
    for k, out_ref in enumerate(out_refs):
        out_ref[request_rows:, :] = stats[k]


def output_kernel(*refs):
    *part_refs, up_ref, weight_ref, out_ref, values, attn = refs
    heads = up_ref.shape[0]
    half = 2 * heads
    rows = 2 * half
    request_rows = LAT_TILES * half
    for b in range(2):
        parts = part_refs[b * len(part_refs) // 2 : (b + 1) * len(part_refs) // 2]
        logs = logs_of(jnp.stack([part[request_rows:, :] for part in parts]))
        factor = jnp.exp2(logs - jnp.max(logs, axis=0, keepdims=True))
        factor = as_column(factor / jnp.sum(factor, axis=0, keepdims=True), half)
        for j in range(LAT_TILES):
            at = slice(j * half, (j + 1) * half)
            attn[b * half : (b + 1) * half, j * LANES : (j + 1) * LANES] = sum(
                part[at, :].astype(jnp.float32) * factor[k] for k, part in enumerate(parts)
            ).astype(jnp.bfloat16)
    latent = attn[...]
    owner = head_of_row(latent.shape, heads)
    up = jnp.zeros((rows, up_ref.shape[2]), jnp.float32)
    for h in range(heads):
        own = jnp.where(owner == h, latent, jnp.zeros_like(latent))
        up += jnp.dot(own, up_ref[h], preferred_element_type=jnp.float32)
    up = up.astype(jnp.bfloat16)
    owner = head_of_row(up.shape, heads)
    spread = jnp.concatenate(
        [jnp.where(owner == h, up, jnp.zeros_like(up)) for h in range(heads)], axis=1
    )
    token = lax.broadcasted_iota(jnp.int32, (8, rows), 0)
    group = lax.broadcasted_iota(jnp.int32, (8, rows), 1) // heads
    pick = jnp.where(token == group, 1.0, 0.0).astype(jnp.bfloat16)
    values[...] = jnp.dot(pick, spread, preferred_element_type=jnp.float32)
    project(values, weight_ref, out_ref, True)


def project(values, weight_ref, out_ref, far):
    blocks, tokens, width = out_ref.shape
    bit = lax.rem(lax.axis_index("ctx") // 2, 2)
    first = (1 - bit if far else bit) * (2 * width)

    @pl.loop(0, blocks // 2)
    def _(k):
        result = jnp.dot(
            values[...].astype(jnp.bfloat16),
            weight_ref[:, pl.ds(pl.multiple_of(first + k * (4 * width), LANES), 2 * width)],
            preferred_element_type=jnp.float32,
        )
        out_ref[2 * k] = result[:tokens, :width].astype(out_ref.dtype)
        out_ref[2 * k + 1] = result[:tokens, width:].astype(out_ref.dtype)


def near_kernel(values, weight_ref, out_ref):
    project(values, weight_ref, out_ref, False)


def add_kernel(own_ref, other_ref, kept_ref, *sent_refs):
    me = lax.axis_index("ctx")
    own = (me // 4) * 2 + lax.rem(me, 2)
    for k, out_ref in enumerate((kept_ref,) + sent_refs):
        block = own_ref[own ^ k] + other_ref[own ^ k].astype(jnp.float32)
        out_ref[...] = block.astype(out_ref.dtype)


def sum_kernel(own_ref, *refs):
    *other_refs, out_ref = refs
    result = own_ref[...]
    for other in other_refs:
        result += other[...].astype(jnp.float32)
    requests, tokens, _ = out_ref.shape
    for b in range(requests):
        out_ref[b] = result[b * tokens : (b + 1) * tokens].astype(out_ref.dtype)


def per_device(
    queries,
    key_absorb,
    latent_cache,
    page_order,
    lengths,
    kerple_scale,
    kerple_rate,
    value_up,
    output_weight,
    *,
    ctx,
):
    requests, query_len, heads, query_width = queries.shape
    keys_dev = latent_cache.shape[1]
    half = query_len * heads
    rows = requests * half
    request_rows = LAT_TILES * half
    width = output_weight.shape[1] // ctx
    chunk = 1024

    hint = pl.CostEstimate(flops=20 * 10**9, bytes_accessed=2**20, transcendentals=0)
    long_hint = pl.CostEstimate(flops=100 * 10**9, bytes_accessed=2**20, transcendentals=0)
    in_hbm = lambda value: pltpu.with_memory_space_constraint(value, pltpu.HBM)
    in_vmem = lambda value: pltpu.with_memory_space_constraint(value, pltpu.VMEM)
    line = ctx // 2
    swap = lambda value, bits: lax.ppermute(value, "ctx", [(i, i ^ bits) for i in range(ctx)])
    packed, again = pl.pallas_call(
        query_kernel,
        in_specs=[pl.BlockSpec(memory_space=pl.ANY)] * 2,
        out_shape=[jax.ShapeDtypeStruct((2 * request_rows + half, LANES), jnp.bfloat16)] * 2,
        scratch_shapes=[
            pltpu.VMEM((rows, query_width), jnp.bfloat16),
            pltpu.VMEM(key_absorb.shape, jnp.bfloat16),
            pltpu.SemaphoreType.DMA((5,)),
        ],
        compiler_params=pltpu.CompilerParams(vmem_limit_bytes=8 * 2**20),
        name="latent_query",
    )(in_hbm(queries.reshape(rows, query_width)), in_hbm(key_absorb))
    columns = (ctx, heads, LANES)
    inv_rate, scale, again = pl.pallas_call(
        column_kernel,
        in_specs=[pl.BlockSpec(memory_space=pltpu.VMEM)] * 2
        + [pl.BlockSpec(memory_space=pl.ANY)],
        out_specs=[pl.BlockSpec(memory_space=pltpu.VMEM)] * 2
        + [pl.BlockSpec(memory_space=pl.ANY)],
        out_shape=[jax.ShapeDtypeStruct(columns, jnp.float32)] * 2
        + [jax.ShapeDtypeStruct(again.shape, again.dtype)],
        input_output_aliases={2: 2},
        compiler_params=pltpu.CompilerParams(vmem_limit_bytes=4 * 2**20),
        name="head_columns",
        cost_estimate=long_hint,
    )(in_hbm(kerple_rate.reshape(1, -1)), in_hbm(kerple_scale.reshape(1, -1)), again)
    column = [packed] + [swap(packed, 2 * k) for k in range(1, line)]
    gathered = column + [swap(value, 1) for value in [again] + column[1:]]

    cache = in_vmem(jnp.swapaxes(latent_cache, 1, 2))
    all_rows = ctx * half
    message = (request_rows + STAT_ROWS, LANES)
    in_smem = pl.BlockSpec(memory_space=pltpu.SMEM)
    whole = pl.BlockSpec(memory_space=pltpu.VMEM)
    parts = []
    for b in range(requests):
        near, far = pl.pallas_call(
            functools.partial(attention_kernel, ctx=ctx, b=b),
            in_specs=[in_smem, in_smem] + [whole] * (ctx + 3),
            out_shape=[jax.ShapeDtypeStruct((line,) + message, jnp.bfloat16)] * 2,
            scratch_shapes=[
                pltpu.VMEM((all_rows, LAT + ROPE), jnp.bfloat16),
                pltpu.VMEM((all_rows, LAT), jnp.float32),
                pltpu.VMEM((all_rows, LANES), jnp.float32),
            ]
            + [pltpu.VMEM((all_rows, chunk), jnp.float32)] * 2
            + [pltpu.VMEM((all_rows, chunk), jnp.bfloat16)] * 2
            + [pltpu.VMEM((all_rows, LANES), jnp.float32)] * 2,
            compiler_params=pltpu.CompilerParams(vmem_limit_bytes=8 * 2**20),
            cost_estimate=hint,
            name="attention",
        )(in_hbm(page_order), in_hbm(lengths), *gathered, cache, inv_rate, scale)
        merged = pl.pallas_call(
            merge_kernel,
            out_shape=[jax.ShapeDtypeStruct(message, jnp.bfloat16) for _ in range(line)],
            compiler_params=pltpu.CompilerParams(vmem_limit_bytes=4 * 2**20),
            name="merge",
        )(near, swap(far, 1))
        parts.append(merged[0])
        parts += [swap(merged[k], 2 * k) for k in range(1, line)]

    tokens = requests * query_len
    weight = in_vmem(output_weight)
    small = pltpu.CompilerParams(vmem_limit_bytes=4 * 2**20)
    far, values = pl.pallas_call(
        output_kernel,
        out_shape=[
            jax.ShapeDtypeStruct((line, tokens, width), jnp.bfloat16),
            jax.ShapeDtypeStruct((8, output_weight.shape[0]), jnp.float32),
        ],
        scratch_shapes=[pltpu.VMEM((rows, LAT), jnp.bfloat16)],
        compiler_params=small,
        cost_estimate=hint,
        name="up_and_far_output",
    )(*parts, in_vmem(value_up), weight)
    near = pl.pallas_call(
        near_kernel,
        out_shape=jax.ShapeDtypeStruct((line, tokens, width), jnp.float32),
        compiler_params=small,
        cost_estimate=hint,
        name="near_output",
    )(values, weight)
    block = (tokens, width)
    kept, *sent = pl.pallas_call(
        add_kernel,
        out_shape=[jax.ShapeDtypeStruct(block, jnp.float32)]
        + [jax.ShapeDtypeStruct(block, jnp.bfloat16)] * 3,
        compiler_params=small,
        name="add_columns",
    )(near, swap(far, 2))
    return pl.pallas_call(
        sum_kernel,
        out_shape=jax.ShapeDtypeStruct((requests, query_len, width), jnp.bfloat16),
        compiler_params=small,
        name="sum_output",
    )(kept, *(swap(part, bits) for part, bits in zip(sent, (1, 4, 5))))


def plain_device(
    queries,
    key_absorb,
    latent_cache,
    page_order,
    lengths,
    kerple_scale,
    kerple_rate,
    value_up,
    output_weight,
    *,
    ctx,
):
    requests, query_len, heads, _ = queries.shape
    width = output_weight.shape[1] // ctx
    latent_query = jnp.einsum(
        "bqhn,hnc->bqhc", queries[..., :NOPE], key_absorb, preferred_element_type=jnp.float32
    ).astype(jnp.bfloat16)
    own_query = jnp.concatenate([latent_query, queries[..., NOPE:]], axis=-1)
    full_query = lax.all_gather(own_query, "ctx", axis=2, tiled=True)
    offsets = jnp.arange(PAGE, dtype=jnp.int32)
    key_pos = (page_order[:, :, None] * PAGE + offsets).reshape(requests, -1)
    query_pos = lengths[:, None] - query_len + jnp.arange(query_len, dtype=jnp.int32)
    distance = query_pos[:, :, None] - key_pos[:, None, :]
    visible = (distance >= 0)[:, :, None, :]
    spread = jnp.maximum(distance, 0).astype(jnp.float32)[:, :, None, :]
    log_bias = kerple_scale[:, None] * jnp.log(1.0 + kerple_rate[:, None] * spread)
    scores = jnp.einsum(
        "bqhc,btc->bqht", full_query, latent_cache, preferred_element_type=jnp.float32
    )
    scores = jnp.where(visible, scores * SOFTMAX_SCALE - log_bias, LOWEST)
    row_max = jnp.max(scores, axis=-1)
    weights = jnp.where(visible, jnp.exp(scores - row_max[..., None]), 0.0)
    summed = jnp.einsum(
        "bqht,btc->bqhc",
        weights.astype(jnp.bfloat16),
        latent_cache[..., :LAT],
        preferred_element_type=jnp.float32,
    )
    factor = jnp.exp(row_max - lax.pmax(row_max, "ctx"))
    shared_total = lax.psum_scatter(
        jnp.sum(weights, axis=-1) * factor, "ctx", scatter_dimension=2, tiled=True
    )
    shared_sum = lax.psum_scatter(
        summed * factor[..., None], "ctx", scatter_dimension=2, tiled=True
    )
    attn_latent = (shared_sum / shared_total[..., None]).astype(jnp.bfloat16)
    up_values = jnp.einsum(
        "bqhc,hcv->bqhv", attn_latent, value_up, preferred_element_type=jnp.float32
    ).astype(jnp.bfloat16)
    partial_out = jnp.dot(
        up_values.reshape(requests * query_len, -1),
        output_weight,
        preferred_element_type=jnp.float32,
    )
    summed_out = lax.psum_scatter(partial_out, "ctx", scatter_dimension=1, tiled=True)
    return summed_out.astype(jnp.bfloat16).reshape(requests, query_len, width)


def solution(mesh):
    ctx = mesh.shape["ctx"]
    in_specs = (
        P("rep", None, "ctx", None),
        P("ctx", None, None),
        P("rep", "ctx", None),
        P("rep", "ctx"),
        P("rep"),
        P(),
        P(),
        P("ctx", None, None),
        P("ctx", None),
    )
    out_specs = P("rep", None, "ctx")

    def device_program(*args):
        heads = args[0].shape[2]
        width = args[-1].shape[1] // ctx
        tiled = ctx == 8 and heads % 16 == 0 and width % LANES == 0
        return (per_device if tiled else plain_device)(*args, ctx=ctx)

    return jax.shard_map(
        device_program, mesh=mesh, in_specs=in_specs, out_specs=out_specs, check_vma=False
    )
```

time: 342 us -> 57.8 us (0.17)
  waiting for transfers between devices: 208 us -> 14.2 us
  blocking collectives: 54.8 us -> 0 us
  matrix products: 35.2 us -> 0 us
  starting transfers between devices: 0.27 us -> 25.8 us
  local copies, waits for them, and re-layouts: 23.1 us -> 0.05 us
  Pallas kernels: 0 us -> 17.4 us
  between operations: 13.9 us -> 0.18 us
  other arithmetic: 6.88 us -> 0.01 us
    unnamed x6 -> x0, waiting for transfers between devices: 208 us -> none
    dot_general x5 -> x0, matrix products: 35.2 us -> none  [the longest x1 13 us: block_terms(): jnp.einsum('bqhc,btc->bqht', full_query, cache_block, preferred_element_t...]
    all_gather x1 -> x0, blocking collectives: 33.4 us -> none  [per_device(): full_query = lax.all_gather(own_query, 'ctx', axis=2, tiled=True)]
    ppermute x0 -> x19, starting transfers between devices: none -> 25.8 us  [per_device(): lax.ppermute(value, 'ctx', [(i, i ^ bits) for i in range(ctx)])]
    pmax x1 -> x0, blocking collectives: 21.4 us -> none  [per_device(): global_max = lax.pmax(row_max, 'ctx')]
    unnamed x16 -> x18, local copies, waits for them, and re-layouts: 19.7 us -> 0.05 us
    pallas_call x0 -> x10, Pallas kernels: none -> 17.4 us  [the longest x2 8.66 us: per_device(): pl.pallas_call(functools.partial(attention_kernel, ctx=ctx, b=b), in_spec...]
    ppermute x0 -> x19, waiting for transfers between devices: none -> 14.2 us  [per_device(): lax.ppermute(value, 'ctx', [(i, i ^ bits) for i in range(ctx)])]
  transfers between devices with their start and end apart: 3 -> 19, of which waited for: 3 -> 9; matrix products, arithmetic and copies ran while one was open for 3% -> 0% of each run, Pallas kernels for 0% -> 14%
where the time goes in v1:
time: 57.8 us; the launch traced here: 57.7 us
  starting transfers between devices  25.8 us (45%)
  Pallas kernels  17.4 us (30%)
  waiting for transfers between devices  14.2 us (25%)
    ppermute x19, starting transfers between devices, per_device(): lax.ppermute(value, 'ctx', [(i, i ^ bits) for i in range(ctx)])  25.8 us
    ppermute x19, waiting for transfers between devices, per_device(): lax.ppermute(value, 'ctx', [(i, i ^ bits) for i in range(ctx)])  14.2 us
    pallas_call x2, Pallas kernels, per_device(): pl.pallas_call(functools.partial(attention_kernel, ctx=ctx, b=b), in_spec...  8.66 us
    pallas_call x1, Pallas kernels, per_device(): pl.pallas_call(output_kernel, out_shape=[jax.ShapeDtypeStruct((line, toke...  2.88 us
    pallas_call x1, Pallas kernels, per_device(): pl.pallas_call(near_kernel, out_shape=jax.ShapeDtypeStruct((line, tokens,...  2.14 us
    pallas_call x1, Pallas kernels, per_device(): pl.pallas_call(query_kernel, in_specs=[pl.BlockSpec(memory_space=pl.ANY)]...  1.8 us
  transfers between devices with their start and end apart: 19, of which 9 were waited for; matrix products, arithmetic and copies ran while one was open for 0% of the time, Pallas kernels for 14%

profile of v1, /device:TPU:0, one launch (start us, length us, event | category | flops | bytes accessed | tf_op | source)
XLA Modules:
  0.0 57.7 jit_solution(6297090044675089187)
XLA Ops:
  0.0 1.8 %latent_query.1 = (bf16[288,128]{1,0:T(8,128)(2,1)S(1)}, bf16[288,128]{1,0:T(8,128)(2,1)S(1)}) custom-call(bf16[64,192]{1,0:T(8,128)(2,1)} %bitcast.8, bf16[16,128,512]{2,1,0:T(8,128)(2,1)} %absorb_hbm.1), custom_call_target="tpu_custom_call" | custom-call | tf_op jit(solution)/shard_map/latent_query/pallas_call | solution.py:343
  1.8 3.1 %collective-permute-start = (bf16[288,128]{1,0:T(8,128)(2,1)S(1)}, bf16[288,128]{1,0:T(8,128)(2,1)S(1)}, u32[]{:S(2)}, u32[]{:S(2)}) collective-permute-start(bf16[288,128]{1,0:T(8,128)(2,1)S(1)} %get-tuple-element.28.refs_0_), channel_id=1, source_target_pairs={{0,8},{4,12},{8,0},{12,4},{16,24},{20,28},{24,16},{28,20},{1,9},{5... | collective-permute-start | bytes 221192 | tf_op jit(solution)/shard_map/ppermute | solution.py:342
  4.9 2.6 %collective-permute-start.1 = (bf16[288,128]{1,0:T(8,128)(2,1)S(1)}, bf16[288,128]{1,0:T(8,128)(2,1)S(1)}, u32[]{:S(2)}, u32[]{:S(2)}) collective-permute-start(bf16[288,128]{1,0:T(8,128)(2,1)S(1)} %get-tuple-element.28.refs_0_), channel_id=1, source_target_pairs={{0,16},{4,20},{8,24},{12,28},{16,0},{20,4},{24,8},{28,12},{1,17},{... | collective-permute-start | bytes 221192 | tf_op jit(solution)/shard_map/ppermute | solution.py:342
  7.5 1.0 %head_columns.1 = (f32[8,16,128]{2,1,0:T(8,128)S(1)}, f32[8,16,128]{2,1,0:T(8,128)S(1)}, bf16[288,128]{1,0:T(8,128)(2,1)S(1)}) custom-call(f32[1,128]{1,0:T(1,128)} %bitcast.9, f32[1,128]{1,0:T(1,128)} %bitcast.10, bf16[288,128]{1,0:T(8,128)(2,1)S(1)} %get-tuple-element.29.through_ref), custom_call_target="tpu_custom_call", output_to_operand_aliasing={{2}: (2, {})} | custom-call | flops 99999997952 | bytes 1048576 | tf_op jit(solution)/shard_map/head_columns/pallas_call | solution.py:356
  8.5 1.8 %collective-permute-start.3 = (bf16[288,128]{1,0:T(8,128)(2,1)S(1)}, bf16[288,128]{1,0:T(8,128)(2,1)S(1)}, u32[]{:S(2)}, u32[]{:S(2)}) collective-permute-start(bf16[288,128]{1,0:T(8,128)(2,1)S(1)} %get-tuple-element.30), channel_id=1, source_target_pairs={{0,4},{4,0},{8,12},{12,8},{16,20},{20,16},{24,28},{28,24},{1,5},{5... | collective-permute-start | bytes 221192 | tf_op jit(solution)/shard_map/ppermute | solution.py:342
  10.2 0.0 collective-permute-done.refs_1_
  10.2 0.3 collective-permute-start.4
  10.5 2.1 %collective-permute-done.1.refs_2_ = bf16[288,128]{1,0:T(8,128)(2,1)S(1)} collective-permute-done((bf16[288,128]{1,0:T(8,128)(2,1)S(1)}, bf16[288,128]{1,0:T(8,128)(2,1)S(1)}, u32[]{:S(2)}, u32[]{:S(2)}) %collective-permute-start.1) | collective-permute-done | bytes 73760 | tf_op jit(solution)/shard_map/ppermute | solution.py:342
  12.7 1.5 %collective-permute-start.5 = (bf16[288,128]{1,0:T(8,128)(2,1)S(1)}, bf16[288,128]{1,0:T(8,128)(2,1)S(1)}, u32[]{:S(2)}, u32[]{:S(2)}) collective-permute-start(bf16[288,128]{1,0:T(8,128)(2,1)S(1)} %collective-permute-done.1.refs_2_), channel_id=1, source_target_pairs={{0,4},{4,0},{8,12},{12,8},{16,20},{20,16},{24,28},{28,24},{1,5},{5... | collective-permute-start | bytes 221192 | tf_op jit(solution)/shard_map/ppermute | solution.py:342
  14.2 0.0 collective-permute-done.2.refs_3_
  14.2 1.1 %collective-permute-start.6 = (bf16[288,128]{1,0:T(8,128)(2,1)S(1)}, bf16[288,128]{1,0:T(8,128)(2,1)S(1)}, u32[]{:S(2)}, u32[]{:S(2)}) collective-permute-start(bf16[288,128]{1,0:T(8,128)(2,1)S(1)} %collective-permute-done.2.refs_3_), channel_id=1, source_target_pairs={{0,4},{4,0},{8,12},{12,8},{16,20},{20,16},{24,28},{28,24},{1,5},{5... | collective-permute-start | bytes 221192 | tf_op jit(solution)/shard_map/ppermute | solution.py:342
  15.2 0.0 collective-permute-done.3.refs_4_
  15.2 0.0 collective-permute-done.4.refs_5_
  15.2 1.8 %collective-permute-done.5.refs_6_ = bf16[288,128]{1,0:T(8,128)(2,1)S(1)} collective-permute-done((bf16[288,128]{1,0:T(8,128)(2,1)S(1)}, bf16[288,128]{1,0:T(8,128)(2,1)S(1)}, u32[]{:S(2)}, u32[]{:S(2)}) %collective-permute-start.5) | collective-permute-done | bytes 73760 | tf_op jit(solution)/shard_map/ppermute | solution.py:342
  17.0 1.5 %collective-permute-done.6.refs_7_ = bf16[288,128]{1,0:T(8,128)(2,1)S(1)} collective-permute-done((bf16[288,128]{1,0:T(8,128)(2,1)S(1)}, bf16[288,128]{1,0:T(8,128)(2,1)S(1)}, u32[]{:S(2)}, u32[]{:S(2)}) %collective-permute-start.6) | collective-permute-done | bytes 73760 | tf_op jit(solution)/shard_map/ppermute | solution.py:342
  18.5 4.3 %attention.2 = (bf16[4,144,128]{2,1,0:T(8,128)(2,1)S(1)}, bf16[4,144,128]{2,1,0:T(8,128)(2,1)S(1)}) custom-call(s32[2,32]{1,0:T(2,128)} %pages_ref.3, s32[2]{0:T(128)} %lengths_ref.3, bf16[288,128]{1,0:T(8,128)(2,1)S(1)} %get-tuple-element.28.refs_0_, bf16[288,128]{1,0:T(8,128)(2,1)S(1)} %collective-permute-done.refs_1_, ...), custom_call_target="tpu_custom_call" | custom-call | flops 20000000000 | bytes 1048576 | tf_op jit(solution)/shard_map/attention/pallas_call | solution.py:379
  22.8 0.0 slice-start
  22.8 0.0 slice-start.1
  22.8 0.0 slice-start.3
  22.8 0.0 slice-start.4
  22.9 0.0 slice-start.6
  22.9 0.0 copy-start.1
  22.9 1.1 %collective-permute-start.7 = (bf16[4,144,128]{2,1,0:T(8,128)(2,1)S(1)}, bf16[4,144,128]{2,1,0:T(8,128)(2,1)S(1)}, u32[]{:S(2)}, u32[]{:S(2)}) collective-permute-start(bf16[4,144,128]{2,1,0:T(8,128)(2,1)S(1)} %get-tuple-element.34), channel_id=1, source_target_pairs={{0,4},{4,0},{8,12},{12,8},{16,20},{20,16},{24,28},{28,24},{1,5},{5... | collective-permute-start | bytes 442376 | tf_op jit(solution)/shard_map/ppermute | solution.py:342
  24.0 4.4 %attention.3 = (bf16[4,144,128]{2,1,0:T(8,128)(2,1)S(1)}, bf16[4,144,128]{2,1,0:T(8,128)(2,1)S(1)}) custom-call(s32[2,32]{1,0:T(2,128)} %pages_ref.3, s32[2]{0:T(128)} %lengths_ref.3, bf16[288,128]{1,0:T(8,128)(2,1)S(1)} %get-tuple-element.28.refs_0_, bf16[288,128]{1,0:T(8,128)(2,1)S(1)} %collective-permute-done.refs_1_, ...), custom_call_target="tpu_custom_call" | custom-call | flops 20000000000 | bytes 1048576 | tf_op jit(solution)/shard_map/attention/pallas_call | solution.py:379
  28.4 1.0 %collective-permute-start.11 = (bf16[4,144,128]{2,1,0:T(8,128)(2,1)S(1)}, bf16[4,144,128]{2,1,0:T(8,128)(2,1)S(1)}, u32[]{:S(2)}, u32[]{:S(2)}) collective-permute-start(bf16[4,144,128]{2,1,0:T(8,128)(2,1)S(1)} %get-tuple-element.40), channel_id=1, source_target_pairs={{0,4},{4,0},{8,12},{12,8},{16,20},{20,16},{24,28},{28,24},{1,5},{5... | collective-permute-start | bytes 442376 | tf_op jit(solution)/shard_map/ppermute | solution.py:342
  29.5 0.1 merge.2
  29.6 0.7 %collective-permute-start.8 = (bf16[144,128]{1,0:T(8,128)(2,1)S(1)}, bf16[144,128]{1,0:T(8,128)(2,1)S(1)}, u32[]{:S(2)}, u32[]{:S(2)}) collective-permute-start(bf16[144,128]{1,0:T(8,128)(2,1)S(1)} %get-tuple-element.36), channel_id=1, source_target_pairs={{0,8},{4,12},{8,0},{12,4},{16,24},{20,28},{24,16},{28,20},{1,9},{5... | collective-permute-start | bytes 110600 | tf_op jit(solution)/shard_map/ppermute | solution.py:342
  30.3 3.2 %collective-permute-start.9 = (bf16[144,128]{1,0:T(8,128)(2,1)S(1)}, bf16[144,128]{1,0:T(8,128)(2,1)S(1)}, u32[]{:S(2)}, u32[]{:S(2)}) collective-permute-start(bf16[144,128]{1,0:T(8,128)(2,1)S(1)} %get-tuple-element.37), channel_id=1, source_target_pairs={{0,16},{4,20},{8,24},{12,28},{16,0},{20,4},{24,8},{28,12},{1,17},{... | collective-permute-start | bytes 110600 | tf_op jit(solution)/shard_map/ppermute | solution.py:342
  33.5 0.6 collective-permute-start.10
  34.1 0.1 merge.3
  34.2 0.7 %collective-permute-start.12 = (bf16[144,128]{1,0:T(8,128)(2,1)S(1)}, bf16[144,128]{1,0:T(8,128)(2,1)S(1)}, u32[]{:S(2)}, u32[]{:S(2)}) collective-permute-start(bf16[144,128]{1,0:T(8,128)(2,1)S(1)} %get-tuple-element.42), channel_id=1, source_target_pairs={{0,8},{4,12},{8,0},{12,4},{16,24},{20,28},{24,16},{28,20},{1,9},{5... | collective-permute-start | bytes 110600 | tf_op jit(solution)/shard_map/ppermute | solution.py:342
  34.9 3.2 %collective-permute-start.13 = (bf16[144,128]{1,0:T(8,128)(2,1)S(1)}, bf16[144,128]{1,0:T(8,128)(2,1)S(1)}, u32[]{:S(2)}, u32[]{:S(2)}) collective-permute-start(bf16[144,128]{1,0:T(8,128)(2,1)S(1)} %get-tuple-element.43), channel_id=1, source_target_pairs={{0,16},{4,20},{8,24},{12,28},{16,0},{20,4},{24,8},{28,12},{1,17},{... | collective-permute-start | bytes 110600 | tf_op jit(solution)/shard_map/ppermute | solution.py:342
  38.1 0.0 collective-permute-done.8.refs_1_
  38.1 0.6 collective-permute-start.14
  38.7 0.0 collective-permute-done.9.refs_2_
  38.7 0.6 collective-permute-done.10.refs_3_
  39.3 0.0 collective-permute-done.12.refs_5_
  39.3 0.8 %collective-permute-done.13.refs_6_ = bf16[144,128]{1,0:T(8,128)(2,1)S(1)} collective-permute-done((bf16[144,128]{1,0:T(8,128)(2,1)S(1)}, bf16[144,128]{1,0:T(8,128)(2,1)S(1)}, u32[]{:S(2)}, u32[]{:S(2)}) %collective-permute-start.13) | collective-permute-done | bytes 36896 | tf_op jit(solution)/shard_map/ppermute | solution.py:342
  40.0 3.8 %collective-permute-done.14.refs_7_ = bf16[144,128]{1,0:T(8,128)(2,1)S(1)} collective-permute-done((bf16[144,128]{1,0:T(8,128)(2,1)S(1)}, bf16[144,128]{1,0:T(8,128)(2,1)S(1)}, u32[]{:S(2)}, u32[]{:S(2)}) %collective-permute-start.14) | collective-permute-done | bytes 36896 | tf_op jit(solution)/shard_map/ppermute | solution.py:342
  44.0 2.9 %up_and_far_output.1 = (bf16[4,4,896]{2,1,0:T(4,128)(2,1)S(1)}, f32[8,2048]{1,0:T(8,128)S(1)}) custom-call(bf16[144,128]{1,0:T(8,128)(2,1)S(1)} %get-tuple-element.35.refs_0_, bf16[144,128]{1,0:T(8,128)(2,1)S(1)} %collective-permute-done.8.refs_1_, bf16[144,128]{1,0:T(8,128)(2,1)S(1)} %collective-permute-done.9.refs_2_, ...), custom_call_target="tpu_custom_call" | custom-call | flops 20000000000 | bytes 1048576 | tf_op jit(solution)/shard_map/up_and_far_output/pallas_call | solution.py:407
  46.8 0.0 collective-permute-start.15
  46.8 2.1 %near_output.1.own_ref = f32[4,4,896]{2,1,0:T(4,128)S(1)} custom-call(f32[8,2048]{1,0:T(8,128)S(1)} %get-tuple-element.45.values, bf16[2048,7168]{1,0:T(8,128)(2,1)S(1)} %bitcast.5), custom_call_target="tpu_custom_call" | custom-call | flops 20000000000 | bytes 1048576 | tf_op jit(solution)/shard_map/near_output/pallas_call | solution.py:418
  49.0 1.7 %collective-permute-done.15.other_ref = bf16[4,4,896]{2,1,0:T(4,128)(2,1)S(1)} collective-permute-done((bf16[4,4,896]{2,1,0:T(4,128)(2,1)S(1)}, bf16[4,4,896]{2,1,0:T(4,128)(2,1)S(1)}, u32[]{:S(2)}, u32[]{:S(2)}) %collective-permute-start.15) | collective-permute-done | bytes 28704 | tf_op jit(solution)/shard_map/ppermute | solution.py:342
  50.7 0.9 %collective-permute-start.16 = (bf16[4,896]{1,0:T(4,128)(2,1)S(1)}, bf16[4,896]{1,0:T(4,128)(2,1)S(1)}, u32[]{:S(2)}, u32[]{:S(2)}) collective-permute-start(bf16[4,896]{1,0:T(4,128)(2,1)S(1)} %get-tuple-element.48), channel_id=1, source_target_pairs={{0,4},{4,0},{8,12},{12,8},{16,20},{20,16},{24,28},{28,24},{1,5},{5... | collective-permute-start | bytes 21512 | tf_op jit(solution)/shard_map/ppermute | solution.py:342
  51.6 3.6 %collective-permute-start.18 = (bf16[4,896]{1,0:T(4,128)(2,1)S(1)}, bf16[4,896]{1,0:T(4,128)(2,1)S(1)}, u32[]{:S(2)}, u32[]{:S(2)}) collective-permute-start(bf16[4,896]{1,0:T(4,128)(2,1)S(1)} %get-tuple-element.50), channel_id=1, source_target_pairs={{0,20},{4,16},{8,28},{12,24},{16,4},{20,0},{24,12},{28,8},{1,21},{... | collective-permute-start | bytes 21512 | tf_op jit(solution)/shard_map/ppermute | solution.py:342
  55.2 1.0 %collective-permute-done.17.refs_1_ = bf16[4,896]{1,0:T(4,128)(2,1)S(1)} collective-permute-done((bf16[4,896]{1,0:T(4,128)(2,1)S(1)}, bf16[4,896]{1,0:T(4,128)(2,1)S(1)}, u32[]{:S(2)}, u32[]{:S(2)}) %collective-permute-start.17) | collective-permute-done | bytes 7200 | tf_op jit(solution)/shard_map/ppermute | solution.py:342
  56.1 0.9 %collective-permute-done.18.refs_2_ = bf16[4,896]{1,0:T(4,128)(2,1)S(1)} collective-permute-done((bf16[4,896]{1,0:T(4,128)(2,1)S(1)}, bf16[4,896]{1,0:T(4,128)(2,1)S(1)}, u32[]{:S(2)}, u32[]{:S(2)}) %collective-permute-start.18) | collective-permute-done | bytes 7200 | tf_op jit(solution)/shard_map/ppermute | solution.py:342
  57.0 0.6 %sum_output.1 = bf16[2,2,896]{2,1,0:T(2,128)(2,1)} custom-call(f32[4,896]{1,0:T(4,128)S(1)} %get-tuple-element.47.own_ref, bf16[4,896]{1,0:T(4,128)(2,1)S(1)} %collective-permute-done.16.refs_0_, bf16[4,896]{1,0:T(4,128)(2,1)S(1)} %collective-permute-done.17.refs_1_, bf16[4,896]{1,0:T(4,128)(2,1)S(1)} %collective-permute-done.18.refs_2_), custom_call_target="tpu_custom_call" | custom-call | tf_op jit(solution)/shard_map/sum_output/pallas_call | solution.py:433
  (19 shorter events, 0.1 us)
Async XLA Ops:
  1.8 8.4 %collective-permute-start = (bf16[288,128]{1,0:T(8,128)(2,1)S(1)}, bf16[288,128]{1,0:T(8,128)(2,1)S(1)}, u32[]{:S(2)}, u32[]{:S(2)}) collective-permute-start(bf16[288,128]{1,0:T(8,128)(2,1)S(1)} %get-tuple-element.28.refs_0_), channel_id=1, source_target_pairs={{0,8},{4,12},{8,0},{12,4},{16,24},{20,28},{24,16},{28,20},{1,9},{5... | collective-permute-start | bytes 221192 | tf_op jit(solution)/shard_map/ppermute | solution.py:342
  4.9 7.8 %collective-permute-start.1 = (bf16[288,128]{1,0:T(8,128)(2,1)S(1)}, bf16[288,128]{1,0:T(8,128)(2,1)S(1)}, u32[]{:S(2)}, u32[]{:S(2)}) collective-permute-start(bf16[288,128]{1,0:T(8,128)(2,1)S(1)} %get-tuple-element.28.refs_0_), channel_id=1, source_target_pairs={{0,16},{4,20},{8,24},{12,28},{16,0},{20,4},{24,8},{28,12},{1,17},{... | collective-permute-start | bytes 221192 | tf_op jit(solution)/shard_map/ppermute | solution.py:342
  7.5 6.7 %collective-permute-start.2 = (bf16[288,128]{1,0:T(8,128)(2,1)S(1)}, bf16[288,128]{1,0:T(8,128)(2,1)S(1)}, u32[]{:S(2)}, u32[]{:S(2)}) collective-permute-start(bf16[288,128]{1,0:T(8,128)(2,1)S(1)} %get-tuple-element.28.refs_0_), channel_id=1, source_target_pairs={{0,24},{4,28},{8,16},{12,20},{16,8},{20,12},{24,0},{28,4},{1,25},{... | collective-permute-start | bytes 221192 | tf_op jit(solution)/shard_map/ppermute | solution.py:342
  7.5 11.0 %copy-start = (bf16[2,4096,576]{1,2,0:T(8,128)(2,1)S(1)}, bf16[2,4096,576]{1,2,0:T(8,128)(2,1)}, u32[]{:S(2)}) copy-start(bf16[2,4096,576]{1,2,0:T(8,128)(2,1)} %param.11) | copy-start | bytes 28311556
  8.5 6.8 %collective-permute-start.3 = (bf16[288,128]{1,0:T(8,128)(2,1)S(1)}, bf16[288,128]{1,0:T(8,128)(2,1)S(1)}, u32[]{:S(2)}, u32[]{:S(2)}) collective-permute-start(bf16[288,128]{1,0:T(8,128)(2,1)S(1)} %get-tuple-element.30), channel_id=1, source_target_pairs={{0,4},{4,0},{8,12},{12,8},{16,20},{20,16},{24,28},{28,24},{1,5},{5... | collective-permute-start | bytes 221192 | tf_op jit(solution)/shard_map/ppermute | solution.py:342
  10.2 5.0 %collective-permute-start.4 = (bf16[288,128]{1,0:T(8,128)(2,1)S(1)}, bf16[288,128]{1,0:T(8,128)(2,1)S(1)}, u32[]{:S(2)}, u32[]{:S(2)}) collective-permute-start(bf16[288,128]{1,0:T(8,128)(2,1)S(1)} %collective-permute-done.refs_1_), channel_id=1, source_target_pairs={{0,4},{4,0},{8,12},{12,8},{16,20},{20,16},{24,28},{28,24},{1,5},{5... | collective-permute-start | bytes 221192 | tf_op jit(solution)/shard_map/ppermute | solution.py:342
  12.7 4.4 %collective-permute-start.5 = (bf16[288,128]{1,0:T(8,128)(2,1)S(1)}, bf16[288,128]{1,0:T(8,128)(2,1)S(1)}, u32[]{:S(2)}, u32[]{:S(2)}) collective-permute-start(bf16[288,128]{1,0:T(8,128)(2,1)S(1)} %collective-permute-done.1.refs_2_), channel_id=1, source_target_pairs={{0,4},{4,0},{8,12},{12,8},{16,20},{20,16},{24,28},{28,24},{1,5},{5... | collective-permute-start | bytes 221192 | tf_op jit(solution)/shard_map/ppermute | solution.py:342
  14.2 4.4 %collective-permute-start.6 = (bf16[288,128]{1,0:T(8,128)(2,1)S(1)}, bf16[288,128]{1,0:T(8,128)(2,1)S(1)}, u32[]{:S(2)}, u32[]{:S(2)}) collective-permute-start(bf16[288,128]{1,0:T(8,128)(2,1)S(1)} %collective-permute-done.2.refs_3_), channel_id=1, source_target_pairs={{0,4},{4,0},{8,12},{12,8},{16,20},{20,16},{24,28},{28,24},{1,5},{5... | collective-permute-start | bytes 221192 | tf_op jit(solution)/shard_map/ppermute | solution.py:342
  22.8 21.1 %slice-start = ((s8[29360128]{0:T(1024)(128)(4,1)}), s8[4194304]{0:T(1024)(128)(4,1)S(1)}, s32[]{:S(2)}) async-start(s8[29360128]{0:T(1024)(128)(4,1)} %bitcast.4), calls=%async_computation | async-start | bytes 8388608
  22.8 21.1 %slice-start.1 = ((s8[29360128]{0:T(1024)(128)(4,1)}), s8[4194304]{0:T(1024)(128)(4,1)S(1)}, s32[]{:S(2)}) async-start(s8[29360128]{0:T(1024)(128)(4,1)} %bitcast.4), calls=%async_computation.1 | async-start | bytes 8388608
  22.8 21.1 %slice-start.2 = ((s8[29360128]{0:T(1024)(128)(4,1)}), s8[4194304]{0:T(1024)(128)(4,1)S(1)}, s32[]{:S(2)}) async-start(s8[29360128]{0:T(1024)(128)(4,1)} %bitcast.4), calls=%async_computation.2 | async-start | bytes 8388608
  22.8 21.1 %slice-start.3 = ((s8[29360128]{0:T(1024)(128)(4,1)}), s8[4194304]{0:T(1024)(128)(4,1)S(1)}, s32[]{:S(2)}) async-start(s8[29360128]{0:T(1024)(128)(4,1)} %bitcast.4), calls=%async_computation.3 | async-start | bytes 8388608
  22.8 21.1 %slice-start.4 = ((s8[29360128]{0:T(1024)(128)(4,1)}), s8[4194304]{0:T(1024)(128)(4,1)S(1)}, s32[]{:S(2)}) async-start(s8[29360128]{0:T(1024)(128)(4,1)} %bitcast.4), calls=%async_computation.4 | async-start | bytes 8388608
  22.9 21.1 %slice-start.5 = ((s8[29360128]{0:T(1024)(128)(4,1)}), s8[4194304]{0:T(1024)(128)(4,1)S(1)}, s32[]{:S(2)}) async-start(s8[29360128]{0:T(1024)(128)(4,1)} %bitcast.4), calls=%async_computation.5 | async-start | bytes 8388608
  22.9 21.1 %slice-start.6 = ((s8[29360128]{0:T(1024)(128)(4,1)}), s8[4194304]{0:T(1024)(128)(4,1)S(1)}, s32[]{:S(2)}) async-start(s8[29360128]{0:T(1024)(128)(4,1)} %bitcast.4), calls=%async_computation.6 | async-start | bytes 8388608
  22.9 21.1 %copy-start.1 = (bf16[16,512,128]{2,1,0:T(8,128)(2,1)S(1)}, bf16[16,512,128]{2,1,0:T(8,128)(2,1)}, u32[]{:S(2)}) copy-start(bf16[16,512,128]{2,1,0:T(8,128)(2,1)} %refs_8_.1) | copy-start | bytes 6291460
  22.9 6.6 %collective-permute-start.7 = (bf16[4,144,128]{2,1,0:T(8,128)(2,1)S(1)}, bf16[4,144,128]{2,1,0:T(8,128)(2,1)S(1)}, u32[]{:S(2)}, u32[]{:S(2)}) collective-permute-start(bf16[4,144,128]{2,1,0:T(8,128)(2,1)S(1)} %get-tuple-element.34), channel_id=1, source_target_pairs={{0,4},{4,0},{8,12},{12,8},{16,20},{20,16},{24,28},{28,24},{1,5},{5... | collective-permute-start | bytes 442376 | tf_op jit(solution)/shard_map/ppermute | solution.py:342
  28.4 5.7 %collective-permute-start.11 = (bf16[4,144,128]{2,1,0:T(8,128)(2,1)S(1)}, bf16[4,144,128]{2,1,0:T(8,128)(2,1)S(1)}, u32[]{:S(2)}, u32[]{:S(2)}) collective-permute-start(bf16[4,144,128]{2,1,0:T(8,128)(2,1)S(1)} %get-tuple-element.40), channel_id=1, source_target_pairs={{0,4},{4,0},{8,12},{12,8},{16,20},{20,16},{24,28},{28,24},{1,5},{5... | collective-permute-start | bytes 442376 | tf_op jit(solution)/shard_map/ppermute | solution.py:342
  29.6 8.5 %collective-permute-start.8 = (bf16[144,128]{1,0:T(8,128)(2,1)S(1)}, bf16[144,128]{1,0:T(8,128)(2,1)S(1)}, u32[]{:S(2)}, u32[]{:S(2)}) collective-permute-start(bf16[144,128]{1,0:T(8,128)(2,1)S(1)} %get-tuple-element.36), channel_id=1, source_target_pairs={{0,8},{4,12},{8,0},{12,4},{16,24},{20,28},{24,16},{28,20},{1,9},{5... | collective-permute-start | bytes 110600 | tf_op jit(solution)/shard_map/ppermute | solution.py:342
  30.3 8.4 %collective-permute-start.9 = (bf16[144,128]{1,0:T(8,128)(2,1)S(1)}, bf16[144,128]{1,0:T(8,128)(2,1)S(1)}, u32[]{:S(2)}, u32[]{:S(2)}) collective-permute-start(bf16[144,128]{1,0:T(8,128)(2,1)S(1)} %get-tuple-element.37), channel_id=1, source_target_pairs={{0,16},{4,20},{8,24},{12,28},{16,0},{20,4},{24,8},{28,12},{1,17},{... | collective-permute-start | bytes 110600 | tf_op jit(solution)/shard_map/ppermute | solution.py:342
  33.5 5.8 %collective-permute-start.10 = (bf16[144,128]{1,0:T(8,128)(2,1)S(1)}, bf16[144,128]{1,0:T(8,128)(2,1)S(1)}, u32[]{:S(2)}, u32[]{:S(2)}) collective-permute-start(bf16[144,128]{1,0:T(8,128)(2,1)S(1)} %get-tuple-element.38), channel_id=1, source_target_pairs={{0,24},{4,28},{8,16},{12,20},{16,8},{20,12},{24,0},{28,4},{1,25},{... | collective-permute-start | bytes 110600 | tf_op jit(solution)/shard_map/ppermute | solution.py:342
  34.2 5.0 %collective-permute-start.12 = (bf16[144,128]{1,0:T(8,128)(2,1)S(1)}, bf16[144,128]{1,0:T(8,128)(2,1)S(1)}, u32[]{:S(2)}, u32[]{:S(2)}) collective-permute-start(bf16[144,128]{1,0:T(8,128)(2,1)S(1)} %get-tuple-element.42), channel_id=1, source_target_pairs={{0,8},{4,12},{8,0},{12,4},{16,24},{20,28},{24,16},{28,20},{1,9},{5... | collective-permute-start | bytes 110600 | tf_op jit(solution)/shard_map/ppermute | solution.py:342
  34.9 5.1 %collective-permute-start.13 = (bf16[144,128]{1,0:T(8,128)(2,1)S(1)}, bf16[144,128]{1,0:T(8,128)(2,1)S(1)}, u32[]{:S(2)}, u32[]{:S(2)}) collective-permute-start(bf16[144,128]{1,0:T(8,128)(2,1)S(1)} %get-tuple-element.43), channel_id=1, source_target_pairs={{0,16},{4,20},{8,24},{12,28},{16,0},{20,4},{24,8},{28,12},{1,17},{... | collective-permute-start | bytes 110600 | tf_op jit(solution)/shard_map/ppermute | solution.py:342
  38.1 5.8 %collective-permute-start.14 = (bf16[144,128]{1,0:T(8,128)(2,1)S(1)}, bf16[144,128]{1,0:T(8,128)(2,1)S(1)}, u32[]{:S(2)}, u32[]{:S(2)}) collective-permute-start(bf16[144,128]{1,0:T(8,128)(2,1)S(1)} %get-tuple-element.44), channel_id=1, source_target_pairs={{0,24},{4,28},{8,16},{12,20},{16,8},{20,12},{24,0},{28,4},{1,25},{... | collective-permute-start | bytes 110600 | tf_op jit(solution)/shard_map/ppermute | solution.py:342
  46.8 3.9 %collective-permute-start.15 = (bf16[4,4,896]{2,1,0:T(4,128)(2,1)S(1)}, bf16[4,4,896]{2,1,0:T(4,128)(2,1)S(1)}, u32[]{:S(2)}, u32[]{:S(2)}) collective-permute-start(bf16[4,4,896]{2,1,0:T(4,128)(2,1)S(1)} %get-tuple-element.46), channel_id=1, source_target_pairs={{0,8},{4,12},{8,0},{12,4},{16,24},{20,28},{24,16},{28,20},{1,9},{5... | collective-permute-start | bytes 86024 | tf_op jit(solution)/shard_map/ppermute | solution.py:342
  50.7 4.5 %collective-permute-start.16 = (bf16[4,896]{1,0:T(4,128)(2,1)S(1)}, bf16[4,896]{1,0:T(4,128)(2,1)S(1)}, u32[]{:S(2)}, u32[]{:S(2)}) collective-permute-start(bf16[4,896]{1,0:T(4,128)(2,1)S(1)} %get-tuple-element.48), channel_id=1, source_target_pairs={{0,4},{4,0},{8,12},{12,8},{16,20},{20,16},{24,28},{28,24},{1,5},{5... | collective-permute-start | bytes 21512 | tf_op jit(solution)/shard_map/ppermute | solution.py:342
  51.6 4.5 %collective-permute-start.17 = (bf16[4,896]{1,0:T(4,128)(2,1)S(1)}, bf16[4,896]{1,0:T(4,128)(2,1)S(1)}, u32[]{:S(2)}, u32[]{:S(2)}) collective-permute-start(bf16[4,896]{1,0:T(4,128)(2,1)S(1)} %get-tuple-element.49), channel_id=1, source_target_pairs={{0,16},{4,20},{8,24},{12,28},{16,0},{20,4},{24,8},{28,12},{1,17},{... | collective-permute-start | bytes 21512 | tf_op jit(solution)/shard_map/ppermute | solution.py:342
  51.6 5.4 %collective-permute-start.18 = (bf16[4,896]{1,0:T(4,128)(2,1)S(1)}, bf16[4,896]{1,0:T(4,128)(2,1)S(1)}, u32[]{:S(2)}, u32[]{:S(2)}) collective-permute-start(bf16[4,896]{1,0:T(4,128)(2,1)S(1)} %get-tuple-element.50), channel_id=1, source_target_pairs={{0,20},{4,16},{8,28},{12,24},{16,4},{20,0},{24,12},{28,8},{1,21},{... | collective-permute-start | bytes 21512 | tf_op jit(solution)/shard_map/ppermute | solution.py:342

commit v2 on v1

--- a/solution.py
+++ b/solution.py
@@ -70,31 +70,36 @@
     again_ref[...] = out_ref[...]
 
 
-def column_kernel(rate_ref, scale_ref, through_ref, inv_rate_ref, scales_ref, passed_ref):
+def lanes_kernel(rate_ref, scale_ref, through_ref, inv_rate_ref, scales_ref, passed_ref, *, ctx):
     del through_ref, passed_ref
-    ctx, heads, _ = inv_rate_ref.shape
     line = ctx // 2
     me = lax.axis_index("ctx")
     for source, target in ((1.0 / rate_ref[...], inv_rate_ref), (scale_ref[...], scales_ref)):
         size = source.shape[1]
+        heads = size // ctx
         same = lax.broadcasted_iota(jnp.int32, (size, size), 0) == lax.broadcasted_iota(
             jnp.int32, (size, size), 1
         )
         column = jnp.sum(jnp.where(same, source, 0.0), axis=1, keepdims=True)
         column = jnp.broadcast_to(column, (size, LANES)).reshape(ctx, heads, LANES)
+        rows = []
         for k in range(ctx):
             owner = me ^ (2 * (k % line) + k // line)
             picked = jnp.zeros((heads, LANES), jnp.float32)
             for device in range(ctx):
                 picked = jnp.where(owner == device, column[device], picked)
-            target[k] = picked
+            rows += [picked, picked]
+        rows = jnp.concatenate(rows, axis=0)
+        for i in range(rows.shape[0] // LANES):
+            at = slice(i * LANES, (i + 1) * LANES)
+            target[:, at] = rows[at].T[: target.shape[0]]
 
 
 def attention_kernel(pages_ref, lengths_ref, *refs, ctx, b):
     query_refs, refs = refs[:ctx], refs[ctx:]
-    cache_ref, inv_rate, scale, near_ref, far_ref, query, acc, total, *buffers = refs
+    cache_ref, inv_rate, scale, near_ref, far_ref, query, acc, *buffers = refs
     scores_of, weights_of, factor_of = buffers[:2], buffers[2:4], buffers[4:]
-    rows, chunk = scores_of[0].shape
+    chunk, rows = scores_of[0].shape
     half = rows // ctx
     heads = half // 2
     line = ctx // 2
@@ -112,35 +117,35 @@
             ]
         query[own, LAT:] = block[2 * request_rows :, b * ROPE : (b + 1) * ROPE]
 
-    lane = lax.broadcasted_iota(jnp.int32, (heads, LANES), 1)
     first_pos = lengths_ref[b] - 2
+    token = lax.rem(lax.broadcasted_iota(jnp.int32, (1, rows), 1) // heads, 2)
+    own_rate, own_scale = inv_rate[0:1, :], scale[0:1, :]
+    slot = lax.broadcasted_iota(jnp.int32, (PAGE, rows), 0)
 
     def raw_scores(at):
-        return jnp.dot(
+        return lax.dot_general(
+            cache_ref[b, :, at * pair_width : (at + 1) * pair_width],
             query[...],
-            cache_ref[b, :, at * pair_width : (at + 1) * pair_width],
+            (((0,), (1,)), ((), ())),
             preferred_element_type=jnp.float32,
         )
 
     def add_products(step):
         weights, factor = weights_of[step % 2], factor_of[step % 2]
-        for columns in (slice(0, LAT // 2), slice(LAT // 2, LAT)):
-            new = lax.dot_general(
+        for at in (slice(0, LAT // 2), slice(LAT // 2, LAT)):
+            new = jnp.dot(
+                cache_ref[b, at, step * chunk : (step + 1) * chunk],
                 weights[...],
-                cache_ref[b, columns, step * chunk : (step + 1) * chunk],
-                (((1,), (1,)), ((), ())),
                 preferred_element_type=jnp.float32,
             )
-            for j in range(columns.start, columns.stop, LANES):
-                part = new[:, j - columns.start : j - columns.start + LANES]
-                at = slice(j, j + LANES)
-                acc[:, at] = acc[:, at] * factor[...] + part if step else part
-
-    top = jnp.full((rows, LANES), LOWEST, jnp.float32)
+            acc[at, :] = acc[at, :] * factor[0:1, :] + new if step else new
+
+    top = jnp.full((1, rows), LOWEST, jnp.float32)
+    total = jnp.zeros((1, rows), jnp.float32)
     ahead = raw_scores(0)
     for step in range(steps):
         scores, weights = scores_of[step % 2], weights_of[step % 2]
-        tops = [None, None]
+        tops = jnp.full((8, rows), LOWEST, jnp.float32)
         for pair in range(pairs):
             raw = ahead
             at = step * pairs + pair
@@ -148,45 +153,51 @@
                 ahead = raw_scores(at + 1)
             for side in range(2):
                 page = pair * 2 + side
-                columns = slice(page * PAGE, (page + 1) * PAGE)
-                part = raw[:, side * PAGE : (side + 1) * PAGE].reshape(ctx, 2, heads, PAGE)
                 base = first_pos - pages_ref[b, step * (chunk // PAGE) + page] * PAGE
-                values = []
-                for q in range(2):
-                    distance = base + q - lane
-                    spread = jnp.where(distance >= 0, distance.astype(jnp.float32), jnp.inf)
-                    logs = jnp.log2(spread[None] + inv_rate[...])
-                    value = part[:, q] * (SOFTMAX_SCALE * LOG2E) - scale[...] * logs
-                    tops[q] = value if tops[q] is None else jnp.maximum(tops[q], value)
-                    values.append(value)
-                scores[:, columns] = jnp.stack(values, axis=1).reshape(rows, PAGE)
-        lane_top = jnp.stack(tops, axis=1).reshape(rows, LANES)
+                distance = (base + token) - slot
+                spread = jnp.where(distance >= 0, distance.astype(jnp.float32), jnp.inf)
+                logs = jnp.log2(spread + own_rate)
+                value = (
+                    raw[side * PAGE : (side + 1) * PAGE] * (SOFTMAX_SCALE * LOG2E)
+                    - own_scale * logs
+                )
+                tops = jnp.maximum(tops, jnp.max(value.reshape(PAGE // 8, 8, rows), axis=0))
+                scores[page * PAGE : (page + 1) * PAGE, :] = value
         before = top
-        top = jnp.maximum(before, jnp.max(lane_top, axis=1, keepdims=True))
+        top = jnp.maximum(before, jnp.max(tops, axis=0, keepdims=True))
         factor = jnp.exp2(before - top)
-        factor_of[step % 2][...] = factor
+        factor_of[step % 2][...] = jnp.broadcast_to(factor, (8, rows))
         if step:
             add_products(step - 1)
-        lane_total = total[...] * factor if step else jnp.zeros((rows, LANES), jnp.float32)
+        sums = jnp.zeros((8, rows), jnp.float32)
         for page in range(chunk // PAGE):
-            columns = slice(page * PAGE, (page + 1) * PAGE)
-            value = jnp.exp2(scores[:, columns] - top)
-            lane_total += value
-            weights[:, columns] = value.astype(jnp.bfloat16)
-        total[...] = lane_total
+            at = slice(page * PAGE, (page + 1) * PAGE)
+            value = jnp.exp2(scores[at, :] - top)
+            sums += jnp.sum(value.reshape(PAGE // 8, 8, rows), axis=0)
+            weights[at, :] = value.astype(jnp.bfloat16)
+        total = total * factor + jnp.sum(sums, axis=0, keepdims=True)
     add_products(steps - 1)
 
-    row_total = jnp.sum(total[...], axis=1, keepdims=True)
-    row_total = jnp.broadcast_to(row_total, (rows, LANES))
-    seen = row_total > 0.0
-    safe = jnp.where(seen, row_total, 1.0)
+    seen = total > 0.0
+    safe = jnp.where(seen, total, 1.0)
     share = 1.0 / safe
-    for j in range(LAT_TILES):
-        columns = slice(j * LANES, (j + 1) * LANES)
-        part = (acc[:, columns] * share).astype(jnp.bfloat16).reshape(ctx, half, LANES)
-        near_ref[:, j * half : (j + 1) * half, :] = part[:line]
-        far_ref[:, j * half : (j + 1) * half, :] = part[line:]
-    log_total = jnp.where(seen, top + jnp.log2(safe), LOWEST).reshape(ctx, half, LANES)
+    logs = jnp.where(seen, top + jnp.log2(safe), LOWEST)
+    logs = jnp.broadcast_to(logs, (LANES, rows))
+    turned = []
+    for i in range(rows // LANES):
+        at = slice(i * LANES, (i + 1) * LANES)
+        turned.append(logs[:, at].T)
+        first, count = i * LANES // half, LANES // half
+        for j in range(LAT_TILES):
+            part = (acc[j * LANES : (j + 1) * LANES, at] * share[:, at]).T
+            part = part.astype(jnp.bfloat16).reshape(count, half, LANES)
+            for k in range(count):
+                to_ref, block = (near_ref, first + k) if first + k < line else (
+                    far_ref,
+                    first + k - line,
+                )
+                to_ref[block, j * half : (j + 1) * half, :] = part[k]
+    log_total = jnp.concatenate(turned, axis=0).reshape(ctx, half, LANES)
     across = jnp.sum(jnp.where(diagonal(half), log_total, 0.0), axis=1, keepdims=True)
     packed = three_parts(across).astype(jnp.bfloat16)
     near_ref[:, request_rows:, :] = packed[:line]
@@ -352,18 +363,18 @@
         compiler_params=pltpu.CompilerParams(vmem_limit_bytes=8 * 2**20),
         name="latent_query",
     )(in_hbm(queries.reshape(rows, query_width)), in_hbm(key_absorb))
-    columns = (ctx, heads, LANES)
+    by_row = (8, ctx * half)
     inv_rate, scale, again = pl.pallas_call(
-        column_kernel,
+        functools.partial(lanes_kernel, ctx=ctx),
         in_specs=[pl.BlockSpec(memory_space=pltpu.VMEM)] * 2
         + [pl.BlockSpec(memory_space=pl.ANY)],
         out_specs=[pl.BlockSpec(memory_space=pltpu.VMEM)] * 2
         + [pl.BlockSpec(memory_space=pl.ANY)],
-        out_shape=[jax.ShapeDtypeStruct(columns, jnp.float32)] * 2
+        out_shape=[jax.ShapeDtypeStruct(by_row, jnp.float32)] * 2
         + [jax.ShapeDtypeStruct(again.shape, again.dtype)],
         input_output_aliases={2: 2},
         compiler_params=pltpu.CompilerParams(vmem_limit_bytes=4 * 2**20),
-        name="head_columns",
+        name="head_lanes",
         cost_estimate=long_hint,
     )(in_hbm(kerple_rate.reshape(1, -1)), in_hbm(kerple_scale.reshape(1, -1)), again)
     column = [packed] + [swap(packed, 2 * k) for k in range(1, line)]
@@ -382,12 +393,11 @@
             out_shape=[jax.ShapeDtypeStruct((line,) + message, jnp.bfloat16)] * 2,
             scratch_shapes=[
                 pltpu.VMEM((all_rows, LAT + ROPE), jnp.bfloat16),
-                pltpu.VMEM((all_rows, LAT), jnp.float32),
-                pltpu.VMEM((all_rows, LANES), jnp.float32),
+                pltpu.VMEM((LAT, all_rows), jnp.float32),
             ]
-            + [pltpu.VMEM((all_rows, chunk), jnp.float32)] * 2
-            + [pltpu.VMEM((all_rows, chunk), jnp.bfloat16)] * 2
-            + [pltpu.VMEM((all_rows, LANES), jnp.float32)] * 2,
+            + [pltpu.VMEM((chunk, all_rows), jnp.float32)] * 2
+            + [pltpu.VMEM((chunk, all_rows), jnp.bfloat16)] * 2
+            + [pltpu.VMEM((8, all_rows), jnp.float32)] * 2,
             compiler_params=pltpu.CompilerParams(vmem_limit_bytes=8 * 2**20),
             cost_estimate=hint,
             name="attention",

time: 57.8 us -> 58.7 us (1.016)
  Pallas kernels: 17.4 us -> 18.3 us
    pallas_call x2, Pallas kernels: 8.66 us -> 9.54 us  [per_device(): pl.pallas_call(functools.partial(attention_kernel, ctx=ctx, b=b), in_spec...]
  transfers between devices with their start and end apart: 19 -> 19, of which waited for: 9 -> 10; matrix products, arithmetic and copies ran while one was open for 0% -> 0% of each run, Pallas kernels for 14% -> 14%
where the time goes in v2:
time: 58.7 us; the launch traced here: 58.6 us
  starting transfers between devices  25.8 us (44%)
  Pallas kernels  18.3 us (31%)
  waiting for transfers between devices  14.2 us (24%)
    ppermute x19, starting transfers between devices, per_device(): lax.ppermute(value, 'ctx', [(i, i ^ bits) for i in range(ctx)])  25.8 us
    ppermute x19, waiting for transfers between devices, per_device(): lax.ppermute(value, 'ctx', [(i, i ^ bits) for i in range(ctx)])  14.2 us
    pallas_call x2, Pallas kernels, per_device(): pl.pallas_call(functools.partial(attention_kernel, ctx=ctx, b=b), in_spec...  9.54 us
    pallas_call x1, Pallas kernels, per_device(): pl.pallas_call(output_kernel, out_shape=[jax.ShapeDtypeStruct((line, toke...  2.88 us
    pallas_call x1, Pallas kernels, per_device(): pl.pallas_call(near_kernel, out_shape=jax.ShapeDtypeStruct((line, tokens,...  2.14 us
    pallas_call x1, Pallas kernels, per_device(): pl.pallas_call(query_kernel, in_specs=[pl.BlockSpec(memory_space=pl.ANY)]...  1.8 us
  transfers between devices with their start and end apart: 19, of which 10 were waited for; matrix products, arithmetic and copies ran while one was open for 0% of the time, Pallas kernels for 14%

profile of v2, /device:TPU:0, one launch (start us, length us, event | category | flops | bytes accessed | tf_op | source)
XLA Modules:
  0.0 58.6 jit_solution(14687728968376149647)
XLA Ops:
  0.0 1.8 %latent_query.1 = (bf16[288,128]{1,0:T(8,128)(2,1)S(1)}, bf16[288,128]{1,0:T(8,128)(2,1)S(1)}) custom-call(bf16[64,192]{1,0:T(8,128)(2,1)} %bitcast.8, bf16[16,128,512]{2,1,0:T(8,128)(2,1)} %absorb_hbm.1), custom_call_target="tpu_custom_call" | custom-call | tf_op jit(solution)/shard_map/latent_query/pallas_call | solution.py:354
  1.8 3.1 %collective-permute-start = (bf16[288,128]{1,0:T(8,128)(2,1)S(1)}, bf16[288,128]{1,0:T(8,128)(2,1)S(1)}, u32[]{:S(2)}, u32[]{:S(2)}) collective-permute-start(bf16[288,128]{1,0:T(8,128)(2,1)S(1)} %get-tuple-element.28.refs_0_), channel_id=1, source_target_pairs={{0,8},{4,12},{8,0},{12,4},{16,24},{20,28},{24,16},{28,20},{1,9},{5... | collective-permute-start | bytes 221192 | tf_op jit(solution)/shard_map/ppermute | solution.py:353
  4.9 2.6 %collective-permute-start.1 = (bf16[288,128]{1,0:T(8,128)(2,1)S(1)}, bf16[288,128]{1,0:T(8,128)(2,1)S(1)}, u32[]{:S(2)}, u32[]{:S(2)}) collective-permute-start(bf16[288,128]{1,0:T(8,128)(2,1)S(1)} %get-tuple-element.28.refs_0_), channel_id=1, source_target_pairs={{0,16},{4,20},{8,24},{12,28},{16,0},{20,4},{24,8},{28,12},{1,17},{... | collective-permute-start | bytes 221192 | tf_op jit(solution)/shard_map/ppermute | solution.py:353
  7.5 0.0 collective-permute-start.2
  7.5 1.0 %head_lanes.1 = (f32[8,256]{1,0:T(8,128)S(1)}, f32[8,256]{1,0:T(8,128)S(1)}, bf16[288,128]{1,0:T(8,128)(2,1)S(1)}) custom-call(f32[1,128]{1,0:T(1,128)} %bitcast.9, f32[1,128]{1,0:T(1,128)} %bitcast.10, bf16[288,128]{1,0:T(8,128)(2,1)S(1)} %get-tuple-element.29.through_ref), custom_call_target="tpu_custom_call", output_to_operand_aliasing={{2}: (2, {})} | custom-call | flops 99999997952 | bytes 1048576 | tf_op jit(solution)/shard_map/head_lanes/pallas_call | solution.py:367
  8.5 1.8 %collective-permute-start.3 = (bf16[288,128]{1,0:T(8,128)(2,1)S(1)}, bf16[288,128]{1,0:T(8,128)(2,1)S(1)}, u32[]{:S(2)}, u32[]{:S(2)}) collective-permute-start(bf16[288,128]{1,0:T(8,128)(2,1)S(1)} %get-tuple-element.30), channel_id=1, source_target_pairs={{0,4},{4,0},{8,12},{12,8},{16,20},{20,16},{24,28},{28,24},{1,5},{5... | collective-permute-start | bytes 221192 | tf_op jit(solution)/shard_map/ppermute | solution.py:353
  10.3 0.0 collective-permute-done.refs_1_
  10.3 0.3 collective-permute-start.4
  10.6 2.1 %collective-permute-done.1.refs_2_ = bf16[288,128]{1,0:T(8,128)(2,1)S(1)} collective-permute-done((bf16[288,128]{1,0:T(8,128)(2,1)S(1)}, bf16[288,128]{1,0:T(8,128)(2,1)S(1)}, u32[]{:S(2)}, u32[]{:S(2)}) %collective-permute-start.1) | collective-permute-done | bytes 73760 | tf_op jit(solution)/shard_map/ppermute | solution.py:353
  12.7 1.5 %collective-permute-start.5 = (bf16[288,128]{1,0:T(8,128)(2,1)S(1)}, bf16[288,128]{1,0:T(8,128)(2,1)S(1)}, u32[]{:S(2)}, u32[]{:S(2)}) collective-permute-start(bf16[288,128]{1,0:T(8,128)(2,1)S(1)} %collective-permute-done.1.refs_2_), channel_id=1, source_target_pairs={{0,4},{4,0},{8,12},{12,8},{16,20},{20,16},{24,28},{28,24},{1,5},{5... | collective-permute-start | bytes 221192 | tf_op jit(solution)/shard_map/ppermute | solution.py:353
  14.2 0.0 collective-permute-done.2.refs_3_
  14.2 1.1 %collective-permute-start.6 = (bf16[288,128]{1,0:T(8,128)(2,1)S(1)}, bf16[288,128]{1,0:T(8,128)(2,1)S(1)}, u32[]{:S(2)}, u32[]{:S(2)}) collective-permute-start(bf16[288,128]{1,0:T(8,128)(2,1)S(1)} %collective-permute-done.2.refs_3_), channel_id=1, source_target_pairs={{0,4},{4,0},{8,12},{12,8},{16,20},{20,16},{24,28},{28,24},{1,5},{5... | collective-permute-start | bytes 221192 | tf_op jit(solution)/shard_map/ppermute | solution.py:353
  15.2 0.0 collective-permute-done.3.refs_4_
  15.2 0.1 collective-permute-done.4.refs_5_
  15.3 1.7 %collective-permute-done.5.refs_6_ = bf16[288,128]{1,0:T(8,128)(2,1)S(1)} collective-permute-done((bf16[288,128]{1,0:T(8,128)(2,1)S(1)}, bf16[288,128]{1,0:T(8,128)(2,1)S(1)}, u32[]{:S(2)}, u32[]{:S(2)}) %collective-permute-start.5) | collective-permute-done | bytes 73760 | tf_op jit(solution)/shard_map/ppermute | solution.py:353
  17.0 1.5 %collective-permute-done.6.refs_7_ = bf16[288,128]{1,0:T(8,128)(2,1)S(1)} collective-permute-done((bf16[288,128]{1,0:T(8,128)(2,1)S(1)}, bf16[288,128]{1,0:T(8,128)(2,1)S(1)}, u32[]{:S(2)}, u32[]{:S(2)}) %collective-permute-start.6) | collective-permute-done | bytes 73760 | tf_op jit(solution)/shard_map/ppermute | solution.py:353
  18.5 4.7 %attention.2 = (bf16[4,144,128]{2,1,0:T(8,128)(2,1)S(1)}, bf16[4,144,128]{2,1,0:T(8,128)(2,1)S(1)}) custom-call(s32[2,32]{1,0:T(2,128)} %pages_ref.3, s32[2]{0:T(128)} %lengths_ref.3, bf16[288,128]{1,0:T(8,128)(2,1)S(1)} %get-tuple-element.28.refs_0_, bf16[288,128]{1,0:T(8,128)(2,1)S(1)} %collective-permute-done.refs_1_, ...), custom_call_target="tpu_custom_call" | custom-call | flops 20000000000 | bytes 1048576 | tf_op jit(solution)/shard_map/attention/pallas_call | solution.py:390
  23.2 0.0 slice-start
  23.2 0.0 slice-start.1
  23.3 0.0 slice-start.2
  23.3 0.0 slice-start.4
  23.3 0.0 slice-start.5
  23.3 0.0 copy-start.1
  23.3 1.1 %collective-permute-start.7 = (bf16[4,144,128]{2,1,0:T(8,128)(2,1)S(1)}, bf16[4,144,128]{2,1,0:T(8,128)(2,1)S(1)}, u32[]{:S(2)}, u32[]{:S(2)}) collective-permute-start(bf16[4,144,128]{2,1,0:T(8,128)(2,1)S(1)} %get-tuple-element.34), channel_id=1, source_target_pairs={{0,4},{4,0},{8,12},{12,8},{16,20},{20,16},{24,28},{28,24},{1,5},{5... | collective-permute-start | bytes 442376 | tf_op jit(solution)/shard_map/ppermute | solution.py:353
  24.5 4.9 %attention.3 = (bf16[4,144,128]{2,1,0:T(8,128)(2,1)S(1)}, bf16[4,144,128]{2,1,0:T(8,128)(2,1)S(1)}) custom-call(s32[2,32]{1,0:T(2,128)} %pages_ref.3, s32[2]{0:T(128)} %lengths_ref.3, bf16[288,128]{1,0:T(8,128)(2,1)S(1)} %get-tuple-element.28.refs_0_, bf16[288,128]{1,0:T(8,128)(2,1)S(1)} %collective-permute-done.refs_1_, ...), custom_call_target="tpu_custom_call" | custom-call | flops 20000000000 | bytes 1048576 | tf_op jit(solution)/shard_map/attention/pallas_call | solution.py:390
  29.3 1.0 %collective-permute-start.11 = (bf16[4,144,128]{2,1,0:T(8,128)(2,1)S(1)}, bf16[4,144,128]{2,1,0:T(8,128)(2,1)S(1)}, u32[]{:S(2)}, u32[]{:S(2)}) collective-permute-start(bf16[4,144,128]{2,1,0:T(8,128)(2,1)S(1)} %get-tuple-element.40), channel_id=1, source_target_pairs={{0,4},{4,0},{8,12},{12,8},{16,20},{20,16},{24,28},{28,24},{1,5},{5... | collective-permute-start | bytes 442376 | tf_op jit(solution)/shard_map/ppermute | solution.py:353
  30.3 0.1 merge.2
  30.5 0.7 %collective-permute-start.8 = (bf16[144,128]{1,0:T(8,128)(2,1)S(1)}, bf16[144,128]{1,0:T(8,128)(2,1)S(1)}, u32[]{:S(2)}, u32[]{:S(2)}) collective-permute-start(bf16[144,128]{1,0:T(8,128)(2,1)S(1)} %get-tuple-element.36), channel_id=1, source_target_pairs={{0,8},{4,12},{8,0},{12,4},{16,24},{20,28},{24,16},{28,20},{1,9},{5... | collective-permute-start | bytes 110600 | tf_op jit(solution)/shard_map/ppermute | solution.py:353
  31.2 3.2 %collective-permute-start.9 = (bf16[144,128]{1,0:T(8,128)(2,1)S(1)}, bf16[144,128]{1,0:T(8,128)(2,1)S(1)}, u32[]{:S(2)}, u32[]{:S(2)}) collective-permute-start(bf16[144,128]{1,0:T(8,128)(2,1)S(1)} %get-tuple-element.37), channel_id=1, source_target_pairs={{0,16},{4,20},{8,24},{12,28},{16,0},{20,4},{24,8},{28,12},{1,17},{... | collective-permute-start | bytes 110600 | tf_op jit(solution)/shard_map/ppermute | solution.py:353
  34.4 0.5 collective-permute-start.10
  34.9 0.1 merge.3
  35.1 0.7 %collective-permute-start.12 = (bf16[144,128]{1,0:T(8,128)(2,1)S(1)}, bf16[144,128]{1,0:T(8,128)(2,1)S(1)}, u32[]{:S(2)}, u32[]{:S(2)}) collective-permute-start(bf16[144,128]{1,0:T(8,128)(2,1)S(1)} %get-tuple-element.42), channel_id=1, source_target_pairs={{0,8},{4,12},{8,0},{12,4},{16,24},{20,28},{24,16},{28,20},{1,9},{5... | collective-permute-start | bytes 110600 | tf_op jit(solution)/shard_map/ppermute | solution.py:353
  35.8 3.2 %collective-permute-start.13 = (bf16[144,128]{1,0:T(8,128)(2,1)S(1)}, bf16[144,128]{1,0:T(8,128)(2,1)S(1)}, u32[]{:S(2)}, u32[]{:S(2)}) collective-permute-start(bf16[144,128]{1,0:T(8,128)(2,1)S(1)} %get-tuple-element.43), channel_id=1, source_target_pairs={{0,16},{4,20},{8,24},{12,28},{16,0},{20,4},{24,8},{28,12},{1,17},{... | collective-permute-start | bytes 110600 | tf_op jit(solution)/shard_map/ppermute | solution.py:353
  39.0 0.0 collective-permute-done.8.refs_1_
  39.0 0.5 collective-permute-start.14
  39.6 0.6 %collective-permute-done.10.refs_3_ = bf16[144,128]{1,0:T(8,128)(2,1)S(1)} collective-permute-done((bf16[144,128]{1,0:T(8,128)(2,1)S(1)}, bf16[144,128]{1,0:T(8,128)(2,1)S(1)}, u32[]{:S(2)}, u32[]{:S(2)}) %collective-permute-start.10) | collective-permute-done | bytes 36896 | tf_op jit(solution)/shard_map/ppermute | solution.py:353
  40.2 0.8 %collective-permute-done.13.refs_6_ = bf16[144,128]{1,0:T(8,128)(2,1)S(1)} collective-permute-done((bf16[144,128]{1,0:T(8,128)(2,1)S(1)}, bf16[144,128]{1,0:T(8,128)(2,1)S(1)}, u32[]{:S(2)}, u32[]{:S(2)}) %collective-permute-start.13) | collective-permute-done | bytes 36896 | tf_op jit(solution)/shard_map/ppermute | solution.py:353
  40.9 3.8 %collective-permute-done.14.refs_7_ = bf16[144,128]{1,0:T(8,128)(2,1)S(1)} collective-permute-done((bf16[144,128]{1,0:T(8,128)(2,1)S(1)}, bf16[144,128]{1,0:T(8,128)(2,1)S(1)}, u32[]{:S(2)}, u32[]{:S(2)}) %collective-permute-start.14) | collective-permute-done | bytes 36896 | tf_op jit(solution)/shard_map/ppermute | solution.py:353
  44.8 2.9 %up_and_far_output.1 = (bf16[4,4,896]{2,1,0:T(4,128)(2,1)S(1)}, f32[8,2048]{1,0:T(8,128)S(1)}) custom-call(bf16[144,128]{1,0:T(8,128)(2,1)S(1)} %get-tuple-element.35.refs_0_, bf16[144,128]{1,0:T(8,128)(2,1)S(1)} %collective-permute-done.8.refs_1_, bf16[144,128]{1,0:T(8,128)(2,1)S(1)} %collective-permute-done.9.refs_2_, ...), custom_call_target="tpu_custom_call" | custom-call | flops 20000000000 | bytes 1048576 | tf_op jit(solution)/shard_map/up_and_far_output/pallas_call | solution.py:417
  47.7 0.0 collective-permute-start.15
  47.7 2.1 %near_output.1.own_ref = f32[4,4,896]{2,1,0:T(4,128)S(1)} custom-call(f32[8,2048]{1,0:T(8,128)S(1)} %get-tuple-element.45.values, bf16[2048,7168]{1,0:T(8,128)(2,1)S(1)} %bitcast.5), custom_call_target="tpu_custom_call" | custom-call | flops 20000000000 | bytes 1048576 | tf_op jit(solution)/shard_map/near_output/pallas_call | solution.py:428
  49.9 1.7 %collective-permute-done.15.other_ref = bf16[4,4,896]{2,1,0:T(4,128)(2,1)S(1)} collective-permute-done((bf16[4,4,896]{2,1,0:T(4,128)(2,1)S(1)}, bf16[4,4,896]{2,1,0:T(4,128)(2,1)S(1)}, u32[]{:S(2)}, u32[]{:S(2)}) %collective-permute-start.15) | collective-permute-done | bytes 28704 | tf_op jit(solution)/shard_map/ppermute | solution.py:353
  51.6 0.9 %collective-permute-start.16 = (bf16[4,896]{1,0:T(4,128)(2,1)S(1)}, bf16[4,896]{1,0:T(4,128)(2,1)S(1)}, u32[]{:S(2)}, u32[]{:S(2)}) collective-permute-start(bf16[4,896]{1,0:T(4,128)(2,1)S(1)} %get-tuple-element.48), channel_id=1, source_target_pairs={{0,4},{4,0},{8,12},{12,8},{16,20},{20,16},{24,28},{28,24},{1,5},{5... | collective-permute-start | bytes 21512 | tf_op jit(solution)/shard_map/ppermute | solution.py:353
  52.5 0.0 collective-permute-start.17
  52.5 3.6 %collective-permute-start.18 = (bf16[4,896]{1,0:T(4,128)(2,1)S(1)}, bf16[4,896]{1,0:T(4,128)(2,1)S(1)}, u32[]{:S(2)}, u32[]{:S(2)}) collective-permute-start(bf16[4,896]{1,0:T(4,128)(2,1)S(1)} %get-tuple-element.50), channel_id=1, source_target_pairs={{0,20},{4,16},{8,28},{12,24},{16,4},{20,0},{24,12},{28,8},{1,21},{... | collective-permute-start | bytes 21512 | tf_op jit(solution)/shard_map/ppermute | solution.py:353
  56.1 1.0 %collective-permute-done.17.refs_1_ = bf16[4,896]{1,0:T(4,128)(2,1)S(1)} collective-permute-done((bf16[4,896]{1,0:T(4,128)(2,1)S(1)}, bf16[4,896]{1,0:T(4,128)(2,1)S(1)}, u32[]{:S(2)}, u32[]{:S(2)}) %collective-permute-start.17) | collective-permute-done | bytes 7200 | tf_op jit(solution)/shard_map/ppermute | solution.py:353
  57.0 0.9 %collective-permute-done.18.refs_2_ = bf16[4,896]{1,0:T(4,128)(2,1)S(1)} collective-permute-done((bf16[4,896]{1,0:T(4,128)(2,1)S(1)}, bf16[4,896]{1,0:T(4,128)(2,1)S(1)}, u32[]{:S(2)}, u32[]{:S(2)}) %collective-permute-start.18) | collective-permute-done | bytes 7200 | tf_op jit(solution)/shard_map/ppermute | solution.py:353
  58.0 0.6 %sum_output.1 = bf16[2,2,896]{2,1,0:T(2,128)(2,1)} custom-call(f32[4,896]{1,0:T(4,128)S(1)} %get-tuple-element.47.own_ref, bf16[4,896]{1,0:T(4,128)(2,1)S(1)} %collective-permute-done.16.refs_0_, bf16[4,896]{1,0:T(4,128)(2,1)S(1)} %collective-permute-done.17.refs_1_, bf16[4,896]{1,0:T(4,128)(2,1)S(1)} %collective-permute-done.18.refs_2_), custom_call_target="tpu_custom_call" | custom-call | tf_op jit(solution)/shard_map/sum_output/pallas_call | solution.py:443
  (19 shorter events, 0.1 us)
Async XLA Ops:
  1.8 8.5 %collective-permute-start = (bf16[288,128]{1,0:T(8,128)(2,1)S(1)}, bf16[288,128]{1,0:T(8,128)(2,1)S(1)}, u32[]{:S(2)}, u32[]{:S(2)}) collective-permute-start(bf16[288,128]{1,0:T(8,128)(2,1)S(1)} %get-tuple-element.28.refs_0_), channel_id=1, source_target_pairs={{0,8},{4,12},{8,0},{12,4},{16,24},{20,28},{24,16},{28,20},{1,9},{5... | collective-permute-start | bytes 221192 | tf_op jit(solution)/shard_map/ppermute | solution.py:353
  4.9 7.8 %collective-permute-start.1 = (bf16[288,128]{1,0:T(8,128)(2,1)S(1)}, bf16[288,128]{1,0:T(8,128)(2,1)S(1)}, u32[]{:S(2)}, u32[]{:S(2)}) collective-permute-start(bf16[288,128]{1,0:T(8,128)(2,1)S(1)} %get-tuple-element.28.refs_0_), channel_id=1, source_target_pairs={{0,16},{4,20},{8,24},{12,28},{16,0},{20,4},{24,8},{28,12},{1,17},{... | collective-permute-start | bytes 221192 | tf_op jit(solution)/shard_map/ppermute | solution.py:353
  7.5 6.7 %collective-permute-start.2 = (bf16[288,128]{1,0:T(8,128)(2,1)S(1)}, bf16[288,128]{1,0:T(8,128)(2,1)S(1)}, u32[]{:S(2)}, u32[]{:S(2)}) collective-permute-start(bf16[288,128]{1,0:T(8,128)(2,1)S(1)} %get-tuple-element.28.refs_0_), channel_id=1, source_target_pairs={{0,24},{4,28},{8,16},{12,20},{16,8},{20,12},{24,0},{28,4},{1,25},{... | collective-permute-start | bytes 221192 | tf_op jit(solution)/shard_map/ppermute | solution.py:353
  7.5 11.0 %copy-start = (bf16[2,4096,576]{1,2,0:T(8,128)(2,1)S(1)}, bf16[2,4096,576]{1,2,0:T(8,128)(2,1)}, u32[]{:S(2)}) copy-start(bf16[2,4096,576]{1,2,0:T(8,128)(2,1)} %param.11) | copy-start | bytes 28311556
  8.5 6.7 %collective-permute-start.3 = (bf16[288,128]{1,0:T(8,128)(2,1)S(1)}, bf16[288,128]{1,0:T(8,128)(2,1)S(1)}, u32[]{:S(2)}, u32[]{:S(2)}) collective-permute-start(bf16[288,128]{1,0:T(8,128)(2,1)S(1)} %get-tuple-element.30), channel_id=1, source_target_pairs={{0,4},{4,0},{8,12},{12,8},{16,20},{20,16},{24,28},{28,24},{1,5},{5... | collective-permute-start | bytes 221192 | tf_op jit(solution)/shard_map/ppermute | solution.py:353
  10.3 5.0 %collective-permute-start.4 = (bf16[288,128]{1,0:T(8,128)(2,1)S(1)}, bf16[288,128]{1,0:T(8,128)(2,1)S(1)}, u32[]{:S(2)}, u32[]{:S(2)}) collective-permute-start(bf16[288,128]{1,0:T(8,128)(2,1)S(1)} %collective-permute-done.refs_1_), channel_id=1, source_target_pairs={{0,4},{4,0},{8,12},{12,8},{16,20},{20,16},{24,28},{28,24},{1,5},{5... | collective-permute-start | bytes 221192 | tf_op jit(solution)/shard_map/ppermute | solution.py:353
  12.7 4.4 %collective-permute-start.5 = (bf16[288,128]{1,0:T(8,128)(2,1)S(1)}, bf16[288,128]{1,0:T(8,128)(2,1)S(1)}, u32[]{:S(2)}, u32[]{:S(2)}) collective-permute-start(bf16[288,128]{1,0:T(8,128)(2,1)S(1)} %collective-permute-done.1.refs_2_), channel_id=1, source_target_pairs={{0,4},{4,0},{8,12},{12,8},{16,20},{20,16},{24,28},{28,24},{1,5},{5... | collective-permute-start | bytes 221192 | tf_op jit(solution)/shard_map/ppermute | solution.py:353
  14.2 4.4 %collective-permute-start.6 = (bf16[288,128]{1,0:T(8,128)(2,1)S(1)}, bf16[288,128]{1,0:T(8,128)(2,1)S(1)}, u32[]{:S(2)}, u32[]{:S(2)}) collective-permute-start(bf16[288,128]{1,0:T(8,128)(2,1)S(1)} %collective-permute-done.2.refs_3_), channel_id=1, source_target_pairs={{0,4},{4,0},{8,12},{12,8},{16,20},{20,16},{24,28},{28,24},{1,5},{5... | collective-permute-start | bytes 221192 | tf_op jit(solution)/shard_map/ppermute | solution.py:353
  23.2 21.5 %slice-start = ((s8[29360128]{0:T(1024)(128)(4,1)}), s8[4194304]{0:T(1024)(128)(4,1)S(1)}, s32[]{:S(2)}) async-start(s8[29360128]{0:T(1024)(128)(4,1)} %bitcast.4), calls=%async_computation | async-start | bytes 8388608
  23.2 21.5 %slice-start.1 = ((s8[29360128]{0:T(1024)(128)(4,1)}), s8[4194304]{0:T(1024)(128)(4,1)S(1)}, s32[]{:S(2)}) async-start(s8[29360128]{0:T(1024)(128)(4,1)} %bitcast.4), calls=%async_computation.1 | async-start | bytes 8388608
  23.3 21.5 %slice-start.2 = ((s8[29360128]{0:T(1024)(128)(4,1)}), s8[4194304]{0:T(1024)(128)(4,1)S(1)}, s32[]{:S(2)}) async-start(s8[29360128]{0:T(1024)(128)(4,1)} %bitcast.4), calls=%async_computation.2 | async-start | bytes 8388608
  23.3 21.5 %slice-start.3 = ((s8[29360128]{0:T(1024)(128)(4,1)}), s8[4194304]{0:T(1024)(128)(4,1)S(1)}, s32[]{:S(2)}) async-start(s8[29360128]{0:T(1024)(128)(4,1)} %bitcast.4), calls=%async_computation.3 | async-start | bytes 8388608
  23.3 21.5 %slice-start.4 = ((s8[29360128]{0:T(1024)(128)(4,1)}), s8[4194304]{0:T(1024)(128)(4,1)S(1)}, s32[]{:S(2)}) async-start(s8[29360128]{0:T(1024)(128)(4,1)} %bitcast.4), calls=%async_computation.4 | async-start | bytes 8388608
  23.3 21.5 %slice-start.5 = ((s8[29360128]{0:T(1024)(128)(4,1)}), s8[4194304]{0:T(1024)(128)(4,1)S(1)}, s32[]{:S(2)}) async-start(s8[29360128]{0:T(1024)(128)(4,1)} %bitcast.4), calls=%async_computation.5 | async-start | bytes 8388608
  23.3 21.5 %slice-start.6 = ((s8[29360128]{0:T(1024)(128)(4,1)}), s8[4194304]{0:T(1024)(128)(4,1)S(1)}, s32[]{:S(2)}) async-start(s8[29360128]{0:T(1024)(128)(4,1)} %bitcast.4), calls=%async_computation.6 | async-start | bytes 8388608
  23.3 21.5 %copy-start.1 = (bf16[16,512,128]{2,1,0:T(8,128)(2,1)S(1)}, bf16[16,512,128]{2,1,0:T(8,128)(2,1)}, u32[]{:S(2)}) copy-start(bf16[16,512,128]{2,1,0:T(8,128)(2,1)} %refs_8_.1) | copy-start | bytes 6291460
  23.3 7.0 %collective-permute-start.7 = (bf16[4,144,128]{2,1,0:T(8,128)(2,1)S(1)}, bf16[4,144,128]{2,1,0:T(8,128)(2,1)S(1)}, u32[]{:S(2)}, u32[]{:S(2)}) collective-permute-start(bf16[4,144,128]{2,1,0:T(8,128)(2,1)S(1)} %get-tuple-element.34), channel_id=1, source_target_pairs={{0,4},{4,0},{8,12},{12,8},{16,20},{20,16},{24,28},{28,24},{1,5},{5... | collective-permute-start | bytes 442376 | tf_op jit(solution)/shard_map/ppermute | solution.py:353
  29.3 5.6 %collective-permute-start.11 = (bf16[4,144,128]{2,1,0:T(8,128)(2,1)S(1)}, bf16[4,144,128]{2,1,0:T(8,128)(2,1)S(1)}, u32[]{:S(2)}, u32[]{:S(2)}) collective-permute-start(bf16[4,144,128]{2,1,0:T(8,128)(2,1)S(1)} %get-tuple-element.40), channel_id=1, source_target_pairs={{0,4},{4,0},{8,12},{12,8},{16,20},{20,16},{24,28},{28,24},{1,5},{5... | collective-permute-start | bytes 442376 | tf_op jit(solution)/shard_map/ppermute | solution.py:353
  30.5 8.5 %collective-permute-start.8 = (bf16[144,128]{1,0:T(8,128)(2,1)S(1)}, bf16[144,128]{1,0:T(8,128)(2,1)S(1)}, u32[]{:S(2)}, u32[]{:S(2)}) collective-permute-start(bf16[144,128]{1,0:T(8,128)(2,1)S(1)} %get-tuple-element.36), channel_id=1, source_target_pairs={{0,8},{4,12},{8,0},{12,4},{16,24},{20,28},{24,16},{28,20},{1,9},{5... | collective-permute-start | bytes 110600 | tf_op jit(solution)/shard_map/ppermute | solution.py:353
  31.2 8.3 %collective-permute-start.9 = (bf16[144,128]{1,0:T(8,128)(2,1)S(1)}, bf16[144,128]{1,0:T(8,128)(2,1)S(1)}, u32[]{:S(2)}, u32[]{:S(2)}) collective-permute-start(bf16[144,128]{1,0:T(8,128)(2,1)S(1)} %get-tuple-element.37), channel_id=1, source_target_pairs={{0,16},{4,20},{8,24},{12,28},{16,0},{20,4},{24,8},{28,12},{1,17},{... | collective-permute-start | bytes 110600 | tf_op jit(solution)/shard_map/ppermute | solution.py:353
  34.4 5.8 %collective-permute-start.10 = (bf16[144,128]{1,0:T(8,128)(2,1)S(1)}, bf16[144,128]{1,0:T(8,128)(2,1)S(1)}, u32[]{:S(2)}, u32[]{:S(2)}) collective-permute-start(bf16[144,128]{1,0:T(8,128)(2,1)S(1)} %get-tuple-element.38), channel_id=1, source_target_pairs={{0,24},{4,28},{8,16},{12,20},{16,8},{20,12},{24,0},{28,4},{1,25},{... | collective-permute-start | bytes 110600 | tf_op jit(solution)/shard_map/ppermute | solution.py:353
  35.1 5.1 %collective-permute-start.12 = (bf16[144,128]{1,0:T(8,128)(2,1)S(1)}, bf16[144,128]{1,0:T(8,128)(2,1)S(1)}, u32[]{:S(2)}, u32[]{:S(2)}) collective-permute-start(bf16[144,128]{1,0:T(8,128)(2,1)S(1)} %get-tuple-element.42), channel_id=1, source_target_pairs={{0,8},{4,12},{8,0},{12,4},{16,24},{20,28},{24,16},{28,20},{1,9},{5... | collective-permute-start | bytes 110600 | tf_op jit(solution)/shard_map/ppermute | solution.py:353
  35.8 5.1 %collective-permute-start.13 = (bf16[144,128]{1,0:T(8,128)(2,1)S(1)}, bf16[144,128]{1,0:T(8,128)(2,1)S(1)}, u32[]{:S(2)}, u32[]{:S(2)}) collective-permute-start(bf16[144,128]{1,0:T(8,128)(2,1)S(1)} %get-tuple-element.43), channel_id=1, source_target_pairs={{0,16},{4,20},{8,24},{12,28},{16,0},{20,4},{24,8},{28,12},{1,17},{... | collective-permute-start | bytes 110600 | tf_op jit(solution)/shard_map/ppermute | solution.py:353
  39.0 5.8 %collective-permute-start.14 = (bf16[144,128]{1,0:T(8,128)(2,1)S(1)}, bf16[144,128]{1,0:T(8,128)(2,1)S(1)}, u32[]{:S(2)}, u32[]{:S(2)}) collective-permute-start(bf16[144,128]{1,0:T(8,128)(2,1)S(1)} %get-tuple-element.44), channel_id=1, source_target_pairs={{0,24},{4,28},{8,16},{12,20},{16,8},{20,12},{24,0},{28,4},{1,25},{... | collective-permute-start | bytes 110600 | tf_op jit(solution)/shard_map/ppermute | solution.py:353
  47.7 3.9 %collective-permute-start.15 = (bf16[4,4,896]{2,1,0:T(4,128)(2,1)S(1)}, bf16[4,4,896]{2,1,0:T(4,128)(2,1)S(1)}, u32[]{:S(2)}, u32[]{:S(2)}) collective-permute-start(bf16[4,4,896]{2,1,0:T(4,128)(2,1)S(1)} %get-tuple-element.46), channel_id=1, source_target_pairs={{0,8},{4,12},{8,0},{12,4},{16,24},{20,28},{24,16},{28,20},{1,9},{5... | collective-permute-start | bytes 86024 | tf_op jit(solution)/shard_map/ppermute | solution.py:353
  51.6 4.5 %collective-permute-start.16 = (bf16[4,896]{1,0:T(4,128)(2,1)S(1)}, bf16[4,896]{1,0:T(4,128)(2,1)S(1)}, u32[]{:S(2)}, u32[]{:S(2)}) collective-permute-start(bf16[4,896]{1,0:T(4,128)(2,1)S(1)} %get-tuple-element.48), channel_id=1, source_target_pairs={{0,4},{4,0},{8,12},{12,8},{16,20},{20,16},{24,28},{28,24},{1,5},{5... | collective-permute-start | bytes 21512 | tf_op jit(solution)/shard_map/ppermute | solution.py:353
  52.5 4.5 %collective-permute-start.17 = (bf16[4,896]{1,0:T(4,128)(2,1)S(1)}, bf16[4,896]{1,0:T(4,128)(2,1)S(1)}, u32[]{:S(2)}, u32[]{:S(2)}) collective-permute-start(bf16[4,896]{1,0:T(4,128)(2,1)S(1)} %get-tuple-element.49), channel_id=1, source_target_pairs={{0,16},{4,20},{8,24},{12,28},{16,0},{20,4},{24,8},{28,12},{1,17},{... | collective-permute-start | bytes 21512 | tf_op jit(solution)/shard_map/ppermute | solution.py:353
  52.5 5.4 %collective-permute-start.18 = (bf16[4,896]{1,0:T(4,128)(2,1)S(1)}, bf16[4,896]{1,0:T(4,128)(2,1)S(1)}, u32[]{:S(2)}, u32[]{:S(2)}) collective-permute-start(bf16[4,896]{1,0:T(4,128)(2,1)S(1)} %get-tuple-element.50), channel_id=1, source_target_pairs={{0,20},{4,16},{8,28},{12,24},{16,4},{20,0},{24,12},{28,8},{1,21},{... | collective-permute-start | bytes 21512 | tf_op jit(solution)/shard_map/ppermute | solution.py:353

commit v3 on v2

--- a/solution.py
+++ b/solution.py
@@ -88,45 +88,51 @@
             picked = jnp.zeros((heads, LANES), jnp.float32)
             for device in range(ctx):
                 picked = jnp.where(owner == device, column[device], picked)
-            rows += [picked, picked]
-        rows = jnp.concatenate(rows, axis=0)
-        for i in range(rows.shape[0] // LANES):
-            at = slice(i * LANES, (i + 1) * LANES)
-            target[:, at] = rows[at].T[: target.shape[0]]
+            rows.append(picked)
+        target[...] = jnp.concatenate(rows, axis=0).T[: target.shape[0]]
+
+
+def turn_kernel(cache_ref, out_ref, *, b):
+    width = 2 * PAGE
+    for i in range(out_ref.shape[0] // width):
+        at = slice(i * width, (i + 1) * width)
+        out_ref[at, :] = cache_ref[b, :, at].T
 
 
 def attention_kernel(pages_ref, lengths_ref, *refs, ctx, b):
     query_refs, refs = refs[:ctx], refs[ctx:]
-    cache_ref, inv_rate, scale, near_ref, far_ref, query, acc, *buffers = refs
+    cache_ref, turned_ref, inv_rate, scale, near_ref, far_ref, query, held, acc, *buffers = refs
     scores_of, weights_of, factor_of = buffers[:2], buffers[2:4], buffers[4:]
     chunk, rows = scores_of[0].shape
     half = rows // ctx
     heads = half // 2
     line = ctx // 2
     steps = cache_ref.shape[2] // chunk
-    pair_width = 2 * PAGE
-    pairs = chunk // pair_width
+    group = 4
+    group_width = group * PAGE
+    groups = chunk // group_width
     request_rows = LAT_TILES * half
     start = b * request_rows
 
+    side = rows // 2
     for k, block in enumerate(query_refs):
-        own = slice(k * half, (k + 1) * half)
-        for j in range(LAT_TILES):
-            query[own, j * LANES : (j + 1) * LANES] = block[
-                start + j * half : start + (j + 1) * half, :
-            ]
-        query[own, LAT:] = block[2 * request_rows :, b * ROPE : (b + 1) * ROPE]
-
+        for q in range(2):
+            own = slice(q * side + k * heads, q * side + (k + 1) * heads)
+            for j in range(LAT_TILES):
+                at = start + j * half + q * heads
+                query[own, j * LANES : (j + 1) * LANES] = block[at : at + heads, :]
+            at = 2 * request_rows + q * heads
+            query[own, LAT:] = block[at : at + heads, b * ROPE : (b + 1) * ROPE]
+
+    held[...] = query[...].T
     first_pos = lengths_ref[b] - 2
-    token = lax.rem(lax.broadcasted_iota(jnp.int32, (1, rows), 1) // heads, 2)
     own_rate, own_scale = inv_rate[0:1, :], scale[0:1, :]
-    slot = lax.broadcasted_iota(jnp.int32, (PAGE, rows), 0)
+    back = lax.broadcasted_iota(jnp.int32, (PAGE + 8, side), 0).astype(jnp.float32)
 
     def raw_scores(at):
-        return lax.dot_general(
-            cache_ref[b, :, at * pair_width : (at + 1) * pair_width],
-            query[...],
-            (((0,), (1,)), ((), ())),
+        return jnp.dot(
+            turned_ref[at * group_width : (at + 1) * group_width, :],
+            held[...],
             preferred_element_type=jnp.float32,
         )
 
@@ -146,21 +152,20 @@
     for step in range(steps):
         scores, weights = scores_of[step % 2], weights_of[step % 2]
         tops = jnp.full((8, rows), LOWEST, jnp.float32)
-        for pair in range(pairs):
+        for piece in range(groups):
             raw = ahead
-            at = step * pairs + pair
-            if at + 1 < steps * pairs:
+            at = step * groups + piece
+            if at + 1 < steps * groups:
                 ahead = raw_scores(at + 1)
-            for side in range(2):
-                page = pair * 2 + side
+            for side_of in range(group):
+                page = piece * group + side_of
                 base = first_pos - pages_ref[b, step * (chunk // PAGE) + page] * PAGE
-                distance = (base + token) - slot
-                spread = jnp.where(distance >= 0, distance.astype(jnp.float32), jnp.inf)
-                logs = jnp.log2(spread + own_rate)
-                value = (
-                    raw[side * PAGE : (side + 1) * PAGE] * (SOFTMAX_SCALE * LOG2E)
-                    - own_scale * logs
-                )
+                reach = (base + 1).astype(jnp.float32) - back
+                spread = jnp.where(reach >= 0.0, reach, jnp.inf)
+                bias = own_scale * jnp.log2(spread + own_rate)
+                value = raw[side_of * PAGE : (side_of + 1) * PAGE] * (
+                    SOFTMAX_SCALE * LOG2E
+                ) - jnp.concatenate([bias[1 : PAGE + 1], bias[:PAGE]], axis=1)
                 tops = jnp.maximum(tops, jnp.max(value.reshape(PAGE // 8, 8, rows), axis=0))
                 scores[page * PAGE : (page + 1) * PAGE, :] = value
         before = top
@@ -184,20 +189,16 @@
     logs = jnp.where(seen, top + jnp.log2(safe), LOWEST)
     logs = jnp.broadcast_to(logs, (LANES, rows))
     turned = []
-    for i in range(rows // LANES):
-        at = slice(i * LANES, (i + 1) * LANES)
-        turned.append(logs[:, at].T)
-        first, count = i * LANES // half, LANES // half
+    for q in range(2):
+        at = slice(q * side, (q + 1) * side)
+        turned.append(logs[:, at].T.reshape(ctx, heads, LANES))
         for j in range(LAT_TILES):
             part = (acc[j * LANES : (j + 1) * LANES, at] * share[:, at]).T
-            part = part.astype(jnp.bfloat16).reshape(count, half, LANES)
-            for k in range(count):
-                to_ref, block = (near_ref, first + k) if first + k < line else (
-                    far_ref,
-                    first + k - line,
-                )
-                to_ref[block, j * half : (j + 1) * half, :] = part[k]
-    log_total = jnp.concatenate(turned, axis=0).reshape(ctx, half, LANES)
+            part = part.astype(jnp.bfloat16).reshape(ctx, heads, LANES)
+            first = j * half + q * heads
+            near_ref[:, first : first + heads, :] = part[:line]
+            far_ref[:, first : first + heads, :] = part[line:]
+    log_total = jnp.concatenate(turned, axis=1)
     across = jnp.sum(jnp.where(diagonal(half), log_total, 0.0), axis=1, keepdims=True)
     packed = three_parts(across).astype(jnp.bfloat16)
     near_ref[:, request_rows:, :] = packed[:line]
@@ -363,7 +364,7 @@
         compiler_params=pltpu.CompilerParams(vmem_limit_bytes=8 * 2**20),
         name="latent_query",
     )(in_hbm(queries.reshape(rows, query_width)), in_hbm(key_absorb))
-    by_row = (8, ctx * half)
+    by_row = (8, ctx * heads)
     inv_rate, scale, again = pl.pallas_call(
         functools.partial(lanes_kernel, ctx=ctx),
         in_specs=[pl.BlockSpec(memory_space=pltpu.VMEM)] * 2
@@ -381,6 +382,15 @@
     gathered = column + [swap(value, 1) for value in [again] + column[1:]]
 
     cache = in_vmem(jnp.swapaxes(latent_cache, 1, 2))
+    turned = [
+        pl.pallas_call(
+            functools.partial(turn_kernel, b=b),
+            out_shape=jax.ShapeDtypeStruct((keys_dev, LAT + ROPE), jnp.bfloat16),
+            compiler_params=pltpu.CompilerParams(vmem_limit_bytes=4 * 2**20),
+            name="turn_cache",
+        )(cache)
+        for b in range(requests)
+    ]
     all_rows = ctx * half
     message = (request_rows + STAT_ROWS, LANES)
     in_smem = pl.BlockSpec(memory_space=pltpu.SMEM)
@@ -389,10 +399,11 @@
     for b in range(requests):
         near, far = pl.pallas_call(
             functools.partial(attention_kernel, ctx=ctx, b=b),
-            in_specs=[in_smem, in_smem] + [whole] * (ctx + 3),
+            in_specs=[in_smem, in_smem] + [whole] * (ctx + 4),
             out_shape=[jax.ShapeDtypeStruct((line,) + message, jnp.bfloat16)] * 2,
             scratch_shapes=[
                 pltpu.VMEM((all_rows, LAT + ROPE), jnp.bfloat16),
+                pltpu.VMEM((LAT + ROPE, all_rows), jnp.bfloat16),
                 pltpu.VMEM((LAT, all_rows), jnp.float32),
             ]
             + [pltpu.VMEM((chunk, all_rows), jnp.float32)] * 2
@@ -401,7 +412,7 @@
             compiler_params=pltpu.CompilerParams(vmem_limit_bytes=8 * 2**20),
             cost_estimate=hint,
             name="attention",
-        )(in_hbm(page_order), in_hbm(lengths), *gathered, cache, inv_rate, scale)
+        )(in_hbm(page_order), in_hbm(lengths), *gathered, cache, in_vmem(turned[b]), inv_rate, scale)
         merged = pl.pallas_call(
             merge_kernel,
             out_shape=[jax.ShapeDtypeStruct(message, jnp.bfloat16) for _ in range(line)],
@@ -525,7 +536,7 @@
     def device_program(*args):
         heads = args[0].shape[2]
         width = args[-1].shape[1] // ctx
-        tiled = ctx == 8 and heads % 16 == 0 and width % LANES == 0
+        tiled = ctx == 8 and ctx * heads == LANES and width % LANES == 0
         return (per_device if tiled else plain_device)(*args, ctx=ctx)
 
     return jax.shard_map(

time: 58.7 us -> 58.2 us (level)
  waiting for transfers between devices: 14.2 us -> 11 us
  Pallas kernels: 18.3 us -> 20.6 us
    ppermute x19, waiting for transfers between devices: 14.2 us -> 11 us  [per_device(): lax.ppermute(value, 'ctx', [(i, i ^ bits) for i in range(ctx)])]
    pallas_call x0 -> x2, Pallas kernels: none -> 2.84 us  [per_device(): pl.pallas_call(functools.partial(turn_kernel, b=b), out_shape=jax.ShapeDt...]
  transfers between devices with their start and end apart: 19 -> 19, of which waited for: 10 -> 8; matrix products, arithmetic and copies ran while one was open for 0% -> 0% of each run, Pallas kernels for 14% -> 19%
where the time goes in v3:
time: 58.2 us; the launch traced here: 58.1 us
  starting transfers between devices  26.2 us (45%)
  Pallas kernels  20.6 us (35%)
  waiting for transfers between devices  11 us (19%)
    ppermute x19, starting transfers between devices, per_device(): lax.ppermute(value, 'ctx', [(i, i ^ bits) for i in range(ctx)])  26.2 us
    ppermute x19, waiting for transfers between devices, per_device(): lax.ppermute(value, 'ctx', [(i, i ^ bits) for i in range(ctx)])  11 us
    pallas_call x2, Pallas kernels, per_device(): pl.pallas_call(functools.partial(attention_kernel, ctx=ctx, b=b), in_spec...  8.97 us
    pallas_call x1, Pallas kernels, per_device(): pl.pallas_call(output_kernel, out_shape=[jax.ShapeDtypeStruct((line, toke...  2.89 us
    pallas_call x2, Pallas kernels, per_device(): pl.pallas_call(functools.partial(turn_kernel, b=b), out_shape=jax.ShapeDt...  2.84 us
    pallas_call x1, Pallas kernels, per_device(): pl.pallas_call(near_kernel, out_shape=jax.ShapeDtypeStruct((line, tokens,...  2.15 us
    pallas_call x1, Pallas kernels, per_device(): pl.pallas_call(query_kernel, in_specs=[pl.BlockSpec(memory_space=pl.ANY)]...  1.8 us
  transfers between devices with their start and end apart: 19, of which 8 were waited for; matrix products, arithmetic and copies ran while one was open for 0% of the time, Pallas kernels for 19%

profile of v3, /device:TPU:0, one launch (start us, length us, event | category | flops | bytes accessed | tf_op | source)
XLA Modules:
  0.0 58.1 jit_solution(16805711539346591928)
XLA Ops:
  0.0 1.8 %latent_query.1 = (bf16[288,128]{1,0:T(8,128)(2,1)S(1)}, bf16[288,128]{1,0:T(8,128)(2,1)S(1)}) custom-call(bf16[64,192]{1,0:T(8,128)(2,1)} %bitcast.12, bf16[16,128,512]{2,1,0:T(8,128)(2,1)} %absorb_hbm.1), custom_call_target="tpu_custom_call" | custom-call | tf_op jit(solution)/shard_map/latent_query/pallas_call | solution.py:355
  1.8 5.1 %collective-permute-start.2 = (bf16[288,128]{1,0:T(8,128)(2,1)S(1)}, bf16[288,128]{1,0:T(8,128)(2,1)S(1)}, u32[]{:S(2)}, u32[]{:S(2)}) collective-permute-start(bf16[288,128]{1,0:T(8,128)(2,1)S(1)} %get-tuple-element.28.refs_0_), channel_id=1, source_target_pairs={{0,24},{4,28},{8,16},{12,20},{16,8},{20,12},{24,0},{28,4},{1,25},{... | collective-permute-start | bytes 221192 | tf_op jit(solution)/shard_map/ppermute | solution.py:354
  6.9 0.0 collective-permute-start.1
  6.9 0.6 %collective-permute-start = (bf16[288,128]{1,0:T(8,128)(2,1)S(1)}, bf16[288,128]{1,0:T(8,128)(2,1)S(1)}, u32[]{:S(2)}, u32[]{:S(2)}) collective-permute-start(bf16[288,128]{1,0:T(8,128)(2,1)S(1)} %get-tuple-element.28.refs_0_), channel_id=1, source_target_pairs={{0,8},{4,12},{8,0},{12,4},{16,24},{20,28},{24,16},{28,20},{1,9},{5... | collective-permute-start | bytes 221192 | tf_op jit(solution)/shard_map/ppermute | solution.py:354
  7.6 1.0 %head_lanes.1 = (f32[8,128]{1,0:T(8,128)S(1)}, f32[8,128]{1,0:T(8,128)S(1)}, bf16[288,128]{1,0:T(8,128)(2,1)S(1)}) custom-call(f32[1,128]{1,0:T(1,128)} %bitcast.13, f32[1,128]{1,0:T(1,128)} %bitcast.14, bf16[288,128]{1,0:T(8,128)(2,1)S(1)} %get-tuple-element.29.through_ref), custom_call_target="tpu_custom_call", output_to_operand_aliasing={{2}: (2, {})} | custom-call | flops 99999997952 | bytes 1048576 | tf_op jit(solution)/shard_map/head_lanes/pallas_call | solution.py:368
  8.6 1.7 %collective-permute-start.3 = (bf16[288,128]{1,0:T(8,128)(2,1)S(1)}, bf16[288,128]{1,0:T(8,128)(2,1)S(1)}, u32[]{:S(2)}, u32[]{:S(2)}) collective-permute-start(bf16[288,128]{1,0:T(8,128)(2,1)S(1)} %get-tuple-element.30), channel_id=1, source_target_pairs={{0,4},{4,0},{8,12},{12,8},{16,20},{20,16},{24,28},{28,24},{1,5},{5... | collective-permute-start | bytes 221192 | tf_op jit(solution)/shard_map/ppermute | solution.py:354
  10.3 1.3 %collective-permute-start.6 = (bf16[288,128]{1,0:T(8,128)(2,1)S(1)}, bf16[288,128]{1,0:T(8,128)(2,1)S(1)}, u32[]{:S(2)}, u32[]{:S(2)}) collective-permute-start(bf16[288,128]{1,0:T(8,128)(2,1)S(1)} %collective-permute-done.2.refs_3_), channel_id=1, source_target_pairs={{0,4},{4,0},{8,12},{12,8},{16,20},{20,16},{24,28},{28,24},{1,5},{5... | collective-permute-start | bytes 221192 | tf_op jit(solution)/shard_map/ppermute | solution.py:354
  11.5 1.6 %collective-permute-done.1.refs_2_ = bf16[288,128]{1,0:T(8,128)(2,1)S(1)} collective-permute-done((bf16[288,128]{1,0:T(8,128)(2,1)S(1)}, bf16[288,128]{1,0:T(8,128)(2,1)S(1)}, u32[]{:S(2)}, u32[]{:S(2)}) %collective-permute-start.1) | collective-permute-done | bytes 73760 | tf_op jit(solution)/shard_map/ppermute | solution.py:354
  13.1 1.5 %collective-permute-start.5 = (bf16[288,128]{1,0:T(8,128)(2,1)S(1)}, bf16[288,128]{1,0:T(8,128)(2,1)S(1)}, u32[]{:S(2)}, u32[]{:S(2)}) collective-permute-start(bf16[288,128]{1,0:T(8,128)(2,1)S(1)} %collective-permute-done.1.refs_2_), channel_id=1, source_target_pairs={{0,4},{4,0},{8,12},{12,8},{16,20},{20,16},{24,28},{28,24},{1,5},{5... | collective-permute-start | bytes 221192 | tf_op jit(solution)/shard_map/ppermute | solution.py:354
  14.6 0.0 collective-permute-done.refs_1_
  14.6 0.5 collective-permute-start.4
  15.2 1.4 %turn_cache.3.refs_9_ = bf16[4096,576]{1,0:T(8,128)(2,1)S(1)} custom-call(bf16[2,576,4096]{2,1,0:T(8,128)(2,1)S(1)} %bitcast.6), custom_call_target="tpu_custom_call" | custom-call | tf_op jit(solution)/shard_map/turn_cache/pallas_call | solution.py:386
  16.6 1.4 %turn_cache.2.refs_9_ = bf16[4096,576]{1,0:T(8,128)(2,1)S(1)} custom-call(bf16[2,576,4096]{2,1,0:T(8,128)(2,1)S(1)} %bitcast.7), custom_call_target="tpu_custom_call" | custom-call | tf_op jit(solution)/shard_map/turn_cache/pallas_call | solution.py:386
  18.0 0.0 collective-permute-done.3.refs_4_
  18.1 0.1 collective-permute-done.5.refs_6_
  18.2 0.8 %collective-permute-done.4.refs_5_ = bf16[288,128]{1,0:T(8,128)(2,1)S(1)} collective-permute-done((bf16[288,128]{1,0:T(8,128)(2,1)S(1)}, bf16[288,128]{1,0:T(8,128)(2,1)S(1)}, u32[]{:S(2)}, u32[]{:S(2)}) %collective-permute-start.4) | collective-permute-done | bytes 73760 | tf_op jit(solution)/shard_map/ppermute | solution.py:354
  19.0 4.5 %attention.3 = (bf16[4,144,128]{2,1,0:T(8,128)(2,1)S(1)}, bf16[4,144,128]{2,1,0:T(8,128)(2,1)S(1)}) custom-call(s32[2,32]{1,0:T(2,128)} %pages_ref.3, s32[2]{0:T(128)} %lengths_ref.3, bf16[288,128]{1,0:T(8,128)(2,1)S(1)} %get-tuple-element.28.refs_0_, bf16[288,128]{1,0:T(8,128)(2,1)S(1)} %collective-permute-done.refs_1_, ...), custom_call_target="tpu_custom_call" | custom-call | flops 20000000000 | bytes 1048576 | tf_op jit(solution)/shard_map/attention/pallas_call | solution.py:400
  23.4 0.0 slice-start.3
  23.5 0.0 slice-start.4
  23.5 0.0 slice-start.7
  23.5 0.0 slice-start.8
  23.5 0.0 copy-start
  23.5 1.1 %collective-permute-start.11 = (bf16[4,144,128]{2,1,0:T(8,128)(2,1)S(1)}, bf16[4,144,128]{2,1,0:T(8,128)(2,1)S(1)}, u32[]{:S(2)}, u32[]{:S(2)}) collective-permute-start(bf16[4,144,128]{2,1,0:T(8,128)(2,1)S(1)} %get-tuple-element.40), channel_id=1, source_target_pairs={{0,4},{4,0},{8,12},{12,8},{16,20},{20,16},{24,28},{28,24},{1,5},{5... | collective-permute-start | bytes 442376 | tf_op jit(solution)/shard_map/ppermute | solution.py:354
  24.7 4.5 %attention.2 = (bf16[4,144,128]{2,1,0:T(8,128)(2,1)S(1)}, bf16[4,144,128]{2,1,0:T(8,128)(2,1)S(1)}) custom-call(s32[2,32]{1,0:T(2,128)} %pages_ref.3, s32[2]{0:T(128)} %lengths_ref.3, bf16[288,128]{1,0:T(8,128)(2,1)S(1)} %get-tuple-element.28.refs_0_, bf16[288,128]{1,0:T(8,128)(2,1)S(1)} %collective-permute-done.refs_1_, ...), custom_call_target="tpu_custom_call" | custom-call | flops 20000000000 | bytes 1048576 | tf_op jit(solution)/shard_map/attention/pallas_call | solution.py:400
  29.2 1.0 %collective-permute-start.7 = (bf16[4,144,128]{2,1,0:T(8,128)(2,1)S(1)}, bf16[4,144,128]{2,1,0:T(8,128)(2,1)S(1)}, u32[]{:S(2)}, u32[]{:S(2)}) collective-permute-start(bf16[4,144,128]{2,1,0:T(8,128)(2,1)S(1)} %get-tuple-element.34), channel_id=1, source_target_pairs={{0,4},{4,0},{8,12},{12,8},{16,20},{20,16},{24,28},{28,24},{1,5},{5... | collective-permute-start | bytes 442376 | tf_op jit(solution)/shard_map/ppermute | solution.py:354
  30.2 0.0 collective-permute-done.11.other_ref
  30.2 0.1 merge.3
  30.4 0.3 collective-permute-start.12
  30.7 3.0 %collective-permute-start.13 = (bf16[144,128]{1,0:T(8,128)(2,1)S(1)}, bf16[144,128]{1,0:T(8,128)(2,1)S(1)}, u32[]{:S(2)}, u32[]{:S(2)}) collective-permute-start(bf16[144,128]{1,0:T(8,128)(2,1)S(1)} %get-tuple-element.43), channel_id=1, source_target_pairs={{0,16},{4,20},{8,24},{12,28},{16,0},{20,4},{24,8},{28,12},{1,17},{... | collective-permute-start | bytes 110600 | tf_op jit(solution)/shard_map/ppermute | solution.py:354
  33.7 1.1 %collective-permute-start.14 = (bf16[144,128]{1,0:T(8,128)(2,1)S(1)}, bf16[144,128]{1,0:T(8,128)(2,1)S(1)}, u32[]{:S(2)}, u32[]{:S(2)}) collective-permute-start(bf16[144,128]{1,0:T(8,128)(2,1)S(1)} %get-tuple-element.44), channel_id=1, source_target_pairs={{0,24},{4,28},{8,16},{12,20},{16,8},{20,12},{24,0},{28,4},{1,25},{... | collective-permute-start | bytes 110600 | tf_op jit(solution)/shard_map/ppermute | solution.py:354
  34.8 0.0 collective-permute-done.7.other_ref
  34.8 0.1 merge.2
  35.0 0.1 collective-permute-start.8
  35.1 3.3 %collective-permute-start.9 = (bf16[144,128]{1,0:T(8,128)(2,1)S(1)}, bf16[144,128]{1,0:T(8,128)(2,1)S(1)}, u32[]{:S(2)}, u32[]{:S(2)}) collective-permute-start(bf16[144,128]{1,0:T(8,128)(2,1)S(1)} %get-tuple-element.37), channel_id=1, source_target_pairs={{0,16},{4,20},{8,24},{12,28},{16,0},{20,4},{24,8},{28,12},{1,17},{... | collective-permute-start | bytes 110600 | tf_op jit(solution)/shard_map/ppermute | solution.py:354
  38.3 1.1 %collective-permute-start.10 = (bf16[144,128]{1,0:T(8,128)(2,1)S(1)}, bf16[144,128]{1,0:T(8,128)(2,1)S(1)}, u32[]{:S(2)}, u32[]{:S(2)}) collective-permute-start(bf16[144,128]{1,0:T(8,128)(2,1)S(1)} %get-tuple-element.38), channel_id=1, source_target_pairs={{0,24},{4,28},{8,16},{12,20},{16,8},{20,12},{24,0},{28,4},{1,25},{... | collective-permute-start | bytes 110600 | tf_op jit(solution)/shard_map/ppermute | solution.py:354
  39.4 0.0 collective-permute-done.13.refs_6_
  39.4 0.0 collective-permute-done.14.refs_7_
  39.5 0.8 %collective-permute-done.9.refs_2_ = bf16[144,128]{1,0:T(8,128)(2,1)S(1)} collective-permute-done((bf16[144,128]{1,0:T(8,128)(2,1)S(1)}, bf16[144,128]{1,0:T(8,128)(2,1)S(1)}, u32[]{:S(2)}, u32[]{:S(2)}) %collective-permute-start.9) | collective-permute-done | bytes 36896 | tf_op jit(solution)/shard_map/ppermute | solution.py:354
  40.3 3.8 %collective-permute-done.10.refs_3_ = bf16[144,128]{1,0:T(8,128)(2,1)S(1)} collective-permute-done((bf16[144,128]{1,0:T(8,128)(2,1)S(1)}, bf16[144,128]{1,0:T(8,128)(2,1)S(1)}, u32[]{:S(2)}, u32[]{:S(2)}) %collective-permute-start.10) | collective-permute-done | bytes 36896 | tf_op jit(solution)/shard_map/ppermute | solution.py:354
  44.2 2.9 %up_and_far_output.1 = (bf16[4,4,896]{2,1,0:T(4,128)(2,1)S(1)}, f32[8,2048]{1,0:T(8,128)S(1)}) custom-call(bf16[144,128]{1,0:T(8,128)(2,1)S(1)} %get-tuple-element.35.refs_0_, bf16[144,128]{1,0:T(8,128)(2,1)S(1)} %collective-permute-done.8.refs_1_, bf16[144,128]{1,0:T(8,128)(2,1)S(1)} %collective-permute-done.9.refs_2_, ...), custom_call_target="tpu_custom_call" | custom-call | flops 20000000000 | bytes 1048576 | tf_op jit(solution)/shard_map/up_and_far_output/pallas_call | solution.py:428
  47.1 2.1 %near_output.1.own_ref = f32[4,4,896]{2,1,0:T(4,128)S(1)} custom-call(f32[8,2048]{1,0:T(8,128)S(1)} %get-tuple-element.45.values, bf16[2048,7168]{1,0:T(8,128)(2,1)S(1)} %bitcast.11), custom_call_target="tpu_custom_call" | custom-call | flops 20000000000 | bytes 1048576 | tf_op jit(solution)/shard_map/near_output/pallas_call | solution.py:439
  49.2 1.7 %collective-permute-done.15.other_ref = bf16[4,4,896]{2,1,0:T(4,128)(2,1)S(1)} collective-permute-done((bf16[4,4,896]{2,1,0:T(4,128)(2,1)S(1)}, bf16[4,4,896]{2,1,0:T(4,128)(2,1)S(1)}, u32[]{:S(2)}, u32[]{:S(2)}) %collective-permute-start.15) | collective-permute-done | bytes 28704 | tf_op jit(solution)/shard_map/ppermute | solution.py:354
  51.0 0.8 %collective-permute-start.16 = (bf16[4,896]{1,0:T(4,128)(2,1)S(1)}, bf16[4,896]{1,0:T(4,128)(2,1)S(1)}, u32[]{:S(2)}, u32[]{:S(2)}) collective-permute-start(bf16[4,896]{1,0:T(4,128)(2,1)S(1)} %get-tuple-element.48), channel_id=1, source_target_pairs={{0,4},{4,0},{8,12},{12,8},{16,20},{20,16},{24,28},{28,24},{1,5},{5... | collective-permute-start | bytes 21512 | tf_op jit(solution)/shard_map/ppermute | solution.py:354
  51.8 0.2 collective-permute-start.17
  52.0 3.4 %collective-permute-start.18 = (bf16[4,896]{1,0:T(4,128)(2,1)S(1)}, bf16[4,896]{1,0:T(4,128)(2,1)S(1)}, u32[]{:S(2)}, u32[]{:S(2)}) collective-permute-start(bf16[4,896]{1,0:T(4,128)(2,1)S(1)} %get-tuple-element.50), channel_id=1, source_target_pairs={{0,20},{4,16},{8,28},{12,24},{16,4},{20,0},{24,12},{28,8},{1,21},{... | collective-permute-start | bytes 21512 | tf_op jit(solution)/shard_map/ppermute | solution.py:354
  55.4 0.9 %collective-permute-done.17.refs_1_ = bf16[4,896]{1,0:T(4,128)(2,1)S(1)} collective-permute-done((bf16[4,896]{1,0:T(4,128)(2,1)S(1)}, bf16[4,896]{1,0:T(4,128)(2,1)S(1)}, u32[]{:S(2)}, u32[]{:S(2)}) %collective-permute-start.17) | collective-permute-done | bytes 7200 | tf_op jit(solution)/shard_map/ppermute | solution.py:354
  56.3 1.1 %collective-permute-done.18.refs_2_ = bf16[4,896]{1,0:T(4,128)(2,1)S(1)} collective-permute-done((bf16[4,896]{1,0:T(4,128)(2,1)S(1)}, bf16[4,896]{1,0:T(4,128)(2,1)S(1)}, u32[]{:S(2)}, u32[]{:S(2)}) %collective-permute-start.18) | collective-permute-done | bytes 7200 | tf_op jit(solution)/shard_map/ppermute | solution.py:354
  57.5 0.6 %sum_output.1 = bf16[2,2,896]{2,1,0:T(2,128)(2,1)} custom-call(f32[4,896]{1,0:T(4,128)S(1)} %get-tuple-element.47.own_ref, bf16[4,896]{1,0:T(4,128)(2,1)S(1)} %collective-permute-done.16.refs_0_, bf16[4,896]{1,0:T(4,128)(2,1)S(1)} %collective-permute-done.17.refs_1_, bf16[4,896]{1,0:T(4,128)(2,1)S(1)} %collective-permute-done.18.refs_2_), custom_call_target="tpu_custom_call" | custom-call | tf_op jit(solution)/shard_map/sum_output/pallas_call | solution.py:454
  (26 shorter events, 0.1 us)
Async XLA Ops:
  1.8 8.5 %collective-permute-start.2 = (bf16[288,128]{1,0:T(8,128)(2,1)S(1)}, bf16[288,128]{1,0:T(8,128)(2,1)S(1)}, u32[]{:S(2)}, u32[]{:S(2)}) collective-permute-start(bf16[288,128]{1,0:T(8,128)(2,1)S(1)} %get-tuple-element.28.refs_0_), channel_id=1, source_target_pairs={{0,24},{4,28},{8,16},{12,20},{16,8},{20,12},{24,0},{28,4},{1,25},{... | collective-permute-start | bytes 221192 | tf_op jit(solution)/shard_map/ppermute | solution.py:354
  6.9 6.2 %collective-permute-start.1 = (bf16[288,128]{1,0:T(8,128)(2,1)S(1)}, bf16[288,128]{1,0:T(8,128)(2,1)S(1)}, u32[]{:S(2)}, u32[]{:S(2)}) collective-permute-start(bf16[288,128]{1,0:T(8,128)(2,1)S(1)} %get-tuple-element.28.refs_0_), channel_id=1, source_target_pairs={{0,16},{4,20},{8,24},{12,28},{16,0},{20,4},{24,8},{28,12},{1,17},{... | collective-permute-start | bytes 221192 | tf_op jit(solution)/shard_map/ppermute | solution.py:354
  6.9 7.7 %collective-permute-start = (bf16[288,128]{1,0:T(8,128)(2,1)S(1)}, bf16[288,128]{1,0:T(8,128)(2,1)S(1)}, u32[]{:S(2)}, u32[]{:S(2)}) collective-permute-start(bf16[288,128]{1,0:T(8,128)(2,1)S(1)} %get-tuple-element.28.refs_0_), channel_id=1, source_target_pairs={{0,8},{4,12},{8,0},{12,4},{16,24},{20,28},{24,16},{28,20},{1,9},{5... | collective-permute-start | bytes 221192 | tf_op jit(solution)/shard_map/ppermute | solution.py:354
  7.6 7.6 %slice-start = ((s8[9437184]{0:T(1024)(128)(4,1)}), s8[4194304]{0:T(1024)(128)(4,1)S(1)}, s32[]{:S(2)}) async-start(s8[9437184]{0:T(1024)(128)(4,1)} %bitcast.4), calls=%async_computation | async-start | bytes 8388608
  7.6 7.6 %slice-start.1 = ((s8[9437184]{0:T(1024)(128)(4,1)}), s8[4194304]{0:T(1024)(128)(4,1)S(1)}, s32[]{:S(2)}) async-start(s8[9437184]{0:T(1024)(128)(4,1)} %bitcast.4), calls=%async_computation.1 | async-start | bytes 8388608
  7.6 7.6 %slice-start.2 = ((s8[9437184]{0:T(1024)(128)(4,1)}), s8[1048576]{0:T(1024)(128)(4,1)S(1)}, s32[]{:S(2)}) async-start(s8[9437184]{0:T(1024)(128)(4,1)} %bitcast.4), calls=%async_computation.2 | async-start | bytes 2097152
  8.6 9.5 %collective-permute-start.3 = (bf16[288,128]{1,0:T(8,128)(2,1)S(1)}, bf16[288,128]{1,0:T(8,128)(2,1)S(1)}, u32[]{:S(2)}, u32[]{:S(2)}) collective-permute-start(bf16[288,128]{1,0:T(8,128)(2,1)S(1)} %get-tuple-element.30), channel_id=1, source_target_pairs={{0,4},{4,0},{8,12},{12,8},{16,20},{20,16},{24,28},{28,24},{1,5},{5... | collective-permute-start | bytes 221192 | tf_op jit(solution)/shard_map/ppermute | solution.py:354
  10.3 7.8 %collective-permute-start.6 = (bf16[288,128]{1,0:T(8,128)(2,1)S(1)}, bf16[288,128]{1,0:T(8,128)(2,1)S(1)}, u32[]{:S(2)}, u32[]{:S(2)}) collective-permute-start(bf16[288,128]{1,0:T(8,128)(2,1)S(1)} %collective-permute-done.2.refs_3_), channel_id=1, source_target_pairs={{0,4},{4,0},{8,12},{12,8},{16,20},{20,16},{24,28},{28,24},{1,5},{5... | collective-permute-start | bytes 221192 | tf_op jit(solution)/shard_map/ppermute | solution.py:354
  13.1 5.0 %collective-permute-start.5 = (bf16[288,128]{1,0:T(8,128)(2,1)S(1)}, bf16[288,128]{1,0:T(8,128)(2,1)S(1)}, u32[]{:S(2)}, u32[]{:S(2)}) collective-permute-start(bf16[288,128]{1,0:T(8,128)(2,1)S(1)} %collective-permute-done.1.refs_2_), channel_id=1, source_target_pairs={{0,4},{4,0},{8,12},{12,8},{16,20},{20,16},{24,28},{28,24},{1,5},{5... | collective-permute-start | bytes 221192 | tf_op jit(solution)/shard_map/ppermute | solution.py:354
  14.6 4.4 %collective-permute-start.4 = (bf16[288,128]{1,0:T(8,128)(2,1)S(1)}, bf16[288,128]{1,0:T(8,128)(2,1)S(1)}, u32[]{:S(2)}, u32[]{:S(2)}) collective-permute-start(bf16[288,128]{1,0:T(8,128)(2,1)S(1)} %collective-permute-done.refs_1_), channel_id=1, source_target_pairs={{0,4},{4,0},{8,12},{12,8},{16,20},{20,16},{24,28},{28,24},{1,5},{5... | collective-permute-start | bytes 221192 | tf_op jit(solution)/shard_map/ppermute | solution.py:354
  23.4 20.6 %slice-start.3 = ((s8[29360128]{0:T(1024)(128)(4,1)}), s8[4194304]{0:T(1024)(128)(4,1)S(1)}, s32[]{:S(2)}) async-start(s8[29360128]{0:T(1024)(128)(4,1)} %bitcast.10), calls=%async_computation.3 | async-start | bytes 8388608
  23.5 20.6 %slice-start.4 = ((s8[29360128]{0:T(1024)(128)(4,1)}), s8[4194304]{0:T(1024)(128)(4,1)S(1)}, s32[]{:S(2)}) async-start(s8[29360128]{0:T(1024)(128)(4,1)} %bitcast.10), calls=%async_computation.4 | async-start | bytes 8388608
  23.5 20.6 %slice-start.5 = ((s8[29360128]{0:T(1024)(128)(4,1)}), s8[4194304]{0:T(1024)(128)(4,1)S(1)}, s32[]{:S(2)}) async-start(s8[29360128]{0:T(1024)(128)(4,1)} %bitcast.10), calls=%async_computation.5 | async-start | bytes 8388608
  23.5 20.6 %slice-start.6 = ((s8[29360128]{0:T(1024)(128)(4,1)}), s8[4194304]{0:T(1024)(128)(4,1)S(1)}, s32[]{:S(2)}) async-start(s8[29360128]{0:T(1024)(128)(4,1)} %bitcast.10), calls=%async_computation.6 | async-start | bytes 8388608
  23.5 20.6 %slice-start.7 = ((s8[29360128]{0:T(1024)(128)(4,1)}), s8[4194304]{0:T(1024)(128)(4,1)S(1)}, s32[]{:S(2)}) async-start(s8[29360128]{0:T(1024)(128)(4,1)} %bitcast.10), calls=%async_computation.7 | async-start | bytes 8388608
  23.5 20.6 %slice-start.8 = ((s8[29360128]{0:T(1024)(128)(4,1)}), s8[4194304]{0:T(1024)(128)(4,1)S(1)}, s32[]{:S(2)}) async-start(s8[29360128]{0:T(1024)(128)(4,1)} %bitcast.10), calls=%async_computation.8 | async-start | bytes 8388608
  23.5 20.6 %slice-start.9 = ((s8[29360128]{0:T(1024)(128)(4,1)}), s8[4194304]{0:T(1024)(128)(4,1)S(1)}, s32[]{:S(2)}) async-start(s8[29360128]{0:T(1024)(128)(4,1)} %bitcast.10), calls=%async_computation.9 | async-start | bytes 8388608
  23.5 20.6 %copy-start = (bf16[16,512,128]{2,1,0:T(8,128)(2,1)S(1)}, bf16[16,512,128]{2,1,0:T(8,128)(2,1)}, u32[]{:S(2)}) copy-start(bf16[16,512,128]{2,1,0:T(8,128)(2,1)} %refs_8_.1) | copy-start | bytes 6291460
  23.5 6.7 %collective-permute-start.11 = (bf16[4,144,128]{2,1,0:T(8,128)(2,1)S(1)}, bf16[4,144,128]{2,1,0:T(8,128)(2,1)S(1)}, u32[]{:S(2)}, u32[]{:S(2)}) collective-permute-start(bf16[4,144,128]{2,1,0:T(8,128)(2,1)S(1)} %get-tuple-element.40), channel_id=1, source_target_pairs={{0,4},{4,0},{8,12},{12,8},{16,20},{20,16},{24,28},{28,24},{1,5},{5... | collective-permute-start | bytes 442376 | tf_op jit(solution)/shard_map/ppermute | solution.py:354
  29.2 5.7 %collective-permute-start.7 = (bf16[4,144,128]{2,1,0:T(8,128)(2,1)S(1)}, bf16[4,144,128]{2,1,0:T(8,128)(2,1)S(1)}, u32[]{:S(2)}, u32[]{:S(2)}) collective-permute-start(bf16[4,144,128]{2,1,0:T(8,128)(2,1)S(1)} %get-tuple-element.34), channel_id=1, source_target_pairs={{0,4},{4,0},{8,12},{12,8},{16,20},{20,16},{24,28},{28,24},{1,5},{5... | collective-permute-start | bytes 442376 | tf_op jit(solution)/shard_map/ppermute | solution.py:354
  30.4 8.0 %collective-permute-start.12 = (bf16[144,128]{1,0:T(8,128)(2,1)S(1)}, bf16[144,128]{1,0:T(8,128)(2,1)S(1)}, u32[]{:S(2)}, u32[]{:S(2)}) collective-permute-start(bf16[144,128]{1,0:T(8,128)(2,1)S(1)} %get-tuple-element.42), channel_id=1, source_target_pairs={{0,8},{4,12},{8,0},{12,4},{16,24},{20,28},{24,16},{28,20},{1,9},{5... | collective-permute-start | bytes 110600 | tf_op jit(solution)/shard_map/ppermute | solution.py:354
  30.7 8.8 %collective-permute-start.13 = (bf16[144,128]{1,0:T(8,128)(2,1)S(1)}, bf16[144,128]{1,0:T(8,128)(2,1)S(1)}, u32[]{:S(2)}, u32[]{:S(2)}) collective-permute-start(bf16[144,128]{1,0:T(8,128)(2,1)S(1)} %get-tuple-element.43), channel_id=1, source_target_pairs={{0,16},{4,20},{8,24},{12,28},{16,0},{20,4},{24,8},{28,12},{1,17},{... | collective-permute-start | bytes 110600 | tf_op jit(solution)/shard_map/ppermute | solution.py:354
  33.7 5.8 %collective-permute-start.14 = (bf16[144,128]{1,0:T(8,128)(2,1)S(1)}, bf16[144,128]{1,0:T(8,128)(2,1)S(1)}, u32[]{:S(2)}, u32[]{:S(2)}) collective-permute-start(bf16[144,128]{1,0:T(8,128)(2,1)S(1)} %get-tuple-element.44), channel_id=1, source_target_pairs={{0,24},{4,28},{8,16},{12,20},{16,8},{20,12},{24,0},{28,4},{1,25},{... | collective-permute-start | bytes 110600 | tf_op jit(solution)/shard_map/ppermute | solution.py:354
  35.0 4.5 %collective-permute-start.8 = (bf16[144,128]{1,0:T(8,128)(2,1)S(1)}, bf16[144,128]{1,0:T(8,128)(2,1)S(1)}, u32[]{:S(2)}, u32[]{:S(2)}) collective-permute-start(bf16[144,128]{1,0:T(8,128)(2,1)S(1)} %get-tuple-element.36), channel_id=1, source_target_pairs={{0,8},{4,12},{8,0},{12,4},{16,24},{20,28},{24,16},{28,20},{1,9},{5... | collective-permute-start | bytes 110600 | tf_op jit(solution)/shard_map/ppermute | solution.py:354
  35.1 5.2 %collective-permute-start.9 = (bf16[144,128]{1,0:T(8,128)(2,1)S(1)}, bf16[144,128]{1,0:T(8,128)(2,1)S(1)}, u32[]{:S(2)}, u32[]{:S(2)}) collective-permute-start(bf16[144,128]{1,0:T(8,128)(2,1)S(1)} %get-tuple-element.37), channel_id=1, source_target_pairs={{0,16},{4,20},{8,24},{12,28},{16,0},{20,4},{24,8},{28,12},{1,17},{... | collective-permute-start | bytes 110600 | tf_op jit(solution)/shard_map/ppermute | solution.py:354
  38.3 5.8 %collective-permute-start.10 = (bf16[144,128]{1,0:T(8,128)(2,1)S(1)}, bf16[144,128]{1,0:T(8,128)(2,1)S(1)}, u32[]{:S(2)}, u32[]{:S(2)}) collective-permute-start(bf16[144,128]{1,0:T(8,128)(2,1)S(1)} %get-tuple-element.38), channel_id=1, source_target_pairs={{0,24},{4,28},{8,16},{12,20},{16,8},{20,12},{24,0},{28,4},{1,25},{... | collective-permute-start | bytes 110600 | tf_op jit(solution)/shard_map/ppermute | solution.py:354
  47.0 3.9 %collective-permute-start.15 = (bf16[4,4,896]{2,1,0:T(4,128)(2,1)S(1)}, bf16[4,4,896]{2,1,0:T(4,128)(2,1)S(1)}, u32[]{:S(2)}, u32[]{:S(2)}) collective-permute-start(bf16[4,4,896]{2,1,0:T(4,128)(2,1)S(1)} %get-tuple-element.46), channel_id=1, source_target_pairs={{0,8},{4,12},{8,0},{12,4},{16,24},{20,28},{24,16},{28,20},{1,9},{5... | collective-permute-start | bytes 86024 | tf_op jit(solution)/shard_map/ppermute | solution.py:354
  51.0 4.5 %collective-permute-start.16 = (bf16[4,896]{1,0:T(4,128)(2,1)S(1)}, bf16[4,896]{1,0:T(4,128)(2,1)S(1)}, u32[]{:S(2)}, u32[]{:S(2)}) collective-permute-start(bf16[4,896]{1,0:T(4,128)(2,1)S(1)} %get-tuple-element.48), channel_id=1, source_target_pairs={{0,4},{4,0},{8,12},{12,8},{16,20},{20,16},{24,28},{28,24},{1,5},{5... | collective-permute-start | bytes 21512 | tf_op jit(solution)/shard_map/ppermute | solution.py:354
  51.8 4.5 %collective-permute-start.17 = (bf16[4,896]{1,0:T(4,128)(2,1)S(1)}, bf16[4,896]{1,0:T(4,128)(2,1)S(1)}, u32[]{:S(2)}, u32[]{:S(2)}) collective-permute-start(bf16[4,896]{1,0:T(4,128)(2,1)S(1)} %get-tuple-element.49), channel_id=1, source_target_pairs={{0,16},{4,20},{8,24},{12,28},{16,0},{20,4},{24,8},{28,12},{1,17},{... | collective-permute-start | bytes 21512 | tf_op jit(solution)/shard_map/ppermute | solution.py:354
  52.0 5.4 %collective-permute-start.18 = (bf16[4,896]{1,0:T(4,128)(2,1)S(1)}, bf16[4,896]{1,0:T(4,128)(2,1)S(1)}, u32[]{:S(2)}, u32[]{:S(2)}) collective-permute-start(bf16[4,896]{1,0:T(4,128)(2,1)S(1)} %get-tuple-element.50), channel_id=1, source_target_pairs={{0,20},{4,16},{8,28},{12,24},{16,4},{20,0},{24,12},{28,8},{1,21},{... | collective-permute-start | bytes 21512 | tf_op jit(solution)/shard_map/ppermute | solution.py:354

commit v4 on v1

--- a/solution.py
+++ b/solution.py
@@ -399,7 +399,7 @@
             name="merge",
         )(near, swap(far, 1))
         parts.append(merged[0])
-        parts += [swap(merged[k], 2 * k) for k in range(1, line)]
+        parts += [swap(merged[k], 2 * k) for k in reversed(range(1, line))]
 
     tokens = requests * query_len
     weight = in_vmem(output_weight)
@@ -435,7 +435,7 @@
         out_shape=jax.ShapeDtypeStruct((requests, query_len, width), jnp.bfloat16),
         compiler_params=small,
         name="sum_output",
-    )(kept, *(swap(part, bits) for part, bits in zip(sent, (1, 4, 5))))
+    )(kept, *(swap(part, bits) for part, bits in reversed([*zip(sent, (1, 4, 5))])))
 
 
 def plain_device(

time: 57.8 us -> 57 us (0.986)
  waiting for transfers between devices: 14.2 us -> 13.2 us
    ppermute x19, waiting for transfers between devices: 14.2 us -> 13.2 us  [per_device(): lax.ppermute(value, 'ctx', [(i, i ^ bits) for i in range(ctx)])]
  transfers between devices with their start and end apart: 19 -> 19, of which waited for: 9 -> 8; matrix products, arithmetic and copies ran while one was open for 0% -> 0% of each run, Pallas kernels for 14% -> 14%
where the time goes in v4:
time: 57 us; the launch traced here: 56.9 us
  starting transfers between devices  26.1 us (46%)
  Pallas kernels  17.3 us (30%)
  waiting for transfers between devices  13.2 us (23%)
    ppermute x19, starting transfers between devices, per_device(): lax.ppermute(value, 'ctx', [(i, i ^ bits) for i in range(ctx)])  26.1 us
    ppermute x19, waiting for transfers between devices, per_device(): lax.ppermute(value, 'ctx', [(i, i ^ bits) for i in range(ctx)])  13.2 us
    pallas_call x2, Pallas kernels, per_device(): pl.pallas_call(functools.partial(attention_kernel, ctx=ctx, b=b), in_spec...  8.66 us
    pallas_call x1, Pallas kernels, per_device(): pl.pallas_call(output_kernel, out_shape=[jax.ShapeDtypeStruct((line, toke...  2.88 us
    pallas_call x1, Pallas kernels, per_device(): pl.pallas_call(near_kernel, out_shape=jax.ShapeDtypeStruct((line, tokens,...  2.14 us
    pallas_call x1, Pallas kernels, per_device(): pl.pallas_call(query_kernel, in_specs=[pl.BlockSpec(memory_space=pl.ANY)]...  1.8 us
  transfers between devices with their start and end apart: 19, of which 8 were waited for; matrix products, arithmetic and copies ran while one was open for 0% of the time, Pallas kernels for 14%

profile of v4, /device:TPU:0, one launch (start us, length us, event | category | flops | bytes accessed | tf_op | source)
XLA Modules:
  0.0 56.9 jit_solution(7481487531652478468)
XLA Ops:
  0.0 1.8 %latent_query.1 = (bf16[288,128]{1,0:T(8,128)(2,1)S(1)}, bf16[288,128]{1,0:T(8,128)(2,1)S(1)}) custom-call(bf16[64,192]{1,0:T(8,128)(2,1)} %bitcast.8, bf16[16,128,512]{2,1,0:T(8,128)(2,1)} %absorb_hbm.1), custom_call_target="tpu_custom_call" | custom-call | tf_op jit(solution)/shard_map/latent_query/pallas_call | solution.py:343
  1.8 3.1 %collective-permute-start = (bf16[288,128]{1,0:T(8,128)(2,1)S(1)}, bf16[288,128]{1,0:T(8,128)(2,1)S(1)}, u32[]{:S(2)}, u32[]{:S(2)}) collective-permute-start(bf16[288,128]{1,0:T(8,128)(2,1)S(1)} %get-tuple-element.28.refs_0_), channel_id=1, source_target_pairs={{0,8},{4,12},{8,0},{12,4},{16,24},{20,28},{24,16},{28,20},{1,9},{5... | collective-permute-start | bytes 221192 | tf_op jit(solution)/shard_map/ppermute | solution.py:342
  4.9 2.6 %collective-permute-start.1 = (bf16[288,128]{1,0:T(8,128)(2,1)S(1)}, bf16[288,128]{1,0:T(8,128)(2,1)S(1)}, u32[]{:S(2)}, u32[]{:S(2)}) collective-permute-start(bf16[288,128]{1,0:T(8,128)(2,1)S(1)} %get-tuple-element.28.refs_0_), channel_id=1, source_target_pairs={{0,16},{4,20},{8,24},{12,28},{16,0},{20,4},{24,8},{28,12},{1,17},{... | collective-permute-start | bytes 221192 | tf_op jit(solution)/shard_map/ppermute | solution.py:342
  7.5 0.0 collective-permute-start.2
  7.5 1.0 %head_columns.1 = (f32[8,16,128]{2,1,0:T(8,128)S(1)}, f32[8,16,128]{2,1,0:T(8,128)S(1)}, bf16[288,128]{1,0:T(8,128)(2,1)S(1)}) custom-call(f32[1,128]{1,0:T(1,128)} %bitcast.9, f32[1,128]{1,0:T(1,128)} %bitcast.10, bf16[288,128]{1,0:T(8,128)(2,1)S(1)} %get-tuple-element.29.through_ref), custom_call_target="tpu_custom_call", output_to_operand_aliasing={{2}: (2, {})} | custom-call | flops 99999997952 | bytes 1048576 | tf_op jit(solution)/shard_map/head_columns/pallas_call | solution.py:356
  8.5 1.8 %collective-permute-start.3 = (bf16[288,128]{1,0:T(8,128)(2,1)S(1)}, bf16[288,128]{1,0:T(8,128)(2,1)S(1)}, u32[]{:S(2)}, u32[]{:S(2)}) collective-permute-start(bf16[288,128]{1,0:T(8,128)(2,1)S(1)} %get-tuple-element.30), channel_id=1, source_target_pairs={{0,4},{4,0},{8,12},{12,8},{16,20},{20,16},{24,28},{28,24},{1,5},{5... | collective-permute-start | bytes 221192 | tf_op jit(solution)/shard_map/ppermute | solution.py:342
  10.2 0.0 collective-permute-done.refs_1_
  10.2 0.3 collective-permute-start.4
  10.5 2.1 %collective-permute-done.1.refs_2_ = bf16[288,128]{1,0:T(8,128)(2,1)S(1)} collective-permute-done((bf16[288,128]{1,0:T(8,128)(2,1)S(1)}, bf16[288,128]{1,0:T(8,128)(2,1)S(1)}, u32[]{:S(2)}, u32[]{:S(2)}) %collective-permute-start.1) | collective-permute-done | bytes 73760 | tf_op jit(solution)/shard_map/ppermute | solution.py:342
  12.7 1.5 %collective-permute-start.5 = (bf16[288,128]{1,0:T(8,128)(2,1)S(1)}, bf16[288,128]{1,0:T(8,128)(2,1)S(1)}, u32[]{:S(2)}, u32[]{:S(2)}) collective-permute-start(bf16[288,128]{1,0:T(8,128)(2,1)S(1)} %collective-permute-done.1.refs_2_), channel_id=1, source_target_pairs={{0,4},{4,0},{8,12},{12,8},{16,20},{20,16},{24,28},{28,24},{1,5},{5... | collective-permute-start | bytes 221192 | tf_op jit(solution)/shard_map/ppermute | solution.py:342
  14.2 0.0 collective-permute-done.2.refs_3_
  14.2 1.1 %collective-permute-start.6 = (bf16[288,128]{1,0:T(8,128)(2,1)S(1)}, bf16[288,128]{1,0:T(8,128)(2,1)S(1)}, u32[]{:S(2)}, u32[]{:S(2)}) collective-permute-start(bf16[288,128]{1,0:T(8,128)(2,1)S(1)} %collective-permute-done.2.refs_3_), channel_id=1, source_target_pairs={{0,4},{4,0},{8,12},{12,8},{16,20},{20,16},{24,28},{28,24},{1,5},{5... | collective-permute-start | bytes 221192 | tf_op jit(solution)/shard_map/ppermute | solution.py:342
  15.2 0.0 collective-permute-done.3.refs_4_
  15.2 0.0 collective-permute-done.4.refs_5_
  15.2 1.8 %collective-permute-done.5.refs_6_ = bf16[288,128]{1,0:T(8,128)(2,1)S(1)} collective-permute-done((bf16[288,128]{1,0:T(8,128)(2,1)S(1)}, bf16[288,128]{1,0:T(8,128)(2,1)S(1)}, u32[]{:S(2)}, u32[]{:S(2)}) %collective-permute-start.5) | collective-permute-done | bytes 73760 | tf_op jit(solution)/shard_map/ppermute | solution.py:342
  17.0 1.5 %collective-permute-done.6.refs_7_ = bf16[288,128]{1,0:T(8,128)(2,1)S(1)} collective-permute-done((bf16[288,128]{1,0:T(8,128)(2,1)S(1)}, bf16[288,128]{1,0:T(8,128)(2,1)S(1)}, u32[]{:S(2)}, u32[]{:S(2)}) %collective-permute-start.6) | collective-permute-done | bytes 73760 | tf_op jit(solution)/shard_map/ppermute | solution.py:342
  18.5 4.3 %attention.2 = (bf16[4,144,128]{2,1,0:T(8,128)(2,1)S(1)}, bf16[4,144,128]{2,1,0:T(8,128)(2,1)S(1)}) custom-call(s32[2,32]{1,0:T(2,128)} %pages_ref.3, s32[2]{0:T(128)} %lengths_ref.3, bf16[288,128]{1,0:T(8,128)(2,1)S(1)} %get-tuple-element.28.refs_0_, bf16[288,128]{1,0:T(8,128)(2,1)S(1)} %collective-permute-done.refs_1_, ...), custom_call_target="tpu_custom_call" | custom-call | flops 20000000000 | bytes 1048576 | tf_op jit(solution)/shard_map/attention/pallas_call | solution.py:379
  22.8 0.0 slice-start
  22.8 0.0 slice-start.3
  22.8 0.0 slice-start.4
  22.9 0.0 slice-start.6
  22.9 0.0 copy-start.1
  22.9 1.1 %collective-permute-start.7 = (bf16[4,144,128]{2,1,0:T(8,128)(2,1)S(1)}, bf16[4,144,128]{2,1,0:T(8,128)(2,1)S(1)}, u32[]{:S(2)}, u32[]{:S(2)}) collective-permute-start(bf16[4,144,128]{2,1,0:T(8,128)(2,1)S(1)} %get-tuple-element.34), channel_id=1, source_target_pairs={{0,4},{4,0},{8,12},{12,8},{16,20},{20,16},{24,28},{28,24},{1,5},{5... | collective-permute-start | bytes 442376 | tf_op jit(solution)/shard_map/ppermute | solution.py:342
  24.0 4.4 %attention.3 = (bf16[4,144,128]{2,1,0:T(8,128)(2,1)S(1)}, bf16[4,144,128]{2,1,0:T(8,128)(2,1)S(1)}) custom-call(s32[2,32]{1,0:T(2,128)} %pages_ref.3, s32[2]{0:T(128)} %lengths_ref.3, bf16[288,128]{1,0:T(8,128)(2,1)S(1)} %get-tuple-element.28.refs_0_, bf16[288,128]{1,0:T(8,128)(2,1)S(1)} %collective-permute-done.refs_1_, ...), custom_call_target="tpu_custom_call" | custom-call | flops 20000000000 | bytes 1048576 | tf_op jit(solution)/shard_map/attention/pallas_call | solution.py:379
  28.4 1.0 %collective-permute-start.11 = (bf16[4,144,128]{2,1,0:T(8,128)(2,1)S(1)}, bf16[4,144,128]{2,1,0:T(8,128)(2,1)S(1)}, u32[]{:S(2)}, u32[]{:S(2)}) collective-permute-start(bf16[4,144,128]{2,1,0:T(8,128)(2,1)S(1)} %get-tuple-element.40), channel_id=1, source_target_pairs={{0,4},{4,0},{8,12},{12,8},{16,20},{20,16},{24,28},{28,24},{1,5},{5... | collective-permute-start | bytes 442376 | tf_op jit(solution)/shard_map/ppermute | solution.py:342
  29.4 0.0 collective-permute-done.7.other_ref
  29.5 0.1 merge.2
  29.6 3.3 %collective-permute-start.8 = (bf16[144,128]{1,0:T(8,128)(2,1)S(1)}, bf16[144,128]{1,0:T(8,128)(2,1)S(1)}, u32[]{:S(2)}, u32[]{:S(2)}) collective-permute-start(bf16[144,128]{1,0:T(8,128)(2,1)S(1)} %get-tuple-element.36), channel_id=1, source_target_pairs={{0,24},{4,28},{8,16},{12,20},{16,8},{20,12},{24,0},{28,4},{1,25},{... | collective-permute-start | bytes 110600 | tf_op jit(solution)/shard_map/ppermute | solution.py:342
  32.9 1.1 %collective-permute-start.10 = (bf16[144,128]{1,0:T(8,128)(2,1)S(1)}, bf16[144,128]{1,0:T(8,128)(2,1)S(1)}, u32[]{:S(2)}, u32[]{:S(2)}) collective-permute-start(bf16[144,128]{1,0:T(8,128)(2,1)S(1)} %get-tuple-element.38), channel_id=1, source_target_pairs={{0,8},{4,12},{8,0},{12,4},{16,24},{20,28},{24,16},{28,20},{1,9},{5... | collective-permute-start | bytes 110600 | tf_op jit(solution)/shard_map/ppermute | solution.py:342
  34.1 0.0 collective-permute-done.11.other_ref
  34.1 0.1 merge.3
  34.2 3.3 %collective-permute-start.12 = (bf16[144,128]{1,0:T(8,128)(2,1)S(1)}, bf16[144,128]{1,0:T(8,128)(2,1)S(1)}, u32[]{:S(2)}, u32[]{:S(2)}) collective-permute-start(bf16[144,128]{1,0:T(8,128)(2,1)S(1)} %get-tuple-element.42), channel_id=1, source_target_pairs={{0,24},{4,28},{8,16},{12,20},{16,8},{20,12},{24,0},{28,4},{1,25},{... | collective-permute-start | bytes 110600 | tf_op jit(solution)/shard_map/ppermute | solution.py:342
  37.5 0.0 collective-permute-start.13
  37.5 0.0 collective-permute-done.8.refs_1_
  37.6 1.1 %collective-permute-start.14 = (bf16[144,128]{1,0:T(8,128)(2,1)S(1)}, bf16[144,128]{1,0:T(8,128)(2,1)S(1)}, u32[]{:S(2)}, u32[]{:S(2)}) collective-permute-start(bf16[144,128]{1,0:T(8,128)(2,1)S(1)} %get-tuple-element.44), channel_id=1, source_target_pairs={{0,8},{4,12},{8,0},{12,4},{16,24},{20,28},{24,16},{28,20},{1,9},{5... | collective-permute-start | bytes 110600 | tf_op jit(solution)/shard_map/ppermute | solution.py:342
  38.7 1.4 %collective-permute-done.12.refs_5_ = bf16[144,128]{1,0:T(8,128)(2,1)S(1)} collective-permute-done((bf16[144,128]{1,0:T(8,128)(2,1)S(1)}, bf16[144,128]{1,0:T(8,128)(2,1)S(1)}, u32[]{:S(2)}, u32[]{:S(2)}) %collective-permute-start.12) | collective-permute-done | bytes 36896 | tf_op jit(solution)/shard_map/ppermute | solution.py:342
  40.0 2.4 %collective-permute-done.13.refs_6_ = bf16[144,128]{1,0:T(8,128)(2,1)S(1)} collective-permute-done((bf16[144,128]{1,0:T(8,128)(2,1)S(1)}, bf16[144,128]{1,0:T(8,128)(2,1)S(1)}, u32[]{:S(2)}, u32[]{:S(2)}) %collective-permute-start.13) | collective-permute-done | bytes 36896 | tf_op jit(solution)/shard_map/ppermute | solution.py:342
  42.4 0.0 collective-permute-done.14.refs_7_
  42.5 2.9 %up_and_far_output.1 = (bf16[4,4,896]{2,1,0:T(4,128)(2,1)S(1)}, f32[8,2048]{1,0:T(8,128)S(1)}) custom-call(bf16[144,128]{1,0:T(8,128)(2,1)S(1)} %get-tuple-element.35.refs_0_, bf16[144,128]{1,0:T(8,128)(2,1)S(1)} %collective-permute-done.8.refs_1_, bf16[144,128]{1,0:T(8,128)(2,1)S(1)} %collective-permute-done.9.refs_2_, ...), custom_call_target="tpu_custom_call" | custom-call | flops 20000000000 | bytes 1048576 | tf_op jit(solution)/shard_map/up_and_far_output/pallas_call | solution.py:407
  45.4 0.2 collective-permute-start.15
  45.6 2.1 %near_output.1.own_ref = f32[4,4,896]{2,1,0:T(4,128)S(1)} custom-call(f32[8,2048]{1,0:T(8,128)S(1)} %get-tuple-element.45.values, bf16[2048,7168]{1,0:T(8,128)(2,1)S(1)} %bitcast.5), custom_call_target="tpu_custom_call" | custom-call | flops 20000000000 | bytes 1048576 | tf_op jit(solution)/shard_map/near_output/pallas_call | solution.py:418
  47.7 1.5 %collective-permute-done.15.other_ref = bf16[4,4,896]{2,1,0:T(4,128)(2,1)S(1)} collective-permute-done((bf16[4,4,896]{2,1,0:T(4,128)(2,1)S(1)}, bf16[4,4,896]{2,1,0:T(4,128)(2,1)S(1)}, u32[]{:S(2)}, u32[]{:S(2)}) %collective-permute-start.15) | collective-permute-done | bytes 28704 | tf_op jit(solution)/shard_map/ppermute | solution.py:342
  49.3 2.4 %collective-permute-start.16 = (bf16[4,896]{1,0:T(4,128)(2,1)S(1)}, bf16[4,896]{1,0:T(4,128)(2,1)S(1)}, u32[]{:S(2)}, u32[]{:S(2)}) collective-permute-start(bf16[4,896]{1,0:T(4,128)(2,1)S(1)} %get-tuple-element.48), channel_id=1, source_target_pairs={{0,20},{4,16},{8,28},{12,24},{16,4},{20,0},{24,12},{28,8},{1,21},{... | collective-permute-start | bytes 21512 | tf_op jit(solution)/shard_map/ppermute | solution.py:342
  51.7 0.8 %collective-permute-start.17 = (bf16[4,896]{1,0:T(4,128)(2,1)S(1)}, bf16[4,896]{1,0:T(4,128)(2,1)S(1)}, u32[]{:S(2)}, u32[]{:S(2)}) collective-permute-start(bf16[4,896]{1,0:T(4,128)(2,1)S(1)} %get-tuple-element.49), channel_id=1, source_target_pairs={{0,16},{4,20},{8,24},{12,28},{16,0},{20,4},{24,8},{28,12},{1,17},{... | collective-permute-start | bytes 21512 | tf_op jit(solution)/shard_map/ppermute | solution.py:342
  52.5 1.2 %collective-permute-start.18 = (bf16[4,896]{1,0:T(4,128)(2,1)S(1)}, bf16[4,896]{1,0:T(4,128)(2,1)S(1)}, u32[]{:S(2)}, u32[]{:S(2)}) collective-permute-start(bf16[4,896]{1,0:T(4,128)(2,1)S(1)} %get-tuple-element.50), channel_id=1, source_target_pairs={{0,4},{4,0},{8,12},{12,8},{16,20},{20,16},{24,28},{28,24},{1,5},{5... | collective-permute-start | bytes 21512 | tf_op jit(solution)/shard_map/ppermute | solution.py:342
  53.7 1.0 %collective-permute-done.16.refs_0_ = bf16[4,896]{1,0:T(4,128)(2,1)S(1)} collective-permute-done((bf16[4,896]{1,0:T(4,128)(2,1)S(1)}, bf16[4,896]{1,0:T(4,128)(2,1)S(1)}, u32[]{:S(2)}, u32[]{:S(2)}) %collective-permute-start.16) | collective-permute-done | bytes 7200 | tf_op jit(solution)/shard_map/ppermute | solution.py:342
  54.8 1.5 %collective-permute-done.17.refs_1_ = bf16[4,896]{1,0:T(4,128)(2,1)S(1)} collective-permute-done((bf16[4,896]{1,0:T(4,128)(2,1)S(1)}, bf16[4,896]{1,0:T(4,128)(2,1)S(1)}, u32[]{:S(2)}, u32[]{:S(2)}) %collective-permute-start.17) | collective-permute-done | bytes 7200 | tf_op jit(solution)/shard_map/ppermute | solution.py:342
  56.2 0.6 %sum_output.1 = bf16[2,2,896]{2,1,0:T(2,128)(2,1)} custom-call(f32[4,896]{1,0:T(4,128)S(1)} %get-tuple-element.47.own_ref, bf16[4,896]{1,0:T(4,128)(2,1)S(1)} %collective-permute-done.16.refs_0_, bf16[4,896]{1,0:T(4,128)(2,1)S(1)} %collective-permute-done.17.refs_1_, bf16[4,896]{1,0:T(4,128)(2,1)S(1)} %collective-permute-done.18.refs_2_), custom_call_target="tpu_custom_call" | custom-call | tf_op jit(solution)/shard_map/sum_output/pallas_call | solution.py:433
  (19 shorter events, 0.1 us)
Async XLA Ops:
  1.8 8.4 %collective-permute-start = (bf16[288,128]{1,0:T(8,128)(2,1)S(1)}, bf16[288,128]{1,0:T(8,128)(2,1)S(1)}, u32[]{:S(2)}, u32[]{:S(2)}) collective-permute-start(bf16[288,128]{1,0:T(8,128)(2,1)S(1)} %get-tuple-element.28.refs_0_), channel_id=1, source_target_pairs={{0,8},{4,12},{8,0},{12,4},{16,24},{20,28},{24,16},{28,20},{1,9},{5... | collective-permute-start | bytes 221192 | tf_op jit(solution)/shard_map/ppermute | solution.py:342
  4.9 7.8 %collective-permute-start.1 = (bf16[288,128]{1,0:T(8,128)(2,1)S(1)}, bf16[288,128]{1,0:T(8,128)(2,1)S(1)}, u32[]{:S(2)}, u32[]{:S(2)}) collective-permute-start(bf16[288,128]{1,0:T(8,128)(2,1)S(1)} %get-tuple-element.28.refs_0_), channel_id=1, source_target_pairs={{0,16},{4,20},{8,24},{12,28},{16,0},{20,4},{24,8},{28,12},{1,17},{... | collective-permute-start | bytes 221192 | tf_op jit(solution)/shard_map/ppermute | solution.py:342
  7.5 6.7 %collective-permute-start.2 = (bf16[288,128]{1,0:T(8,128)(2,1)S(1)}, bf16[288,128]{1,0:T(8,128)(2,1)S(1)}, u32[]{:S(2)}, u32[]{:S(2)}) collective-permute-start(bf16[288,128]{1,0:T(8,128)(2,1)S(1)} %get-tuple-element.28.refs_0_), channel_id=1, source_target_pairs={{0,24},{4,28},{8,16},{12,20},{16,8},{20,12},{24,0},{28,4},{1,25},{... | collective-permute-start | bytes 221192 | tf_op jit(solution)/shard_map/ppermute | solution.py:342
  7.5 11.0 %copy-start = (bf16[2,4096,576]{1,2,0:T(8,128)(2,1)S(1)}, bf16[2,4096,576]{1,2,0:T(8,128)(2,1)}, u32[]{:S(2)}) copy-start(bf16[2,4096,576]{1,2,0:T(8,128)(2,1)} %param.11) | copy-start | bytes 28311556
  8.5 6.8 %collective-permute-start.3 = (bf16[288,128]{1,0:T(8,128)(2,1)S(1)}, bf16[288,128]{1,0:T(8,128)(2,1)S(1)}, u32[]{:S(2)}, u32[]{:S(2)}) collective-permute-start(bf16[288,128]{1,0:T(8,128)(2,1)S(1)} %get-tuple-element.30), channel_id=1, source_target_pairs={{0,4},{4,0},{8,12},{12,8},{16,20},{20,16},{24,28},{28,24},{1,5},{5... | collective-permute-start | bytes 221192 | tf_op jit(solution)/shard_map/ppermute | solution.py:342
  10.2 5.0 %collective-permute-start.4 = (bf16[288,128]{1,0:T(8,128)(2,1)S(1)}, bf16[288,128]{1,0:T(8,128)(2,1)S(1)}, u32[]{:S(2)}, u32[]{:S(2)}) collective-permute-start(bf16[288,128]{1,0:T(8,128)(2,1)S(1)} %collective-permute-done.refs_1_), channel_id=1, source_target_pairs={{0,4},{4,0},{8,12},{12,8},{16,20},{20,16},{24,28},{28,24},{1,5},{5... | collective-permute-start | bytes 221192 | tf_op jit(solution)/shard_map/ppermute | solution.py:342
  12.7 4.4 %collective-permute-start.5 = (bf16[288,128]{1,0:T(8,128)(2,1)S(1)}, bf16[288,128]{1,0:T(8,128)(2,1)S(1)}, u32[]{:S(2)}, u32[]{:S(2)}) collective-permute-start(bf16[288,128]{1,0:T(8,128)(2,1)S(1)} %collective-permute-done.1.refs_2_), channel_id=1, source_target_pairs={{0,4},{4,0},{8,12},{12,8},{16,20},{20,16},{24,28},{28,24},{1,5},{5... | collective-permute-start | bytes 221192 | tf_op jit(solution)/shard_map/ppermute | solution.py:342
  14.2 4.4 %collective-permute-start.6 = (bf16[288,128]{1,0:T(8,128)(2,1)S(1)}, bf16[288,128]{1,0:T(8,128)(2,1)S(1)}, u32[]{:S(2)}, u32[]{:S(2)}) collective-permute-start(bf16[288,128]{1,0:T(8,128)(2,1)S(1)} %collective-permute-done.2.refs_3_), channel_id=1, source_target_pairs={{0,4},{4,0},{8,12},{12,8},{16,20},{20,16},{24,28},{28,24},{1,5},{5... | collective-permute-start | bytes 221192 | tf_op jit(solution)/shard_map/ppermute | solution.py:342
  22.8 19.6 %slice-start = ((s8[29360128]{0:T(1024)(128)(4,1)}), s8[4194304]{0:T(1024)(128)(4,1)S(1)}, s32[]{:S(2)}) async-start(s8[29360128]{0:T(1024)(128)(4,1)} %bitcast.4), calls=%async_computation | async-start | bytes 8388608
  22.8 19.6 %slice-start.1 = ((s8[29360128]{0:T(1024)(128)(4,1)}), s8[4194304]{0:T(1024)(128)(4,1)S(1)}, s32[]{:S(2)}) async-start(s8[29360128]{0:T(1024)(128)(4,1)} %bitcast.4), calls=%async_computation.1 | async-start | bytes 8388608
  22.8 19.6 %slice-start.2 = ((s8[29360128]{0:T(1024)(128)(4,1)}), s8[4194304]{0:T(1024)(128)(4,1)S(1)}, s32[]{:S(2)}) async-start(s8[29360128]{0:T(1024)(128)(4,1)} %bitcast.4), calls=%async_computation.2 | async-start | bytes 8388608
  22.8 19.6 %slice-start.3 = ((s8[29360128]{0:T(1024)(128)(4,1)}), s8[4194304]{0:T(1024)(128)(4,1)S(1)}, s32[]{:S(2)}) async-start(s8[29360128]{0:T(1024)(128)(4,1)} %bitcast.4), calls=%async_computation.3 | async-start | bytes 8388608
  22.8 19.6 %slice-start.4 = ((s8[29360128]{0:T(1024)(128)(4,1)}), s8[4194304]{0:T(1024)(128)(4,1)S(1)}, s32[]{:S(2)}) async-start(s8[29360128]{0:T(1024)(128)(4,1)} %bitcast.4), calls=%async_computation.4 | async-start | bytes 8388608
  22.9 19.6 %slice-start.5 = ((s8[29360128]{0:T(1024)(128)(4,1)}), s8[4194304]{0:T(1024)(128)(4,1)S(1)}, s32[]{:S(2)}) async-start(s8[29360128]{0:T(1024)(128)(4,1)} %bitcast.4), calls=%async_computation.5 | async-start | bytes 8388608
  22.9 19.6 %slice-start.6 = ((s8[29360128]{0:T(1024)(128)(4,1)}), s8[4194304]{0:T(1024)(128)(4,1)S(1)}, s32[]{:S(2)}) async-start(s8[29360128]{0:T(1024)(128)(4,1)} %bitcast.4), calls=%async_computation.6 | async-start | bytes 8388608
  22.9 19.6 %copy-start.1 = (bf16[16,512,128]{2,1,0:T(8,128)(2,1)S(1)}, bf16[16,512,128]{2,1,0:T(8,128)(2,1)}, u32[]{:S(2)}) copy-start(bf16[16,512,128]{2,1,0:T(8,128)(2,1)} %refs_8_.1) | copy-start | bytes 6291460
  22.9 6.6 %collective-permute-start.7 = (bf16[4,144,128]{2,1,0:T(8,128)(2,1)S(1)}, bf16[4,144,128]{2,1,0:T(8,128)(2,1)S(1)}, u32[]{:S(2)}, u32[]{:S(2)}) collective-permute-start(bf16[4,144,128]{2,1,0:T(8,128)(2,1)S(1)} %get-tuple-element.34), channel_id=1, source_target_pairs={{0,4},{4,0},{8,12},{12,8},{16,20},{20,16},{24,28},{28,24},{1,5},{5... | collective-permute-start | bytes 442376 | tf_op jit(solution)/shard_map/ppermute | solution.py:342
  28.4 5.7 %collective-permute-start.11 = (bf16[4,144,128]{2,1,0:T(8,128)(2,1)S(1)}, bf16[4,144,128]{2,1,0:T(8,128)(2,1)S(1)}, u32[]{:S(2)}, u32[]{:S(2)}) collective-permute-start(bf16[4,144,128]{2,1,0:T(8,128)(2,1)S(1)} %get-tuple-element.40), channel_id=1, source_target_pairs={{0,4},{4,0},{8,12},{12,8},{16,20},{20,16},{24,28},{28,24},{1,5},{5... | collective-permute-start | bytes 442376 | tf_op jit(solution)/shard_map/ppermute | solution.py:342
  29.6 7.9 %collective-permute-start.8 = (bf16[144,128]{1,0:T(8,128)(2,1)S(1)}, bf16[144,128]{1,0:T(8,128)(2,1)S(1)}, u32[]{:S(2)}, u32[]{:S(2)}) collective-permute-start(bf16[144,128]{1,0:T(8,128)(2,1)S(1)} %get-tuple-element.36), channel_id=1, source_target_pairs={{0,24},{4,28},{8,16},{12,20},{16,8},{20,12},{24,0},{28,4},{1,25},{... | collective-permute-start | bytes 110600 | tf_op jit(solution)/shard_map/ppermute | solution.py:342
  32.9 5.7 %collective-permute-start.9 = (bf16[144,128]{1,0:T(8,128)(2,1)S(1)}, bf16[144,128]{1,0:T(8,128)(2,1)S(1)}, u32[]{:S(2)}, u32[]{:S(2)}) collective-permute-start(bf16[144,128]{1,0:T(8,128)(2,1)S(1)} %get-tuple-element.37), channel_id=1, source_target_pairs={{0,16},{4,20},{8,24},{12,28},{16,0},{20,4},{24,8},{28,12},{1,17},{... | collective-permute-start | bytes 110600 | tf_op jit(solution)/shard_map/ppermute | solution.py:342
  32.9 5.7 %collective-permute-start.10 = (bf16[144,128]{1,0:T(8,128)(2,1)S(1)}, bf16[144,128]{1,0:T(8,128)(2,1)S(1)}, u32[]{:S(2)}, u32[]{:S(2)}) collective-permute-start(bf16[144,128]{1,0:T(8,128)(2,1)S(1)} %get-tuple-element.38), channel_id=1, source_target_pairs={{0,8},{4,12},{8,0},{12,4},{16,24},{20,28},{24,16},{28,20},{1,9},{5... | collective-permute-start | bytes 110600 | tf_op jit(solution)/shard_map/ppermute | solution.py:342
  34.2 5.8 %collective-permute-start.12 = (bf16[144,128]{1,0:T(8,128)(2,1)S(1)}, bf16[144,128]{1,0:T(8,128)(2,1)S(1)}, u32[]{:S(2)}, u32[]{:S(2)}) collective-permute-start(bf16[144,128]{1,0:T(8,128)(2,1)S(1)} %get-tuple-element.42), channel_id=1, source_target_pairs={{0,24},{4,28},{8,16},{12,20},{16,8},{20,12},{24,0},{28,4},{1,25},{... | collective-permute-start | bytes 110600 | tf_op jit(solution)/shard_map/ppermute | solution.py:342
  37.5 4.9 %collective-permute-start.13 = (bf16[144,128]{1,0:T(8,128)(2,1)S(1)}, bf16[144,128]{1,0:T(8,128)(2,1)S(1)}, u32[]{:S(2)}, u32[]{:S(2)}) collective-permute-start(bf16[144,128]{1,0:T(8,128)(2,1)S(1)} %get-tuple-element.43), channel_id=1, source_target_pairs={{0,16},{4,20},{8,24},{12,28},{16,0},{20,4},{24,8},{28,12},{1,17},{... | collective-permute-start | bytes 110600 | tf_op jit(solution)/shard_map/ppermute | solution.py:342
  37.6 4.9 %collective-permute-start.14 = (bf16[144,128]{1,0:T(8,128)(2,1)S(1)}, bf16[144,128]{1,0:T(8,128)(2,1)S(1)}, u32[]{:S(2)}, u32[]{:S(2)}) collective-permute-start(bf16[144,128]{1,0:T(8,128)(2,1)S(1)} %get-tuple-element.44), channel_id=1, source_target_pairs={{0,8},{4,12},{8,0},{12,4},{16,24},{20,28},{24,16},{28,20},{1,9},{5... | collective-permute-start | bytes 110600 | tf_op jit(solution)/shard_map/ppermute | solution.py:342
  45.4 3.9 %collective-permute-start.15 = (bf16[4,4,896]{2,1,0:T(4,128)(2,1)S(1)}, bf16[4,4,896]{2,1,0:T(4,128)(2,1)S(1)}, u32[]{:S(2)}, u32[]{:S(2)}) collective-permute-start(bf16[4,4,896]{2,1,0:T(4,128)(2,1)S(1)} %get-tuple-element.46), channel_id=1, source_target_pairs={{0,8},{4,12},{8,0},{12,4},{16,24},{20,28},{24,16},{28,20},{1,9},{5... | collective-permute-start | bytes 86024 | tf_op jit(solution)/shard_map/ppermute | solution.py:342
  49.3 5.5 %collective-permute-start.16 = (bf16[4,896]{1,0:T(4,128)(2,1)S(1)}, bf16[4,896]{1,0:T(4,128)(2,1)S(1)}, u32[]{:S(2)}, u32[]{:S(2)}) collective-permute-start(bf16[4,896]{1,0:T(4,128)(2,1)S(1)} %get-tuple-element.48), channel_id=1, source_target_pairs={{0,20},{4,16},{8,28},{12,24},{16,4},{20,0},{24,12},{28,8},{1,21},{... | collective-permute-start | bytes 21512 | tf_op jit(solution)/shard_map/ppermute | solution.py:342
  51.7 4.5 %collective-permute-start.17 = (bf16[4,896]{1,0:T(4,128)(2,1)S(1)}, bf16[4,896]{1,0:T(4,128)(2,1)S(1)}, u32[]{:S(2)}, u32[]{:S(2)}) collective-permute-start(bf16[4,896]{1,0:T(4,128)(2,1)S(1)} %get-tuple-element.49), channel_id=1, source_target_pairs={{0,16},{4,20},{8,24},{12,28},{16,0},{20,4},{24,8},{28,12},{1,17},{... | collective-permute-start | bytes 21512 | tf_op jit(solution)/shard_map/ppermute | solution.py:342
  52.5 3.8 %collective-permute-start.18 = (bf16[4,896]{1,0:T(4,128)(2,1)S(1)}, bf16[4,896]{1,0:T(4,128)(2,1)S(1)}, u32[]{:S(2)}, u32[]{:S(2)}) collective-permute-start(bf16[4,896]{1,0:T(4,128)(2,1)S(1)} %get-tuple-element.50), channel_id=1, source_target_pairs={{0,4},{4,0},{8,12},{12,8},{16,20},{20,16},{24,28},{28,24},{1,5},{5... | collective-permute-start | bytes 21512 | tf_op jit(solution)/shard_map/ppermute | solution.py:342

commit v5 on v4

--- a/solution.py
+++ b/solution.py
@@ -277,14 +277,14 @@
 
 def project(values, weight_ref, out_ref, far):
     blocks, tokens, width = out_ref.shape
-    bit = lax.rem(lax.axis_index("ctx") // 2, 2)
-    first = (1 - bit if far else bit) * (2 * width)
+    bit = lax.axis_index("ctx") // blocks
+    first = (1 - bit if far else bit) * (blocks * width)
 
     @pl.loop(0, blocks // 2)
     def _(k):
         result = jnp.dot(
             values[...].astype(jnp.bfloat16),
-            weight_ref[:, pl.ds(pl.multiple_of(first + k * (4 * width), LANES), 2 * width)],
+            weight_ref[:, pl.ds(pl.multiple_of(first + k * (2 * width), LANES), 2 * width)],
             preferred_element_type=jnp.float32,
         )
         out_ref[2 * k] = result[:tokens, :width].astype(out_ref.dtype)
@@ -296,8 +296,7 @@
 
 
 def add_kernel(own_ref, other_ref, kept_ref, *sent_refs):
-    me = lax.axis_index("ctx")
-    own = (me // 4) * 2 + lax.rem(me, 2)
+    own = lax.rem(lax.axis_index("ctx"), own_ref.shape[0])
     for k, out_ref in enumerate((kept_ref,) + sent_refs):
         block = own_ref[own ^ k] + other_ref[own ^ k].astype(jnp.float32)
         out_ref[...] = block.astype(out_ref.dtype)
@@ -429,13 +428,13 @@
         + [jax.ShapeDtypeStruct(block, jnp.bfloat16)] * 3,
         compiler_params=small,
         name="add_columns",
-    )(near, swap(far, 2))
+    )(near, swap(far, 4))
     return pl.pallas_call(
         sum_kernel,
         out_shape=jax.ShapeDtypeStruct((requests, query_len, width), jnp.bfloat16),
         compiler_params=small,
         name="sum_output",
-    )(kept, *(swap(part, bits) for part, bits in reversed([*zip(sent, (1, 4, 5))])))
+    )(kept, *(swap(part, bits) for part, bits in reversed([*zip(sent, (1, 2, 3))])))
 
 
 def plain_device(

time: 57 us -> 57.1 us (level)
  starting transfers between devices: 26.1 us -> 27 us
  waiting for transfers between devices: 13.2 us -> 12.4 us
    ppermute x19, starting transfers between devices: 26.1 us -> 27 us  [per_device(): lax.ppermute(value, 'ctx', [(i, i ^ bits) for i in range(ctx)])]
    ppermute x19, waiting for transfers between devices: 13.2 us -> 12.4 us  [per_device(): lax.ppermute(value, 'ctx', [(i, i ^ bits) for i in range(ctx)])]
where the time goes in v5:
time: 57.1 us; the launch traced here: 57 us
  starting transfers between devices  27 us (47%)
  Pallas kernels  17.3 us (30%)
  waiting for transfers between devices  12.4 us (22%)
    ppermute x19, starting transfers between devices, per_device(): lax.ppermute(value, 'ctx', [(i, i ^ bits) for i in range(ctx)])  27 us
    ppermute x19, waiting for transfers between devices, per_device(): lax.ppermute(value, 'ctx', [(i, i ^ bits) for i in range(ctx)])  12.4 us
    pallas_call x2, Pallas kernels, per_device(): pl.pallas_call(functools.partial(attention_kernel, ctx=ctx, b=b), in_spec...  8.66 us
    pallas_call x1, Pallas kernels, per_device(): pl.pallas_call(output_kernel, out_shape=[jax.ShapeDtypeStruct((line, toke...  2.87 us
    pallas_call x1, Pallas kernels, per_device(): pl.pallas_call(near_kernel, out_shape=jax.ShapeDtypeStruct((line, tokens,...  2.14 us
    pallas_call x1, Pallas kernels, per_device(): pl.pallas_call(query_kernel, in_specs=[pl.BlockSpec(memory_space=pl.ANY)]...  1.8 us
  transfers between devices with their start and end apart: 19, of which 8 were waited for; matrix products, arithmetic and copies ran while one was open for 0% of the time, Pallas kernels for 14%

profile of v5, /device:TPU:0, one launch (start us, length us, event | category | flops | bytes accessed | tf_op | source)
XLA Modules:
  0.0 57.0 jit_solution(1599489494882007452)
XLA Ops:
  0.0 1.8 %latent_query.1 = (bf16[288,128]{1,0:T(8,128)(2,1)S(1)}, bf16[288,128]{1,0:T(8,128)(2,1)S(1)}) custom-call(bf16[64,192]{1,0:T(8,128)(2,1)} %bitcast.8, bf16[16,128,512]{2,1,0:T(8,128)(2,1)} %absorb_hbm.1), custom_call_target="tpu_custom_call" | custom-call | tf_op jit(solution)/shard_map/latent_query/pallas_call | solution.py:342
  1.8 3.1 %collective-permute-start = (bf16[288,128]{1,0:T(8,128)(2,1)S(1)}, bf16[288,128]{1,0:T(8,128)(2,1)S(1)}, u32[]{:S(2)}, u32[]{:S(2)}) collective-permute-start(bf16[288,128]{1,0:T(8,128)(2,1)S(1)} %get-tuple-element.28.refs_0_), channel_id=1, source_target_pairs={{0,8},{4,12},{8,0},{12,4},{16,24},{20,28},{24,16},{28,20},{1,9},{5... | collective-permute-start | bytes 221192 | tf_op jit(solution)/shard_map/ppermute | solution.py:341
  4.9 2.6 %collective-permute-start.1 = (bf16[288,128]{1,0:T(8,128)(2,1)S(1)}, bf16[288,128]{1,0:T(8,128)(2,1)S(1)}, u32[]{:S(2)}, u32[]{:S(2)}) collective-permute-start(bf16[288,128]{1,0:T(8,128)(2,1)S(1)} %get-tuple-element.28.refs_0_), channel_id=1, source_target_pairs={{0,16},{4,20},{8,24},{12,28},{16,0},{20,4},{24,8},{28,12},{1,17},{... | collective-permute-start | bytes 221192 | tf_op jit(solution)/shard_map/ppermute | solution.py:341
  7.5 0.0 collective-permute-start.2
  7.5 1.0 %head_columns.1 = (f32[8,16,128]{2,1,0:T(8,128)S(1)}, f32[8,16,128]{2,1,0:T(8,128)S(1)}, bf16[288,128]{1,0:T(8,128)(2,1)S(1)}) custom-call(f32[1,128]{1,0:T(1,128)} %bitcast.9, f32[1,128]{1,0:T(1,128)} %bitcast.10, bf16[288,128]{1,0:T(8,128)(2,1)S(1)} %get-tuple-element.29.through_ref), custom_call_target="tpu_custom_call", output_to_operand_aliasing={{2}: (2, {})} | custom-call | flops 99999997952 | bytes 1048576 | tf_op jit(solution)/shard_map/head_columns/pallas_call | solution.py:355
  8.5 1.8 %collective-permute-start.3 = (bf16[288,128]{1,0:T(8,128)(2,1)S(1)}, bf16[288,128]{1,0:T(8,128)(2,1)S(1)}, u32[]{:S(2)}, u32[]{:S(2)}) collective-permute-start(bf16[288,128]{1,0:T(8,128)(2,1)S(1)} %get-tuple-element.30), channel_id=1, source_target_pairs={{0,4},{4,0},{8,12},{12,8},{16,20},{20,16},{24,28},{28,24},{1,5},{5... | collective-permute-start | bytes 221192 | tf_op jit(solution)/shard_map/ppermute | solution.py:341
  10.2 0.0 collective-permute-done.refs_1_
  10.2 0.3 collective-permute-start.4
  10.5 2.1 %collective-permute-done.1.refs_2_ = bf16[288,128]{1,0:T(8,128)(2,1)S(1)} collective-permute-done((bf16[288,128]{1,0:T(8,128)(2,1)S(1)}, bf16[288,128]{1,0:T(8,128)(2,1)S(1)}, u32[]{:S(2)}, u32[]{:S(2)}) %collective-permute-start.1) | collective-permute-done | bytes 73760 | tf_op jit(solution)/shard_map/ppermute | solution.py:341
  12.7 1.5 %collective-permute-start.5 = (bf16[288,128]{1,0:T(8,128)(2,1)S(1)}, bf16[288,128]{1,0:T(8,128)(2,1)S(1)}, u32[]{:S(2)}, u32[]{:S(2)}) collective-permute-start(bf16[288,128]{1,0:T(8,128)(2,1)S(1)} %collective-permute-done.1.refs_2_), channel_id=1, source_target_pairs={{0,4},{4,0},{8,12},{12,8},{16,20},{20,16},{24,28},{28,24},{1,5},{5... | collective-permute-start | bytes 221192 | tf_op jit(solution)/shard_map/ppermute | solution.py:341
  14.2 0.0 collective-permute-done.2.refs_3_
  14.2 1.1 %collective-permute-start.6 = (bf16[288,128]{1,0:T(8,128)(2,1)S(1)}, bf16[288,128]{1,0:T(8,128)(2,1)S(1)}, u32[]{:S(2)}, u32[]{:S(2)}) collective-permute-start(bf16[288,128]{1,0:T(8,128)(2,1)S(1)} %collective-permute-done.2.refs_3_), channel_id=1, source_target_pairs={{0,4},{4,0},{8,12},{12,8},{16,20},{20,16},{24,28},{28,24},{1,5},{5... | collective-permute-start | bytes 221192 | tf_op jit(solution)/shard_map/ppermute | solution.py:341
  15.2 0.0 collective-permute-done.3.refs_4_
  15.2 0.0 collective-permute-done.4.refs_5_
  15.2 1.8 %collective-permute-done.5.refs_6_ = bf16[288,128]{1,0:T(8,128)(2,1)S(1)} collective-permute-done((bf16[288,128]{1,0:T(8,128)(2,1)S(1)}, bf16[288,128]{1,0:T(8,128)(2,1)S(1)}, u32[]{:S(2)}, u32[]{:S(2)}) %collective-permute-start.5) | collective-permute-done | bytes 73760 | tf_op jit(solution)/shard_map/ppermute | solution.py:341
  17.0 1.5 %collective-permute-done.6.refs_7_ = bf16[288,128]{1,0:T(8,128)(2,1)S(1)} collective-permute-done((bf16[288,128]{1,0:T(8,128)(2,1)S(1)}, bf16[288,128]{1,0:T(8,128)(2,1)S(1)}, u32[]{:S(2)}, u32[]{:S(2)}) %collective-permute-start.6) | collective-permute-done | bytes 73760 | tf_op jit(solution)/shard_map/ppermute | solution.py:341
  18.5 4.3 %attention.2 = (bf16[4,144,128]{2,1,0:T(8,128)(2,1)S(1)}, bf16[4,144,128]{2,1,0:T(8,128)(2,1)S(1)}) custom-call(s32[2,32]{1,0:T(2,128)} %pages_ref.3, s32[2]{0:T(128)} %lengths_ref.3, bf16[288,128]{1,0:T(8,128)(2,1)S(1)} %get-tuple-element.28.refs_0_, bf16[288,128]{1,0:T(8,128)(2,1)S(1)} %collective-permute-done.refs_1_, ...), custom_call_target="tpu_custom_call" | custom-call | flops 20000000000 | bytes 1048576 | tf_op jit(solution)/shard_map/attention/pallas_call | solution.py:378
  22.8 0.0 slice-start
  22.8 0.0 slice-start.1
  22.8 0.0 slice-start.2
  22.8 0.0 slice-start.3
  22.9 0.0 slice-start.5
  22.9 0.0 copy-start.1
  22.9 1.1 %collective-permute-start.7 = (bf16[4,144,128]{2,1,0:T(8,128)(2,1)S(1)}, bf16[4,144,128]{2,1,0:T(8,128)(2,1)S(1)}, u32[]{:S(2)}, u32[]{:S(2)}) collective-permute-start(bf16[4,144,128]{2,1,0:T(8,128)(2,1)S(1)} %get-tuple-element.34), channel_id=1, source_target_pairs={{0,4},{4,0},{8,12},{12,8},{16,20},{20,16},{24,28},{28,24},{1,5},{5... | collective-permute-start | bytes 442376 | tf_op jit(solution)/shard_map/ppermute | solution.py:341
  24.0 4.4 %attention.3 = (bf16[4,144,128]{2,1,0:T(8,128)(2,1)S(1)}, bf16[4,144,128]{2,1,0:T(8,128)(2,1)S(1)}) custom-call(s32[2,32]{1,0:T(2,128)} %pages_ref.3, s32[2]{0:T(128)} %lengths_ref.3, bf16[288,128]{1,0:T(8,128)(2,1)S(1)} %get-tuple-element.28.refs_0_, bf16[288,128]{1,0:T(8,128)(2,1)S(1)} %collective-permute-done.refs_1_, ...), custom_call_target="tpu_custom_call" | custom-call | flops 20000000000 | bytes 1048576 | tf_op jit(solution)/shard_map/attention/pallas_call | solution.py:378
  28.4 1.0 %collective-permute-start.11 = (bf16[4,144,128]{2,1,0:T(8,128)(2,1)S(1)}, bf16[4,144,128]{2,1,0:T(8,128)(2,1)S(1)}, u32[]{:S(2)}, u32[]{:S(2)}) collective-permute-start(bf16[4,144,128]{2,1,0:T(8,128)(2,1)S(1)} %get-tuple-element.40), channel_id=1, source_target_pairs={{0,4},{4,0},{8,12},{12,8},{16,20},{20,16},{24,28},{28,24},{1,5},{5... | collective-permute-start | bytes 442376 | tf_op jit(solution)/shard_map/ppermute | solution.py:341
  29.4 0.0 collective-permute-done.7.other_ref
  29.5 0.1 merge.2
  29.6 3.3 %collective-permute-start.8 = (bf16[144,128]{1,0:T(8,128)(2,1)S(1)}, bf16[144,128]{1,0:T(8,128)(2,1)S(1)}, u32[]{:S(2)}, u32[]{:S(2)}) collective-permute-start(bf16[144,128]{1,0:T(8,128)(2,1)S(1)} %get-tuple-element.36), channel_id=1, source_target_pairs={{0,24},{4,28},{8,16},{12,20},{16,8},{20,12},{24,0},{28,4},{1,25},{... | collective-permute-start | bytes 110600 | tf_op jit(solution)/shard_map/ppermute | solution.py:341
  32.9 0.0 collective-permute-start.9
  32.9 1.1 %collective-permute-start.10 = (bf16[144,128]{1,0:T(8,128)(2,1)S(1)}, bf16[144,128]{1,0:T(8,128)(2,1)S(1)}, u32[]{:S(2)}, u32[]{:S(2)}) collective-permute-start(bf16[144,128]{1,0:T(8,128)(2,1)S(1)} %get-tuple-element.38), channel_id=1, source_target_pairs={{0,8},{4,12},{8,0},{12,4},{16,24},{20,28},{24,16},{28,20},{1,9},{5... | collective-permute-start | bytes 110600 | tf_op jit(solution)/shard_map/ppermute | solution.py:341
  34.1 0.1 merge.3
  34.2 3.3 %collective-permute-start.12 = (bf16[144,128]{1,0:T(8,128)(2,1)S(1)}, bf16[144,128]{1,0:T(8,128)(2,1)S(1)}, u32[]{:S(2)}, u32[]{:S(2)}) collective-permute-start(bf16[144,128]{1,0:T(8,128)(2,1)S(1)} %get-tuple-element.42), channel_id=1, source_target_pairs={{0,24},{4,28},{8,16},{12,20},{16,8},{20,12},{24,0},{28,4},{1,25},{... | collective-permute-start | bytes 110600 | tf_op jit(solution)/shard_map/ppermute | solution.py:341
  37.6 1.1 %collective-permute-start.14 = (bf16[144,128]{1,0:T(8,128)(2,1)S(1)}, bf16[144,128]{1,0:T(8,128)(2,1)S(1)}, u32[]{:S(2)}, u32[]{:S(2)}) collective-permute-start(bf16[144,128]{1,0:T(8,128)(2,1)S(1)} %get-tuple-element.44), channel_id=1, source_target_pairs={{0,8},{4,12},{8,0},{12,4},{16,24},{20,28},{24,16},{28,20},{1,9},{5... | collective-permute-start | bytes 110600 | tf_op jit(solution)/shard_map/ppermute | solution.py:341
  38.7 0.0 collective-permute-done.9.refs_2_
  38.7 0.0 collective-permute-done.10.refs_3_
  38.7 1.4 %collective-permute-done.12.refs_5_ = bf16[144,128]{1,0:T(8,128)(2,1)S(1)} collective-permute-done((bf16[144,128]{1,0:T(8,128)(2,1)S(1)}, bf16[144,128]{1,0:T(8,128)(2,1)S(1)}, u32[]{:S(2)}, u32[]{:S(2)}) %collective-permute-start.12) | collective-permute-done | bytes 36896 | tf_op jit(solution)/shard_map/ppermute | solution.py:341
  40.0 2.4 %collective-permute-done.13.refs_6_ = bf16[144,128]{1,0:T(8,128)(2,1)S(1)} collective-permute-done((bf16[144,128]{1,0:T(8,128)(2,1)S(1)}, bf16[144,128]{1,0:T(8,128)(2,1)S(1)}, u32[]{:S(2)}, u32[]{:S(2)}) %collective-permute-start.13) | collective-permute-done | bytes 36896 | tf_op jit(solution)/shard_map/ppermute | solution.py:341
  42.5 2.9 %up_and_far_output.1 = (bf16[4,4,896]{2,1,0:T(4,128)(2,1)S(1)}, f32[8,2048]{1,0:T(8,128)S(1)}) custom-call(bf16[144,128]{1,0:T(8,128)(2,1)S(1)} %get-tuple-element.35.refs_0_, bf16[144,128]{1,0:T(8,128)(2,1)S(1)} %collective-permute-done.8.refs_1_, bf16[144,128]{1,0:T(8,128)(2,1)S(1)} %collective-permute-done.9.refs_2_, ...), custom_call_target="tpu_custom_call" | custom-call | flops 20000000000 | bytes 1048576 | tf_op jit(solution)/shard_map/up_and_far_output/pallas_call | solution.py:406
  45.4 2.0 %collective-permute-start.15 = (bf16[4,4,896]{2,1,0:T(4,128)(2,1)S(1)}, bf16[4,4,896]{2,1,0:T(4,128)(2,1)S(1)}, u32[]{:S(2)}, u32[]{:S(2)}) collective-permute-start(bf16[4,4,896]{2,1,0:T(4,128)(2,1)S(1)} %get-tuple-element.46), channel_id=1, source_target_pairs={{0,16},{4,20},{8,24},{12,28},{16,0},{20,4},{24,8},{28,12},{1,17},{... | collective-permute-start | bytes 86024 | tf_op jit(solution)/shard_map/ppermute | solution.py:341
  47.4 2.1 %near_output.1.own_ref = f32[4,4,896]{2,1,0:T(4,128)S(1)} custom-call(f32[8,2048]{1,0:T(8,128)S(1)} %get-tuple-element.45.values, bf16[2048,7168]{1,0:T(8,128)(2,1)S(1)} %bitcast.5), custom_call_target="tpu_custom_call" | custom-call | flops 20000000000 | bytes 1048576 | tf_op jit(solution)/shard_map/near_output/pallas_call | solution.py:417
  49.5 0.6 %collective-permute-done.15.other_ref = bf16[4,4,896]{2,1,0:T(4,128)(2,1)S(1)} collective-permute-done((bf16[4,4,896]{2,1,0:T(4,128)(2,1)S(1)}, bf16[4,4,896]{2,1,0:T(4,128)(2,1)S(1)}, u32[]{:S(2)}, u32[]{:S(2)}) %collective-permute-start.15) | collective-permute-done | bytes 28704 | tf_op jit(solution)/shard_map/ppermute | solution.py:341
  50.2 0.8 %collective-permute-start.16 = (bf16[4,896]{1,0:T(4,128)(2,1)S(1)}, bf16[4,896]{1,0:T(4,128)(2,1)S(1)}, u32[]{:S(2)}, u32[]{:S(2)}) collective-permute-start(bf16[4,896]{1,0:T(4,128)(2,1)S(1)} %get-tuple-element.48), channel_id=1, source_target_pairs={{0,12},{4,8},{8,4},{12,0},{16,28},{20,24},{24,20},{28,16},{1,13},{... | collective-permute-start | bytes 21512 | tf_op jit(solution)/shard_map/ppermute | solution.py:341
  51.0 1.7 %collective-permute-start.17 = (bf16[4,896]{1,0:T(4,128)(2,1)S(1)}, bf16[4,896]{1,0:T(4,128)(2,1)S(1)}, u32[]{:S(2)}, u32[]{:S(2)}) collective-permute-start(bf16[4,896]{1,0:T(4,128)(2,1)S(1)} %get-tuple-element.49), channel_id=1, source_target_pairs={{0,8},{4,12},{8,0},{12,4},{16,24},{20,28},{24,16},{28,20},{1,9},{5... | collective-permute-start | bytes 21512 | tf_op jit(solution)/shard_map/ppermute | solution.py:341
  52.7 1.0 %collective-permute-start.18 = (bf16[4,896]{1,0:T(4,128)(2,1)S(1)}, bf16[4,896]{1,0:T(4,128)(2,1)S(1)}, u32[]{:S(2)}, u32[]{:S(2)}) collective-permute-start(bf16[4,896]{1,0:T(4,128)(2,1)S(1)} %get-tuple-element.50), channel_id=1, source_target_pairs={{0,4},{4,0},{8,12},{12,8},{16,20},{20,16},{24,28},{28,24},{1,5},{5... | collective-permute-start | bytes 21512 | tf_op jit(solution)/shard_map/ppermute | solution.py:341
  53.7 1.0 %collective-permute-done.16.refs_0_ = bf16[4,896]{1,0:T(4,128)(2,1)S(1)} collective-permute-done((bf16[4,896]{1,0:T(4,128)(2,1)S(1)}, bf16[4,896]{1,0:T(4,128)(2,1)S(1)}, u32[]{:S(2)}, u32[]{:S(2)}) %collective-permute-start.16) | collective-permute-done | bytes 7200 | tf_op jit(solution)/shard_map/ppermute | solution.py:341
  54.8 1.6 %collective-permute-done.18.refs_2_ = bf16[4,896]{1,0:T(4,128)(2,1)S(1)} collective-permute-done((bf16[4,896]{1,0:T(4,128)(2,1)S(1)}, bf16[4,896]{1,0:T(4,128)(2,1)S(1)}, u32[]{:S(2)}, u32[]{:S(2)}) %collective-permute-start.18) | collective-permute-done | bytes 7200 | tf_op jit(solution)/shard_map/ppermute | solution.py:341
  56.3 0.6 %sum_output.1 = bf16[2,2,896]{2,1,0:T(2,128)(2,1)} custom-call(f32[4,896]{1,0:T(4,128)S(1)} %get-tuple-element.47.own_ref, bf16[4,896]{1,0:T(4,128)(2,1)S(1)} %collective-permute-done.16.refs_0_, bf16[4,896]{1,0:T(4,128)(2,1)S(1)} %collective-permute-done.17.refs_1_, bf16[4,896]{1,0:T(4,128)(2,1)S(1)} %collective-permute-done.18.refs_2_), custom_call_target="tpu_custom_call" | custom-call | tf_op jit(solution)/shard_map/sum_output/pallas_call | solution.py:432
  (19 shorter events, 0.1 us)
Async XLA Ops:
  1.8 8.4 %collective-permute-start = (bf16[288,128]{1,0:T(8,128)(2,1)S(1)}, bf16[288,128]{1,0:T(8,128)(2,1)S(1)}, u32[]{:S(2)}, u32[]{:S(2)}) collective-permute-start(bf16[288,128]{1,0:T(8,128)(2,1)S(1)} %get-tuple-element.28.refs_0_), channel_id=1, source_target_pairs={{0,8},{4,12},{8,0},{12,4},{16,24},{20,28},{24,16},{28,20},{1,9},{5... | collective-permute-start | bytes 221192 | tf_op jit(solution)/shard_map/ppermute | solution.py:341
  4.9 7.8 %collective-permute-start.1 = (bf16[288,128]{1,0:T(8,128)(2,1)S(1)}, bf16[288,128]{1,0:T(8,128)(2,1)S(1)}, u32[]{:S(2)}, u32[]{:S(2)}) collective-permute-start(bf16[288,128]{1,0:T(8,128)(2,1)S(1)} %get-tuple-element.28.refs_0_), channel_id=1, source_target_pairs={{0,16},{4,20},{8,24},{12,28},{16,0},{20,4},{24,8},{28,12},{1,17},{... | collective-permute-start | bytes 221192 | tf_op jit(solution)/shard_map/ppermute | solution.py:341
  7.5 6.7 %collective-permute-start.2 = (bf16[288,128]{1,0:T(8,128)(2,1)S(1)}, bf16[288,128]{1,0:T(8,128)(2,1)S(1)}, u32[]{:S(2)}, u32[]{:S(2)}) collective-permute-start(bf16[288,128]{1,0:T(8,128)(2,1)S(1)} %get-tuple-element.28.refs_0_), channel_id=1, source_target_pairs={{0,24},{4,28},{8,16},{12,20},{16,8},{20,12},{24,0},{28,4},{1,25},{... | collective-permute-start | bytes 221192 | tf_op jit(solution)/shard_map/ppermute | solution.py:341
  7.5 11.0 %copy-start = (bf16[2,4096,576]{1,2,0:T(8,128)(2,1)S(1)}, bf16[2,4096,576]{1,2,0:T(8,128)(2,1)}, u32[]{:S(2)}) copy-start(bf16[2,4096,576]{1,2,0:T(8,128)(2,1)} %param.11) | copy-start | bytes 28311556
  8.5 6.8 %collective-permute-start.3 = (bf16[288,128]{1,0:T(8,128)(2,1)S(1)}, bf16[288,128]{1,0:T(8,128)(2,1)S(1)}, u32[]{:S(2)}, u32[]{:S(2)}) collective-permute-start(bf16[288,128]{1,0:T(8,128)(2,1)S(1)} %get-tuple-element.30), channel_id=1, source_target_pairs={{0,4},{4,0},{8,12},{12,8},{16,20},{20,16},{24,28},{28,24},{1,5},{5... | collective-permute-start | bytes 221192 | tf_op jit(solution)/shard_map/ppermute | solution.py:341
  10.2 5.0 %collective-permute-start.4 = (bf16[288,128]{1,0:T(8,128)(2,1)S(1)}, bf16[288,128]{1,0:T(8,128)(2,1)S(1)}, u32[]{:S(2)}, u32[]{:S(2)}) collective-permute-start(bf16[288,128]{1,0:T(8,128)(2,1)S(1)} %collective-permute-done.refs_1_), channel_id=1, source_target_pairs={{0,4},{4,0},{8,12},{12,8},{16,20},{20,16},{24,28},{28,24},{1,5},{5... | collective-permute-start | bytes 221192 | tf_op jit(solution)/shard_map/ppermute | solution.py:341
  12.7 4.4 %collective-permute-start.5 = (bf16[288,128]{1,0:T(8,128)(2,1)S(1)}, bf16[288,128]{1,0:T(8,128)(2,1)S(1)}, u32[]{:S(2)}, u32[]{:S(2)}) collective-permute-start(bf16[288,128]{1,0:T(8,128)(2,1)S(1)} %collective-permute-done.1.refs_2_), channel_id=1, source_target_pairs={{0,4},{4,0},{8,12},{12,8},{16,20},{20,16},{24,28},{28,24},{1,5},{5... | collective-permute-start | bytes 221192 | tf_op jit(solution)/shard_map/ppermute | solution.py:341
  14.2 4.4 %collective-permute-start.6 = (bf16[288,128]{1,0:T(8,128)(2,1)S(1)}, bf16[288,128]{1,0:T(8,128)(2,1)S(1)}, u32[]{:S(2)}, u32[]{:S(2)}) collective-permute-start(bf16[288,128]{1,0:T(8,128)(2,1)S(1)} %collective-permute-done.2.refs_3_), channel_id=1, source_target_pairs={{0,4},{4,0},{8,12},{12,8},{16,20},{20,16},{24,28},{28,24},{1,5},{5... | collective-permute-start | bytes 221192 | tf_op jit(solution)/shard_map/ppermute | solution.py:341
  22.8 19.6 %slice-start = ((s8[29360128]{0:T(1024)(128)(4,1)}), s8[4194304]{0:T(1024)(128)(4,1)S(1)}, s32[]{:S(2)}) async-start(s8[29360128]{0:T(1024)(128)(4,1)} %bitcast.4), calls=%async_computation | async-start | bytes 8388608
  22.8 19.6 %slice-start.1 = ((s8[29360128]{0:T(1024)(128)(4,1)}), s8[4194304]{0:T(1024)(128)(4,1)S(1)}, s32[]{:S(2)}) async-start(s8[29360128]{0:T(1024)(128)(4,1)} %bitcast.4), calls=%async_computation.1 | async-start | bytes 8388608
  22.8 19.6 %slice-start.2 = ((s8[29360128]{0:T(1024)(128)(4,1)}), s8[4194304]{0:T(1024)(128)(4,1)S(1)}, s32[]{:S(2)}) async-start(s8[29360128]{0:T(1024)(128)(4,1)} %bitcast.4), calls=%async_computation.2 | async-start | bytes 8388608
  22.8 19.6 %slice-start.3 = ((s8[29360128]{0:T(1024)(128)(4,1)}), s8[4194304]{0:T(1024)(128)(4,1)S(1)}, s32[]{:S(2)}) async-start(s8[29360128]{0:T(1024)(128)(4,1)} %bitcast.4), calls=%async_computation.3 | async-start | bytes 8388608
  22.8 19.6 %slice-start.4 = ((s8[29360128]{0:T(1024)(128)(4,1)}), s8[4194304]{0:T(1024)(128)(4,1)S(1)}, s32[]{:S(2)}) async-start(s8[29360128]{0:T(1024)(128)(4,1)} %bitcast.4), calls=%async_computation.4 | async-start | bytes 8388608
  22.9 19.6 %slice-start.5 = ((s8[29360128]{0:T(1024)(128)(4,1)}), s8[4194304]{0:T(1024)(128)(4,1)S(1)}, s32[]{:S(2)}) async-start(s8[29360128]{0:T(1024)(128)(4,1)} %bitcast.4), calls=%async_computation.5 | async-start | bytes 8388608
  22.9 19.6 %slice-start.6 = ((s8[29360128]{0:T(1024)(128)(4,1)}), s8[4194304]{0:T(1024)(128)(4,1)S(1)}, s32[]{:S(2)}) async-start(s8[29360128]{0:T(1024)(128)(4,1)} %bitcast.4), calls=%async_computation.6 | async-start | bytes 8388608
  22.9 19.6 %copy-start.1 = (bf16[16,512,128]{2,1,0:T(8,128)(2,1)S(1)}, bf16[16,512,128]{2,1,0:T(8,128)(2,1)}, u32[]{:S(2)}) copy-start(bf16[16,512,128]{2,1,0:T(8,128)(2,1)} %refs_8_.1) | copy-start | bytes 6291460
  22.9 6.6 %collective-permute-start.7 = (bf16[4,144,128]{2,1,0:T(8,128)(2,1)S(1)}, bf16[4,144,128]{2,1,0:T(8,128)(2,1)S(1)}, u32[]{:S(2)}, u32[]{:S(2)}) collective-permute-start(bf16[4,144,128]{2,1,0:T(8,128)(2,1)S(1)} %get-tuple-element.34), channel_id=1, source_target_pairs={{0,4},{4,0},{8,12},{12,8},{16,20},{20,16},{24,28},{28,24},{1,5},{5... | collective-permute-start | bytes 442376 | tf_op jit(solution)/shard_map/ppermute | solution.py:341
  28.4 5.7 %collective-permute-start.11 = (bf16[4,144,128]{2,1,0:T(8,128)(2,1)S(1)}, bf16[4,144,128]{2,1,0:T(8,128)(2,1)S(1)}, u32[]{:S(2)}, u32[]{:S(2)}) collective-permute-start(bf16[4,144,128]{2,1,0:T(8,128)(2,1)S(1)} %get-tuple-element.40), channel_id=1, source_target_pairs={{0,4},{4,0},{8,12},{12,8},{16,20},{20,16},{24,28},{28,24},{1,5},{5... | collective-permute-start | bytes 442376 | tf_op jit(solution)/shard_map/ppermute | solution.py:341
  29.6 7.9 %collective-permute-start.8 = (bf16[144,128]{1,0:T(8,128)(2,1)S(1)}, bf16[144,128]{1,0:T(8,128)(2,1)S(1)}, u32[]{:S(2)}, u32[]{:S(2)}) collective-permute-start(bf16[144,128]{1,0:T(8,128)(2,1)S(1)} %get-tuple-element.36), channel_id=1, source_target_pairs={{0,24},{4,28},{8,16},{12,20},{16,8},{20,12},{24,0},{28,4},{1,25},{... | collective-permute-start | bytes 110600 | tf_op jit(solution)/shard_map/ppermute | solution.py:341
  32.9 5.7 %collective-permute-start.9 = (bf16[144,128]{1,0:T(8,128)(2,1)S(1)}, bf16[144,128]{1,0:T(8,128)(2,1)S(1)}, u32[]{:S(2)}, u32[]{:S(2)}) collective-permute-start(bf16[144,128]{1,0:T(8,128)(2,1)S(1)} %get-tuple-element.37), channel_id=1, source_target_pairs={{0,16},{4,20},{8,24},{12,28},{16,0},{20,4},{24,8},{28,12},{1,17},{... | collective-permute-start | bytes 110600 | tf_op jit(solution)/shard_map/ppermute | solution.py:341
  32.9 5.7 %collective-permute-start.10 = (bf16[144,128]{1,0:T(8,128)(2,1)S(1)}, bf16[144,128]{1,0:T(8,128)(2,1)S(1)}, u32[]{:S(2)}, u32[]{:S(2)}) collective-permute-start(bf16[144,128]{1,0:T(8,128)(2,1)S(1)} %get-tuple-element.38), channel_id=1, source_target_pairs={{0,8},{4,12},{8,0},{12,4},{16,24},{20,28},{24,16},{28,20},{1,9},{5... | collective-permute-start | bytes 110600 | tf_op jit(solution)/shard_map/ppermute | solution.py:341
  34.2 5.8 %collective-permute-start.12 = (bf16[144,128]{1,0:T(8,128)(2,1)S(1)}, bf16[144,128]{1,0:T(8,128)(2,1)S(1)}, u32[]{:S(2)}, u32[]{:S(2)}) collective-permute-start(bf16[144,128]{1,0:T(8,128)(2,1)S(1)} %get-tuple-element.42), channel_id=1, source_target_pairs={{0,24},{4,28},{8,16},{12,20},{16,8},{20,12},{24,0},{28,4},{1,25},{... | collective-permute-start | bytes 110600 | tf_op jit(solution)/shard_map/ppermute | solution.py:341
  37.5 4.9 %collective-permute-start.13 = (bf16[144,128]{1,0:T(8,128)(2,1)S(1)}, bf16[144,128]{1,0:T(8,128)(2,1)S(1)}, u32[]{:S(2)}, u32[]{:S(2)}) collective-permute-start(bf16[144,128]{1,0:T(8,128)(2,1)S(1)} %get-tuple-element.43), channel_id=1, source_target_pairs={{0,16},{4,20},{8,24},{12,28},{16,0},{20,4},{24,8},{28,12},{1,17},{... | collective-permute-start | bytes 110600 | tf_op jit(solution)/shard_map/ppermute | solution.py:341
  37.6 4.9 %collective-permute-start.14 = (bf16[144,128]{1,0:T(8,128)(2,1)S(1)}, bf16[144,128]{1,0:T(8,128)(2,1)S(1)}, u32[]{:S(2)}, u32[]{:S(2)}) collective-permute-start(bf16[144,128]{1,0:T(8,128)(2,1)S(1)} %get-tuple-element.44), channel_id=1, source_target_pairs={{0,8},{4,12},{8,0},{12,4},{16,24},{20,28},{24,16},{28,20},{1,9},{5... | collective-permute-start | bytes 110600 | tf_op jit(solution)/shard_map/ppermute | solution.py:341
  45.4 4.8 %collective-permute-start.15 = (bf16[4,4,896]{2,1,0:T(4,128)(2,1)S(1)}, bf16[4,4,896]{2,1,0:T(4,128)(2,1)S(1)}, u32[]{:S(2)}, u32[]{:S(2)}) collective-permute-start(bf16[4,4,896]{2,1,0:T(4,128)(2,1)S(1)} %get-tuple-element.46), channel_id=1, source_target_pairs={{0,16},{4,20},{8,24},{12,28},{16,0},{20,4},{24,8},{28,12},{1,17},{... | collective-permute-start | bytes 86024 | tf_op jit(solution)/shard_map/ppermute | solution.py:341
  50.2 4.6 %collective-permute-start.16 = (bf16[4,896]{1,0:T(4,128)(2,1)S(1)}, bf16[4,896]{1,0:T(4,128)(2,1)S(1)}, u32[]{:S(2)}, u32[]{:S(2)}) collective-permute-start(bf16[4,896]{1,0:T(4,128)(2,1)S(1)} %get-tuple-element.48), channel_id=1, source_target_pairs={{0,12},{4,8},{8,4},{12,0},{16,28},{20,24},{24,20},{28,16},{1,13},{... | collective-permute-start | bytes 21512 | tf_op jit(solution)/shard_map/ppermute | solution.py:341
  51.0 3.8 %collective-permute-start.17 = (bf16[4,896]{1,0:T(4,128)(2,1)S(1)}, bf16[4,896]{1,0:T(4,128)(2,1)S(1)}, u32[]{:S(2)}, u32[]{:S(2)}) collective-permute-start(bf16[4,896]{1,0:T(4,128)(2,1)S(1)} %get-tuple-element.49), channel_id=1, source_target_pairs={{0,8},{4,12},{8,0},{12,4},{16,24},{20,28},{24,16},{28,20},{1,9},{5... | collective-permute-start | bytes 21512 | tf_op jit(solution)/shard_map/ppermute | solution.py:341
  52.7 3.6 %collective-permute-start.18 = (bf16[4,896]{1,0:T(4,128)(2,1)S(1)}, bf16[4,896]{1,0:T(4,128)(2,1)S(1)}, u32[]{:S(2)}, u32[]{:S(2)}) collective-permute-start(bf16[4,896]{1,0:T(4,128)(2,1)S(1)} %get-tuple-element.50), channel_id=1, source_target_pairs={{0,4},{4,0},{8,12},{12,8},{16,20},{20,16},{24,28},{28,24},{1,5},{5... | collective-permute-start | bytes 21512 | tf_op jit(solution)/shard_map/ppermute | solution.py:341

commit v6 on v4

--- a/solution.py
+++ b/solution.py
@@ -366,8 +366,9 @@
         name="head_columns",
         cost_estimate=long_hint,
     )(in_hbm(kerple_rate.reshape(1, -1)), in_hbm(kerple_scale.reshape(1, -1)), again)
-    column = [packed] + [swap(packed, 2 * k) for k in range(1, line)]
-    gathered = column + [swap(value, 1) for value in [again] + column[1:]]
+    column = [swap(packed, 2 * k) for k in reversed(range(1, line))]
+    beside = [swap(value, 1) for value in column + [again]]
+    gathered = [packed] + column[::-1] + beside[::-1]
 
     cache = in_vmem(jnp.swapaxes(latent_cache, 1, 2))
     all_rows = ctx * half

time: 57 us -> 57 us (level)
  no operation moved by 1% of the time
where the time goes in v6:
time: 57 us; the launch traced here: 56.9 us
  starting transfers between devices  26.1 us (46%)
  Pallas kernels  17.3 us (30%)
  waiting for transfers between devices  13.2 us (23%)
    ppermute x19, starting transfers between devices, per_device(): lax.ppermute(value, 'ctx', [(i, i ^ bits) for i in range(ctx)])  26.1 us
    ppermute x19, waiting for transfers between devices, per_device(): lax.ppermute(value, 'ctx', [(i, i ^ bits) for i in range(ctx)])  13.2 us
    pallas_call x2, Pallas kernels, per_device(): pl.pallas_call(functools.partial(attention_kernel, ctx=ctx, b=b), in_spec...  8.66 us
    pallas_call x1, Pallas kernels, per_device(): pl.pallas_call(output_kernel, out_shape=[jax.ShapeDtypeStruct((line, toke...  2.88 us
    pallas_call x1, Pallas kernels, per_device(): pl.pallas_call(near_kernel, out_shape=jax.ShapeDtypeStruct((line, tokens,...  2.14 us
    pallas_call x1, Pallas kernels, per_device(): pl.pallas_call(query_kernel, in_specs=[pl.BlockSpec(memory_space=pl.ANY)]...  1.8 us
  transfers between devices with their start and end apart: 19, of which 8 were waited for; matrix products, arithmetic and copies ran while one was open for 0% of the time, Pallas kernels for 14%

profile of v6, /device:TPU:0, one launch (start us, length us, event | category | flops | bytes accessed | tf_op | source)
XLA Modules:
  0.0 56.9 jit_solution(7481487531652478468)
XLA Ops:
  0.0 1.8 %latent_query.1 = (bf16[288,128]{1,0:T(8,128)(2,1)S(1)}, bf16[288,128]{1,0:T(8,128)(2,1)S(1)}) custom-call(bf16[64,192]{1,0:T(8,128)(2,1)} %bitcast.8, bf16[16,128,512]{2,1,0:T(8,128)(2,1)} %absorb_hbm.1), custom_call_target="tpu_custom_call" | custom-call | tf_op jit(solution)/shard_map/latent_query/pallas_call | solution.py:343
  1.8 3.1 %collective-permute-start = (bf16[288,128]{1,0:T(8,128)(2,1)S(1)}, bf16[288,128]{1,0:T(8,128)(2,1)S(1)}, u32[]{:S(2)}, u32[]{:S(2)}) collective-permute-start(bf16[288,128]{1,0:T(8,128)(2,1)S(1)} %get-tuple-element.28.refs_0_), channel_id=1, source_target_pairs={{0,8},{4,12},{8,0},{12,4},{16,24},{20,28},{24,16},{28,20},{1,9},{5... | collective-permute-start | bytes 221192 | tf_op jit(solution)/shard_map/ppermute | solution.py:342
  4.9 2.6 %collective-permute-start.1 = (bf16[288,128]{1,0:T(8,128)(2,1)S(1)}, bf16[288,128]{1,0:T(8,128)(2,1)S(1)}, u32[]{:S(2)}, u32[]{:S(2)}) collective-permute-start(bf16[288,128]{1,0:T(8,128)(2,1)S(1)} %get-tuple-element.28.refs_0_), channel_id=1, source_target_pairs={{0,16},{4,20},{8,24},{12,28},{16,0},{20,4},{24,8},{28,12},{1,17},{... | collective-permute-start | bytes 221192 | tf_op jit(solution)/shard_map/ppermute | solution.py:342
  7.5 0.0 collective-permute-start.2
  7.5 1.0 %head_columns.1 = (f32[8,16,128]{2,1,0:T(8,128)S(1)}, f32[8,16,128]{2,1,0:T(8,128)S(1)}, bf16[288,128]{1,0:T(8,128)(2,1)S(1)}) custom-call(f32[1,128]{1,0:T(1,128)} %bitcast.9, f32[1,128]{1,0:T(1,128)} %bitcast.10, bf16[288,128]{1,0:T(8,128)(2,1)S(1)} %get-tuple-element.29.through_ref), custom_call_target="tpu_custom_call", output_to_operand_aliasing={{2}: (2, {})} | custom-call | flops 99999997952 | bytes 1048576 | tf_op jit(solution)/shard_map/head_columns/pallas_call | solution.py:356
  8.5 1.8 %collective-permute-start.3 = (bf16[288,128]{1,0:T(8,128)(2,1)S(1)}, bf16[288,128]{1,0:T(8,128)(2,1)S(1)}, u32[]{:S(2)}, u32[]{:S(2)}) collective-permute-start(bf16[288,128]{1,0:T(8,128)(2,1)S(1)} %get-tuple-element.30), channel_id=1, source_target_pairs={{0,4},{4,0},{8,12},{12,8},{16,20},{20,16},{24,28},{28,24},{1,5},{5... | collective-permute-start | bytes 221192 | tf_op jit(solution)/shard_map/ppermute | solution.py:342
  10.2 0.0 collective-permute-done.refs_1_
  10.2 0.3 collective-permute-start.4
  10.5 2.1 %collective-permute-done.1.refs_2_ = bf16[288,128]{1,0:T(8,128)(2,1)S(1)} collective-permute-done((bf16[288,128]{1,0:T(8,128)(2,1)S(1)}, bf16[288,128]{1,0:T(8,128)(2,1)S(1)}, u32[]{:S(2)}, u32[]{:S(2)}) %collective-permute-start.1) | collective-permute-done | bytes 73760 | tf_op jit(solution)/shard_map/ppermute | solution.py:342
  12.7 1.5 %collective-permute-start.5 = (bf16[288,128]{1,0:T(8,128)(2,1)S(1)}, bf16[288,128]{1,0:T(8,128)(2,1)S(1)}, u32[]{:S(2)}, u32[]{:S(2)}) collective-permute-start(bf16[288,128]{1,0:T(8,128)(2,1)S(1)} %collective-permute-done.1.refs_2_), channel_id=1, source_target_pairs={{0,4},{4,0},{8,12},{12,8},{16,20},{20,16},{24,28},{28,24},{1,5},{5... | collective-permute-start | bytes 221192 | tf_op jit(solution)/shard_map/ppermute | solution.py:342
  14.2 0.0 collective-permute-done.2.refs_3_
  14.2 1.1 %collective-permute-start.6 = (bf16[288,128]{1,0:T(8,128)(2,1)S(1)}, bf16[288,128]{1,0:T(8,128)(2,1)S(1)}, u32[]{:S(2)}, u32[]{:S(2)}) collective-permute-start(bf16[288,128]{1,0:T(8,128)(2,1)S(1)} %collective-permute-done.2.refs_3_), channel_id=1, source_target_pairs={{0,4},{4,0},{8,12},{12,8},{16,20},{20,16},{24,28},{28,24},{1,5},{5... | collective-permute-start | bytes 221192 | tf_op jit(solution)/shard_map/ppermute | solution.py:342
  15.2 0.0 collective-permute-done.3.refs_4_
  15.2 0.0 collective-permute-done.4.refs_5_
  15.2 1.8 %collective-permute-done.5.refs_6_ = bf16[288,128]{1,0:T(8,128)(2,1)S(1)} collective-permute-done((bf16[288,128]{1,0:T(8,128)(2,1)S(1)}, bf16[288,128]{1,0:T(8,128)(2,1)S(1)}, u32[]{:S(2)}, u32[]{:S(2)}) %collective-permute-start.5) | collective-permute-done | bytes 73760 | tf_op jit(solution)/shard_map/ppermute | solution.py:342
  17.0 1.5 %collective-permute-done.6.refs_7_ = bf16[288,128]{1,0:T(8,128)(2,1)S(1)} collective-permute-done((bf16[288,128]{1,0:T(8,128)(2,1)S(1)}, bf16[288,128]{1,0:T(8,128)(2,1)S(1)}, u32[]{:S(2)}, u32[]{:S(2)}) %collective-permute-start.6) | collective-permute-done | bytes 73760 | tf_op jit(solution)/shard_map/ppermute | solution.py:342
  18.5 4.3 %attention.2 = (bf16[4,144,128]{2,1,0:T(8,128)(2,1)S(1)}, bf16[4,144,128]{2,1,0:T(8,128)(2,1)S(1)}) custom-call(s32[2,32]{1,0:T(2,128)} %pages_ref.3, s32[2]{0:T(128)} %lengths_ref.3, bf16[288,128]{1,0:T(8,128)(2,1)S(1)} %get-tuple-element.28.refs_0_, bf16[288,128]{1,0:T(8,128)(2,1)S(1)} %collective-permute-done.refs_1_, ...), custom_call_target="tpu_custom_call" | custom-call | flops 20000000000 | bytes 1048576 | tf_op jit(solution)/shard_map/attention/pallas_call | solution.py:380
  22.8 0.0 slice-start
  22.8 0.0 slice-start.3
  22.8 0.0 slice-start.4
  22.9 0.0 slice-start.6
  22.9 0.0 copy-start.1
  22.9 1.1 %collective-permute-start.7 = (bf16[4,144,128]{2,1,0:T(8,128)(2,1)S(1)}, bf16[4,144,128]{2,1,0:T(8,128)(2,1)S(1)}, u32[]{:S(2)}, u32[]{:S(2)}) collective-permute-start(bf16[4,144,128]{2,1,0:T(8,128)(2,1)S(1)} %get-tuple-element.34), channel_id=1, source_target_pairs={{0,4},{4,0},{8,12},{12,8},{16,20},{20,16},{24,28},{28,24},{1,5},{5... | collective-permute-start | bytes 442376 | tf_op jit(solution)/shard_map/ppermute | solution.py:342
  24.0 4.4 %attention.3 = (bf16[4,144,128]{2,1,0:T(8,128)(2,1)S(1)}, bf16[4,144,128]{2,1,0:T(8,128)(2,1)S(1)}) custom-call(s32[2,32]{1,0:T(2,128)} %pages_ref.3, s32[2]{0:T(128)} %lengths_ref.3, bf16[288,128]{1,0:T(8,128)(2,1)S(1)} %get-tuple-element.28.refs_0_, bf16[288,128]{1,0:T(8,128)(2,1)S(1)} %collective-permute-done.refs_1_, ...), custom_call_target="tpu_custom_call" | custom-call | flops 20000000000 | bytes 1048576 | tf_op jit(solution)/shard_map/attention/pallas_call | solution.py:380
  28.4 1.0 %collective-permute-start.11 = (bf16[4,144,128]{2,1,0:T(8,128)(2,1)S(1)}, bf16[4,144,128]{2,1,0:T(8,128)(2,1)S(1)}, u32[]{:S(2)}, u32[]{:S(2)}) collective-permute-start(bf16[4,144,128]{2,1,0:T(8,128)(2,1)S(1)} %get-tuple-element.40), channel_id=1, source_target_pairs={{0,4},{4,0},{8,12},{12,8},{16,20},{20,16},{24,28},{28,24},{1,5},{5... | collective-permute-start | bytes 442376 | tf_op jit(solution)/shard_map/ppermute | solution.py:342
  29.4 0.0 collective-permute-done.7.other_ref
  29.5 0.1 merge.2
  29.6 3.3 %collective-permute-start.8 = (bf16[144,128]{1,0:T(8,128)(2,1)S(1)}, bf16[144,128]{1,0:T(8,128)(2,1)S(1)}, u32[]{:S(2)}, u32[]{:S(2)}) collective-permute-start(bf16[144,128]{1,0:T(8,128)(2,1)S(1)} %get-tuple-element.36), channel_id=1, source_target_pairs={{0,24},{4,28},{8,16},{12,20},{16,8},{20,12},{24,0},{28,4},{1,25},{... | collective-permute-start | bytes 110600 | tf_op jit(solution)/shard_map/ppermute | solution.py:342
  32.9 1.1 %collective-permute-start.10 = (bf16[144,128]{1,0:T(8,128)(2,1)S(1)}, bf16[144,128]{1,0:T(8,128)(2,1)S(1)}, u32[]{:S(2)}, u32[]{:S(2)}) collective-permute-start(bf16[144,128]{1,0:T(8,128)(2,1)S(1)} %get-tuple-element.38), channel_id=1, source_target_pairs={{0,8},{4,12},{8,0},{12,4},{16,24},{20,28},{24,16},{28,20},{1,9},{5... | collective-permute-start | bytes 110600 | tf_op jit(solution)/shard_map/ppermute | solution.py:342
  34.1 0.0 collective-permute-done.11.other_ref
  34.1 0.1 merge.3
  34.2 3.3 %collective-permute-start.12 = (bf16[144,128]{1,0:T(8,128)(2,1)S(1)}, bf16[144,128]{1,0:T(8,128)(2,1)S(1)}, u32[]{:S(2)}, u32[]{:S(2)}) collective-permute-start(bf16[144,128]{1,0:T(8,128)(2,1)S(1)} %get-tuple-element.42), channel_id=1, source_target_pairs={{0,24},{4,28},{8,16},{12,20},{16,8},{20,12},{24,0},{28,4},{1,25},{... | collective-permute-start | bytes 110600 | tf_op jit(solution)/shard_map/ppermute | solution.py:342
  37.5 0.0 collective-permute-start.13
  37.5 0.0 collective-permute-done.8.refs_1_
  37.6 1.1 %collective-permute-start.14 = (bf16[144,128]{1,0:T(8,128)(2,1)S(1)}, bf16[144,128]{1,0:T(8,128)(2,1)S(1)}, u32[]{:S(2)}, u32[]{:S(2)}) collective-permute-start(bf16[144,128]{1,0:T(8,128)(2,1)S(1)} %get-tuple-element.44), channel_id=1, source_target_pairs={{0,8},{4,12},{8,0},{12,4},{16,24},{20,28},{24,16},{28,20},{1,9},{5... | collective-permute-start | bytes 110600 | tf_op jit(solution)/shard_map/ppermute | solution.py:342
  38.7 1.4 %collective-permute-done.12.refs_5_ = bf16[144,128]{1,0:T(8,128)(2,1)S(1)} collective-permute-done((bf16[144,128]{1,0:T(8,128)(2,1)S(1)}, bf16[144,128]{1,0:T(8,128)(2,1)S(1)}, u32[]{:S(2)}, u32[]{:S(2)}) %collective-permute-start.12) | collective-permute-done | bytes 36896 | tf_op jit(solution)/shard_map/ppermute | solution.py:342
  40.0 2.4 %collective-permute-done.13.refs_6_ = bf16[144,128]{1,0:T(8,128)(2,1)S(1)} collective-permute-done((bf16[144,128]{1,0:T(8,128)(2,1)S(1)}, bf16[144,128]{1,0:T(8,128)(2,1)S(1)}, u32[]{:S(2)}, u32[]{:S(2)}) %collective-permute-start.13) | collective-permute-done | bytes 36896 | tf_op jit(solution)/shard_map/ppermute | solution.py:342
  42.4 0.0 collective-permute-done.14.refs_7_
  42.5 2.9 %up_and_far_output.1 = (bf16[4,4,896]{2,1,0:T(4,128)(2,1)S(1)}, f32[8,2048]{1,0:T(8,128)S(1)}) custom-call(bf16[144,128]{1,0:T(8,128)(2,1)S(1)} %get-tuple-element.35.refs_0_, bf16[144,128]{1,0:T(8,128)(2,1)S(1)} %collective-permute-done.8.refs_1_, bf16[144,128]{1,0:T(8,128)(2,1)S(1)} %collective-permute-done.9.refs_2_, ...), custom_call_target="tpu_custom_call" | custom-call | flops 20000000000 | bytes 1048576 | tf_op jit(solution)/shard_map/up_and_far_output/pallas_call | solution.py:408
  45.4 0.2 collective-permute-start.15
  45.6 2.1 %near_output.1.own_ref = f32[4,4,896]{2,1,0:T(4,128)S(1)} custom-call(f32[8,2048]{1,0:T(8,128)S(1)} %get-tuple-element.45.values, bf16[2048,7168]{1,0:T(8,128)(2,1)S(1)} %bitcast.5), custom_call_target="tpu_custom_call" | custom-call | flops 20000000000 | bytes 1048576 | tf_op jit(solution)/shard_map/near_output/pallas_call | solution.py:419
  47.7 1.5 %collective-permute-done.15.other_ref = bf16[4,4,896]{2,1,0:T(4,128)(2,1)S(1)} collective-permute-done((bf16[4,4,896]{2,1,0:T(4,128)(2,1)S(1)}, bf16[4,4,896]{2,1,0:T(4,128)(2,1)S(1)}, u32[]{:S(2)}, u32[]{:S(2)}) %collective-permute-start.15) | collective-permute-done | bytes 28704 | tf_op jit(solution)/shard_map/ppermute | solution.py:342
  49.3 2.4 %collective-permute-start.16 = (bf16[4,896]{1,0:T(4,128)(2,1)S(1)}, bf16[4,896]{1,0:T(4,128)(2,1)S(1)}, u32[]{:S(2)}, u32[]{:S(2)}) collective-permute-start(bf16[4,896]{1,0:T(4,128)(2,1)S(1)} %get-tuple-element.48), channel_id=1, source_target_pairs={{0,20},{4,16},{8,28},{12,24},{16,4},{20,0},{24,12},{28,8},{1,21},{... | collective-permute-start | bytes 21512 | tf_op jit(solution)/shard_map/ppermute | solution.py:342
  51.7 0.8 %collective-permute-start.17 = (bf16[4,896]{1,0:T(4,128)(2,1)S(1)}, bf16[4,896]{1,0:T(4,128)(2,1)S(1)}, u32[]{:S(2)}, u32[]{:S(2)}) collective-permute-start(bf16[4,896]{1,0:T(4,128)(2,1)S(1)} %get-tuple-element.49), channel_id=1, source_target_pairs={{0,16},{4,20},{8,24},{12,28},{16,0},{20,4},{24,8},{28,12},{1,17},{... | collective-permute-start | bytes 21512 | tf_op jit(solution)/shard_map/ppermute | solution.py:342
  52.5 1.2 %collective-permute-start.18 = (bf16[4,896]{1,0:T(4,128)(2,1)S(1)}, bf16[4,896]{1,0:T(4,128)(2,1)S(1)}, u32[]{:S(2)}, u32[]{:S(2)}) collective-permute-start(bf16[4,896]{1,0:T(4,128)(2,1)S(1)} %get-tuple-element.50), channel_id=1, source_target_pairs={{0,4},{4,0},{8,12},{12,8},{16,20},{20,16},{24,28},{28,24},{1,5},{5... | collective-permute-start | bytes 21512 | tf_op jit(solution)/shard_map/ppermute | solution.py:342
  53.7 1.0 %collective-permute-done.16.refs_0_ = bf16[4,896]{1,0:T(4,128)(2,1)S(1)} collective-permute-done((bf16[4,896]{1,0:T(4,128)(2,1)S(1)}, bf16[4,896]{1,0:T(4,128)(2,1)S(1)}, u32[]{:S(2)}, u32[]{:S(2)}) %collective-permute-start.16) | collective-permute-done | bytes 7200 | tf_op jit(solution)/shard_map/ppermute | solution.py:342
  54.8 1.5 %collective-permute-done.17.refs_1_ = bf16[4,896]{1,0:T(4,128)(2,1)S(1)} collective-permute-done((bf16[4,896]{1,0:T(4,128)(2,1)S(1)}, bf16[4,896]{1,0:T(4,128)(2,1)S(1)}, u32[]{:S(2)}, u32[]{:S(2)}) %collective-permute-start.17) | collective-permute-done | bytes 7200 | tf_op jit(solution)/shard_map/ppermute | solution.py:342
  56.2 0.6 %sum_output.1 = bf16[2,2,896]{2,1,0:T(2,128)(2,1)} custom-call(f32[4,896]{1,0:T(4,128)S(1)} %get-tuple-element.47.own_ref, bf16[4,896]{1,0:T(4,128)(2,1)S(1)} %collective-permute-done.16.refs_0_, bf16[4,896]{1,0:T(4,128)(2,1)S(1)} %collective-permute-done.17.refs_1_, bf16[4,896]{1,0:T(4,128)(2,1)S(1)} %collective-permute-done.18.refs_2_), custom_call_target="tpu_custom_call" | custom-call | tf_op jit(solution)/shard_map/sum_output/pallas_call | solution.py:434
  (19 shorter events, 0.1 us)
Async XLA Ops:
  1.8 8.4 %collective-permute-start = (bf16[288,128]{1,0:T(8,128)(2,1)S(1)}, bf16[288,128]{1,0:T(8,128)(2,1)S(1)}, u32[]{:S(2)}, u32[]{:S(2)}) collective-permute-start(bf16[288,128]{1,0:T(8,128)(2,1)S(1)} %get-tuple-element.28.refs_0_), channel_id=1, source_target_pairs={{0,8},{4,12},{8,0},{12,4},{16,24},{20,28},{24,16},{28,20},{1,9},{5... | collective-permute-start | bytes 221192 | tf_op jit(solution)/shard_map/ppermute | solution.py:342
  4.9 7.8 %collective-permute-start.1 = (bf16[288,128]{1,0:T(8,128)(2,1)S(1)}, bf16[288,128]{1,0:T(8,128)(2,1)S(1)}, u32[]{:S(2)}, u32[]{:S(2)}) collective-permute-start(bf16[288,128]{1,0:T(8,128)(2,1)S(1)} %get-tuple-element.28.refs_0_), channel_id=1, source_target_pairs={{0,16},{4,20},{8,24},{12,28},{16,0},{20,4},{24,8},{28,12},{1,17},{... | collective-permute-start | bytes 221192 | tf_op jit(solution)/shard_map/ppermute | solution.py:342
  7.5 6.7 %collective-permute-start.2 = (bf16[288,128]{1,0:T(8,128)(2,1)S(1)}, bf16[288,128]{1,0:T(8,128)(2,1)S(1)}, u32[]{:S(2)}, u32[]{:S(2)}) collective-permute-start(bf16[288,128]{1,0:T(8,128)(2,1)S(1)} %get-tuple-element.28.refs_0_), channel_id=1, source_target_pairs={{0,24},{4,28},{8,16},{12,20},{16,8},{20,12},{24,0},{28,4},{1,25},{... | collective-permute-start | bytes 221192 | tf_op jit(solution)/shard_map/ppermute | solution.py:342
  7.5 11.0 %copy-start = (bf16[2,4096,576]{1,2,0:T(8,128)(2,1)S(1)}, bf16[2,4096,576]{1,2,0:T(8,128)(2,1)}, u32[]{:S(2)}) copy-start(bf16[2,4096,576]{1,2,0:T(8,128)(2,1)} %param.11) | copy-start | bytes 28311556
  8.5 6.8 %collective-permute-start.3 = (bf16[288,128]{1,0:T(8,128)(2,1)S(1)}, bf16[288,128]{1,0:T(8,128)(2,1)S(1)}, u32[]{:S(2)}, u32[]{:S(2)}) collective-permute-start(bf16[288,128]{1,0:T(8,128)(2,1)S(1)} %get-tuple-element.30), channel_id=1, source_target_pairs={{0,4},{4,0},{8,12},{12,8},{16,20},{20,16},{24,28},{28,24},{1,5},{5... | collective-permute-start | bytes 221192 | tf_op jit(solution)/shard_map/ppermute | solution.py:342
  10.2 5.0 %collective-permute-start.4 = (bf16[288,128]{1,0:T(8,128)(2,1)S(1)}, bf16[288,128]{1,0:T(8,128)(2,1)S(1)}, u32[]{:S(2)}, u32[]{:S(2)}) collective-permute-start(bf16[288,128]{1,0:T(8,128)(2,1)S(1)} %collective-permute-done.refs_1_), channel_id=1, source_target_pairs={{0,4},{4,0},{8,12},{12,8},{16,20},{20,16},{24,28},{28,24},{1,5},{5... | collective-permute-start | bytes 221192 | tf_op jit(solution)/shard_map/ppermute | solution.py:342
  12.7 4.4 %collective-permute-start.5 = (bf16[288,128]{1,0:T(8,128)(2,1)S(1)}, bf16[288,128]{1,0:T(8,128)(2,1)S(1)}, u32[]{:S(2)}, u32[]{:S(2)}) collective-permute-start(bf16[288,128]{1,0:T(8,128)(2,1)S(1)} %collective-permute-done.1.refs_2_), channel_id=1, source_target_pairs={{0,4},{4,0},{8,12},{12,8},{16,20},{20,16},{24,28},{28,24},{1,5},{5... | collective-permute-start | bytes 221192 | tf_op jit(solution)/shard_map/ppermute | solution.py:342
  14.2 4.4 %collective-permute-start.6 = (bf16[288,128]{1,0:T(8,128)(2,1)S(1)}, bf16[288,128]{1,0:T(8,128)(2,1)S(1)}, u32[]{:S(2)}, u32[]{:S(2)}) collective-permute-start(bf16[288,128]{1,0:T(8,128)(2,1)S(1)} %collective-permute-done.2.refs_3_), channel_id=1, source_target_pairs={{0,4},{4,0},{8,12},{12,8},{16,20},{20,16},{24,28},{28,24},{1,5},{5... | collective-permute-start | bytes 221192 | tf_op jit(solution)/shard_map/ppermute | solution.py:342
  22.8 19.6 %slice-start = ((s8[29360128]{0:T(1024)(128)(4,1)}), s8[4194304]{0:T(1024)(128)(4,1)S(1)}, s32[]{:S(2)}) async-start(s8[29360128]{0:T(1024)(128)(4,1)} %bitcast.4), calls=%async_computation | async-start | bytes 8388608
  22.8 19.6 %slice-start.1 = ((s8[29360128]{0:T(1024)(128)(4,1)}), s8[4194304]{0:T(1024)(128)(4,1)S(1)}, s32[]{:S(2)}) async-start(s8[29360128]{0:T(1024)(128)(4,1)} %bitcast.4), calls=%async_computation.1 | async-start | bytes 8388608
  22.8 19.6 %slice-start.2 = ((s8[29360128]{0:T(1024)(128)(4,1)}), s8[4194304]{0:T(1024)(128)(4,1)S(1)}, s32[]{:S(2)}) async-start(s8[29360128]{0:T(1024)(128)(4,1)} %bitcast.4), calls=%async_computation.2 | async-start | bytes 8388608
  22.8 19.6 %slice-start.3 = ((s8[29360128]{0:T(1024)(128)(4,1)}), s8[4194304]{0:T(1024)(128)(4,1)S(1)}, s32[]{:S(2)}) async-start(s8[29360128]{0:T(1024)(128)(4,1)} %bitcast.4), calls=%async_computation.3 | async-start | bytes 8388608
  22.8 19.6 %slice-start.4 = ((s8[29360128]{0:T(1024)(128)(4,1)}), s8[4194304]{0:T(1024)(128)(4,1)S(1)}, s32[]{:S(2)}) async-start(s8[29360128]{0:T(1024)(128)(4,1)} %bitcast.4), calls=%async_computation.4 | async-start | bytes 8388608
  22.9 19.6 %slice-start.5 = ((s8[29360128]{0:T(1024)(128)(4,1)}), s8[4194304]{0:T(1024)(128)(4,1)S(1)}, s32[]{:S(2)}) async-start(s8[29360128]{0:T(1024)(128)(4,1)} %bitcast.4), calls=%async_computation.5 | async-start | bytes 8388608
  22.9 19.6 %slice-start.6 = ((s8[29360128]{0:T(1024)(128)(4,1)}), s8[4194304]{0:T(1024)(128)(4,1)S(1)}, s32[]{:S(2)}) async-start(s8[29360128]{0:T(1024)(128)(4,1)} %bitcast.4), calls=%async_computation.6 | async-start | bytes 8388608
  22.9 19.6 %copy-start.1 = (bf16[16,512,128]{2,1,0:T(8,128)(2,1)S(1)}, bf16[16,512,128]{2,1,0:T(8,128)(2,1)}, u32[]{:S(2)}) copy-start(bf16[16,512,128]{2,1,0:T(8,128)(2,1)} %refs_8_.1) | copy-start | bytes 6291460
  22.9 6.6 %collective-permute-start.7 = (bf16[4,144,128]{2,1,0:T(8,128)(2,1)S(1)}, bf16[4,144,128]{2,1,0:T(8,128)(2,1)S(1)}, u32[]{:S(2)}, u32[]{:S(2)}) collective-permute-start(bf16[4,144,128]{2,1,0:T(8,128)(2,1)S(1)} %get-tuple-element.34), channel_id=1, source_target_pairs={{0,4},{4,0},{8,12},{12,8},{16,20},{20,16},{24,28},{28,24},{1,5},{5... | collective-permute-start | bytes 442376 | tf_op jit(solution)/shard_map/ppermute | solution.py:342
  28.4 5.7 %collective-permute-start.11 = (bf16[4,144,128]{2,1,0:T(8,128)(2,1)S(1)}, bf16[4,144,128]{2,1,0:T(8,128)(2,1)S(1)}, u32[]{:S(2)}, u32[]{:S(2)}) collective-permute-start(bf16[4,144,128]{2,1,0:T(8,128)(2,1)S(1)} %get-tuple-element.40), channel_id=1, source_target_pairs={{0,4},{4,0},{8,12},{12,8},{16,20},{20,16},{24,28},{28,24},{1,5},{5... | collective-permute-start | bytes 442376 | tf_op jit(solution)/shard_map/ppermute | solution.py:342
  29.6 7.9 %collective-permute-start.8 = (bf16[144,128]{1,0:T(8,128)(2,1)S(1)}, bf16[144,128]{1,0:T(8,128)(2,1)S(1)}, u32[]{:S(2)}, u32[]{:S(2)}) collective-permute-start(bf16[144,128]{1,0:T(8,128)(2,1)S(1)} %get-tuple-element.36), channel_id=1, source_target_pairs={{0,24},{4,28},{8,16},{12,20},{16,8},{20,12},{24,0},{28,4},{1,25},{... | collective-permute-start | bytes 110600 | tf_op jit(solution)/shard_map/ppermute | solution.py:342
  32.9 5.7 %collective-permute-start.9 = (bf16[144,128]{1,0:T(8,128)(2,1)S(1)}, bf16[144,128]{1,0:T(8,128)(2,1)S(1)}, u32[]{:S(2)}, u32[]{:S(2)}) collective-permute-start(bf16[144,128]{1,0:T(8,128)(2,1)S(1)} %get-tuple-element.37), channel_id=1, source_target_pairs={{0,16},{4,20},{8,24},{12,28},{16,0},{20,4},{24,8},{28,12},{1,17},{... | collective-permute-start | bytes 110600 | tf_op jit(solution)/shard_map/ppermute | solution.py:342
  32.9 5.7 %collective-permute-start.10 = (bf16[144,128]{1,0:T(8,128)(2,1)S(1)}, bf16[144,128]{1,0:T(8,128)(2,1)S(1)}, u32[]{:S(2)}, u32[]{:S(2)}) collective-permute-start(bf16[144,128]{1,0:T(8,128)(2,1)S(1)} %get-tuple-element.38), channel_id=1, source_target_pairs={{0,8},{4,12},{8,0},{12,4},{16,24},{20,28},{24,16},{28,20},{1,9},{5... | collective-permute-start | bytes 110600 | tf_op jit(solution)/shard_map/ppermute | solution.py:342
  34.2 5.8 %collective-permute-start.12 = (bf16[144,128]{1,0:T(8,128)(2,1)S(1)}, bf16[144,128]{1,0:T(8,128)(2,1)S(1)}, u32[]{:S(2)}, u32[]{:S(2)}) collective-permute-start(bf16[144,128]{1,0:T(8,128)(2,1)S(1)} %get-tuple-element.42), channel_id=1, source_target_pairs={{0,24},{4,28},{8,16},{12,20},{16,8},{20,12},{24,0},{28,4},{1,25},{... | collective-permute-start | bytes 110600 | tf_op jit(solution)/shard_map/ppermute | solution.py:342
  37.5 4.9 %collective-permute-start.13 = (bf16[144,128]{1,0:T(8,128)(2,1)S(1)}, bf16[144,128]{1,0:T(8,128)(2,1)S(1)}, u32[]{:S(2)}, u32[]{:S(2)}) collective-permute-start(bf16[144,128]{1,0:T(8,128)(2,1)S(1)} %get-tuple-element.43), channel_id=1, source_target_pairs={{0,16},{4,20},{8,24},{12,28},{16,0},{20,4},{24,8},{28,12},{1,17},{... | collective-permute-start | bytes 110600 | tf_op jit(solution)/shard_map/ppermute | solution.py:342
  37.6 4.9 %collective-permute-start.14 = (bf16[144,128]{1,0:T(8,128)(2,1)S(1)}, bf16[144,128]{1,0:T(8,128)(2,1)S(1)}, u32[]{:S(2)}, u32[]{:S(2)}) collective-permute-start(bf16[144,128]{1,0:T(8,128)(2,1)S(1)} %get-tuple-element.44), channel_id=1, source_target_pairs={{0,8},{4,12},{8,0},{12,4},{16,24},{20,28},{24,16},{28,20},{1,9},{5... | collective-permute-start | bytes 110600 | tf_op jit(solution)/shard_map/ppermute | solution.py:342
  45.4 3.9 %collective-permute-start.15 = (bf16[4,4,896]{2,1,0:T(4,128)(2,1)S(1)}, bf16[4,4,896]{2,1,0:T(4,128)(2,1)S(1)}, u32[]{:S(2)}, u32[]{:S(2)}) collective-permute-start(bf16[4,4,896]{2,1,0:T(4,128)(2,1)S(1)} %get-tuple-element.46), channel_id=1, source_target_pairs={{0,8},{4,12},{8,0},{12,4},{16,24},{20,28},{24,16},{28,20},{1,9},{5... | collective-permute-start | bytes 86024 | tf_op jit(solution)/shard_map/ppermute | solution.py:342
  49.3 5.5 %collective-permute-start.16 = (bf16[4,896]{1,0:T(4,128)(2,1)S(1)}, bf16[4,896]{1,0:T(4,128)(2,1)S(1)}, u32[]{:S(2)}, u32[]{:S(2)}) collective-permute-start(bf16[4,896]{1,0:T(4,128)(2,1)S(1)} %get-tuple-element.48), channel_id=1, source_target_pairs={{0,20},{4,16},{8,28},{12,24},{16,4},{20,0},{24,12},{28,8},{1,21},{... | collective-permute-start | bytes 21512 | tf_op jit(solution)/shard_map/ppermute | solution.py:342
  51.7 4.5 %collective-permute-start.17 = (bf16[4,896]{1,0:T(4,128)(2,1)S(1)}, bf16[4,896]{1,0:T(4,128)(2,1)S(1)}, u32[]{:S(2)}, u32[]{:S(2)}) collective-permute-start(bf16[4,896]{1,0:T(4,128)(2,1)S(1)} %get-tuple-element.49), channel_id=1, source_target_pairs={{0,16},{4,20},{8,24},{12,28},{16,0},{20,4},{24,8},{28,12},{1,17},{... | collective-permute-start | bytes 21512 | tf_op jit(solution)/shard_map/ppermute | solution.py:342
  52.5 3.8 %collective-permute-start.18 = (bf16[4,896]{1,0:T(4,128)(2,1)S(1)}, bf16[4,896]{1,0:T(4,128)(2,1)S(1)}, u32[]{:S(2)}, u32[]{:S(2)}) collective-permute-start(bf16[4,896]{1,0:T(4,128)(2,1)S(1)} %get-tuple-element.50), channel_id=1, source_target_pairs={{0,4},{4,0},{8,12},{12,8},{16,20},{20,16},{24,28},{28,24},{1,5},{5... | collective-permute-start | bytes 21512 | tf_op jit(solution)/shard_map/ppermute | solution.py:342

commit v7 on v4

--- a/solution.py
+++ b/solution.py
@@ -99,8 +99,7 @@
     heads = half // 2
     line = ctx // 2
     steps = cache_ref.shape[2] // chunk
-    pair_width = 2 * PAGE
-    pairs = chunk // pair_width
+    chunk_pages = chunk // PAGE
     request_rows = LAT_TILES * half
     start = b * request_rows
 
@@ -118,48 +117,43 @@
     def raw_scores(at):
         return jnp.dot(
             query[...],
-            cache_ref[b, :, at * pair_width : (at + 1) * pair_width],
+            cache_ref[b, :, at * chunk : (at + 1) * chunk],
             preferred_element_type=jnp.float32,
         )
 
     def add_products(step):
         weights, factor = weights_of[step % 2], factor_of[step % 2]
-        for columns in (slice(0, LAT // 2), slice(LAT // 2, LAT)):
-            new = lax.dot_general(
-                weights[...],
-                cache_ref[b, columns, step * chunk : (step + 1) * chunk],
-                (((1,), (1,)), ((), ())),
-                preferred_element_type=jnp.float32,
-            )
-            for j in range(columns.start, columns.stop, LANES):
-                part = new[:, j - columns.start : j - columns.start + LANES]
-                at = slice(j, j + LANES)
-                acc[:, at] = acc[:, at] * factor[...] + part if step else part
+        new = lax.dot_general(
+            weights[...],
+            cache_ref[b, :LAT, step * chunk : (step + 1) * chunk],
+            (((1,), (1,)), ((), ())),
+            preferred_element_type=jnp.float32,
+        )
+        for j in range(LAT_TILES):
+            at = slice(j * LANES, (j + 1) * LANES)
+            acc[:, at] = acc[:, at] * factor[...] + new[:, at] if step else new[:, at]
 
     top = jnp.full((rows, LANES), LOWEST, jnp.float32)
     ahead = raw_scores(0)
     for step in range(steps):
         scores, weights = scores_of[step % 2], weights_of[step % 2]
         tops = [None, None]
-        for pair in range(pairs):
-            raw = ahead
-            at = step * pairs + pair
-            if at + 1 < steps * pairs:
-                ahead = raw_scores(at + 1)
-            for side in range(2):
-                page = pair * 2 + side
-                columns = slice(page * PAGE, (page + 1) * PAGE)
-                part = raw[:, side * PAGE : (side + 1) * PAGE].reshape(ctx, 2, heads, PAGE)
-                base = first_pos - pages_ref[b, step * (chunk // PAGE) + page] * PAGE
-                values = []
-                for q in range(2):
-                    distance = base + q - lane
-                    spread = jnp.where(distance >= 0, distance.astype(jnp.float32), jnp.inf)
-                    logs = jnp.log2(spread[None] + inv_rate[...])
-                    value = part[:, q] * (SOFTMAX_SCALE * LOG2E) - scale[...] * logs
-                    tops[q] = value if tops[q] is None else jnp.maximum(tops[q], value)
-                    values.append(value)
-                scores[:, columns] = jnp.stack(values, axis=1).reshape(rows, PAGE)
+        raw = ahead
+        if step + 1 < steps:
+            ahead = raw_scores(step + 1)
+        for page in range(chunk_pages):
+            columns = slice(page * PAGE, (page + 1) * PAGE)
+            part = raw[:, columns].reshape(ctx, 2, heads, PAGE)
+            base = first_pos - pages_ref[b, step * chunk_pages + page] * PAGE
+            values = []
+            for q in range(2):
+                distance = base + q - lane
+                spread = jnp.where(distance >= 0, distance.astype(jnp.float32), jnp.inf)
+                logs = jnp.log2(spread[None] + inv_rate[...])
+                value = part[:, q] * (SOFTMAX_SCALE * LOG2E) - scale[...] * logs
+                tops[q] = value if tops[q] is None else jnp.maximum(tops[q], value)
+                values.append(value)
+            scores[:, columns] = jnp.stack(values, axis=1).reshape(rows, PAGE)
         lane_top = jnp.stack(tops, axis=1).reshape(rows, LANES)
         before = top
         top = jnp.maximum(before, jnp.max(lane_top, axis=1, keepdims=True))

time: 57 us -> 57 us (level)
  no operation moved by 1% of the time
where the time goes in v7:
time: 57 us; the launch traced here: 56.8 us
  starting transfers between devices  26.1 us (46%)
  Pallas kernels  17.3 us (30%)
  waiting for transfers between devices  13.2 us (23%)
    ppermute x19, starting transfers between devices, per_device(): lax.ppermute(value, 'ctx', [(i, i ^ bits) for i in range(ctx)])  26.1 us
    ppermute x19, waiting for transfers between devices, per_device(): lax.ppermute(value, 'ctx', [(i, i ^ bits) for i in range(ctx)])  13.2 us
    pallas_call x2, Pallas kernels, per_device(): pl.pallas_call(functools.partial(attention_kernel, ctx=ctx, b=b), in_spec...  8.6 us
    pallas_call x1, Pallas kernels, per_device(): pl.pallas_call(output_kernel, out_shape=[jax.ShapeDtypeStruct((line, toke...  2.88 us
    pallas_call x1, Pallas kernels, per_device(): pl.pallas_call(near_kernel, out_shape=jax.ShapeDtypeStruct((line, tokens,...  2.14 us
    pallas_call x1, Pallas kernels, per_device(): pl.pallas_call(query_kernel, in_specs=[pl.BlockSpec(memory_space=pl.ANY)]...  1.8 us
  transfers between devices with their start and end apart: 19, of which 8 were waited for; matrix products, arithmetic and copies ran while one was open for 0% of the time, Pallas kernels for 14%

profile of v7, /device:TPU:0, one launch (start us, length us, event | category | flops | bytes accessed | tf_op | source)
XLA Modules:
  0.0 56.8 jit_solution(15374728863341590194)
XLA Ops:
  0.0 1.8 %latent_query.1 = (bf16[288,128]{1,0:T(8,128)(2,1)S(1)}, bf16[288,128]{1,0:T(8,128)(2,1)S(1)}) custom-call(bf16[64,192]{1,0:T(8,128)(2,1)} %bitcast.8, bf16[16,128,512]{2,1,0:T(8,128)(2,1)} %absorb_hbm.1), custom_call_target="tpu_custom_call" | custom-call | tf_op jit(solution)/shard_map/latent_query/pallas_call | solution.py:337
  1.8 3.1 %collective-permute-start = (bf16[288,128]{1,0:T(8,128)(2,1)S(1)}, bf16[288,128]{1,0:T(8,128)(2,1)S(1)}, u32[]{:S(2)}, u32[]{:S(2)}) collective-permute-start(bf16[288,128]{1,0:T(8,128)(2,1)S(1)} %get-tuple-element.28.refs_0_), channel_id=1, source_target_pairs={{0,8},{4,12},{8,0},{12,4},{16,24},{20,28},{24,16},{28,20},{1,9},{5... | collective-permute-start | bytes 221192 | tf_op jit(solution)/shard_map/ppermute | solution.py:336
  4.9 2.6 %collective-permute-start.1 = (bf16[288,128]{1,0:T(8,128)(2,1)S(1)}, bf16[288,128]{1,0:T(8,128)(2,1)S(1)}, u32[]{:S(2)}, u32[]{:S(2)}) collective-permute-start(bf16[288,128]{1,0:T(8,128)(2,1)S(1)} %get-tuple-element.28.refs_0_), channel_id=1, source_target_pairs={{0,16},{4,20},{8,24},{12,28},{16,0},{20,4},{24,8},{28,12},{1,17},{... | collective-permute-start | bytes 221192 | tf_op jit(solution)/shard_map/ppermute | solution.py:336
  7.5 0.0 collective-permute-start.2
  7.5 1.0 %head_columns.1 = (f32[8,16,128]{2,1,0:T(8,128)S(1)}, f32[8,16,128]{2,1,0:T(8,128)S(1)}, bf16[288,128]{1,0:T(8,128)(2,1)S(1)}) custom-call(f32[1,128]{1,0:T(1,128)} %bitcast.9, f32[1,128]{1,0:T(1,128)} %bitcast.10, bf16[288,128]{1,0:T(8,128)(2,1)S(1)} %get-tuple-element.29.through_ref), custom_call_target="tpu_custom_call", output_to_operand_aliasing={{2}: (2, {})} | custom-call | flops 99999997952 | bytes 1048576 | tf_op jit(solution)/shard_map/head_columns/pallas_call | solution.py:350
  8.5 1.8 %collective-permute-start.3 = (bf16[288,128]{1,0:T(8,128)(2,1)S(1)}, bf16[288,128]{1,0:T(8,128)(2,1)S(1)}, u32[]{:S(2)}, u32[]{:S(2)}) collective-permute-start(bf16[288,128]{1,0:T(8,128)(2,1)S(1)} %get-tuple-element.30), channel_id=1, source_target_pairs={{0,4},{4,0},{8,12},{12,8},{16,20},{20,16},{24,28},{28,24},{1,5},{5... | collective-permute-start | bytes 221192 | tf_op jit(solution)/shard_map/ppermute | solution.py:336
  10.2 0.0 collective-permute-done.refs_1_
  10.2 0.3 collective-permute-start.4
  10.5 2.1 %collective-permute-done.1.refs_2_ = bf16[288,128]{1,0:T(8,128)(2,1)S(1)} collective-permute-done((bf16[288,128]{1,0:T(8,128)(2,1)S(1)}, bf16[288,128]{1,0:T(8,128)(2,1)S(1)}, u32[]{:S(2)}, u32[]{:S(2)}) %collective-permute-start.1) | collective-permute-done | bytes 73760 | tf_op jit(solution)/shard_map/ppermute | solution.py:336
  12.7 1.5 %collective-permute-start.5 = (bf16[288,128]{1,0:T(8,128)(2,1)S(1)}, bf16[288,128]{1,0:T(8,128)(2,1)S(1)}, u32[]{:S(2)}, u32[]{:S(2)}) collective-permute-start(bf16[288,128]{1,0:T(8,128)(2,1)S(1)} %collective-permute-done.1.refs_2_), channel_id=1, source_target_pairs={{0,4},{4,0},{8,12},{12,8},{16,20},{20,16},{24,28},{28,24},{1,5},{5... | collective-permute-start | bytes 221192 | tf_op jit(solution)/shard_map/ppermute | solution.py:336
  14.2 0.0 collective-permute-done.2.refs_3_
  14.2 1.1 %collective-permute-start.6 = (bf16[288,128]{1,0:T(8,128)(2,1)S(1)}, bf16[288,128]{1,0:T(8,128)(2,1)S(1)}, u32[]{:S(2)}, u32[]{:S(2)}) collective-permute-start(bf16[288,128]{1,0:T(8,128)(2,1)S(1)} %collective-permute-done.2.refs_3_), channel_id=1, source_target_pairs={{0,4},{4,0},{8,12},{12,8},{16,20},{20,16},{24,28},{28,24},{1,5},{5... | collective-permute-start | bytes 221192 | tf_op jit(solution)/shard_map/ppermute | solution.py:336
  15.2 0.0 collective-permute-done.3.refs_4_
  15.2 0.0 collective-permute-done.4.refs_5_
  15.2 1.8 %collective-permute-done.5.refs_6_ = bf16[288,128]{1,0:T(8,128)(2,1)S(1)} collective-permute-done((bf16[288,128]{1,0:T(8,128)(2,1)S(1)}, bf16[288,128]{1,0:T(8,128)(2,1)S(1)}, u32[]{:S(2)}, u32[]{:S(2)}) %collective-permute-start.5) | collective-permute-done | bytes 73760 | tf_op jit(solution)/shard_map/ppermute | solution.py:336
  17.0 1.5 %collective-permute-done.6.refs_7_ = bf16[288,128]{1,0:T(8,128)(2,1)S(1)} collective-permute-done((bf16[288,128]{1,0:T(8,128)(2,1)S(1)}, bf16[288,128]{1,0:T(8,128)(2,1)S(1)}, u32[]{:S(2)}, u32[]{:S(2)}) %collective-permute-start.6) | collective-permute-done | bytes 73760 | tf_op jit(solution)/shard_map/ppermute | solution.py:336
  18.5 4.2 %attention.2 = (bf16[4,144,128]{2,1,0:T(8,128)(2,1)S(1)}, bf16[4,144,128]{2,1,0:T(8,128)(2,1)S(1)}) custom-call(s32[2,32]{1,0:T(2,128)} %pages_ref.3, s32[2]{0:T(128)} %lengths_ref.3, bf16[288,128]{1,0:T(8,128)(2,1)S(1)} %get-tuple-element.28.refs_0_, bf16[288,128]{1,0:T(8,128)(2,1)S(1)} %collective-permute-done.refs_1_, ...), custom_call_target="tpu_custom_call" | custom-call | flops 20000000000 | bytes 1048576 | tf_op jit(solution)/shard_map/attention/pallas_call | solution.py:373
  22.8 0.0 slice-start
  22.8 0.0 slice-start.1
  22.8 0.0 slice-start.2
  22.8 0.0 slice-start.3
  22.8 0.0 slice-start.4
  22.8 0.0 slice-start.5
  22.9 0.0 copy-start.1
  22.9 1.1 %collective-permute-start.7 = (bf16[4,144,128]{2,1,0:T(8,128)(2,1)S(1)}, bf16[4,144,128]{2,1,0:T(8,128)(2,1)S(1)}, u32[]{:S(2)}, u32[]{:S(2)}) collective-permute-start(bf16[4,144,128]{2,1,0:T(8,128)(2,1)S(1)} %get-tuple-element.34), channel_id=1, source_target_pairs={{0,4},{4,0},{8,12},{12,8},{16,20},{20,16},{24,28},{28,24},{1,5},{5... | collective-permute-start | bytes 442376 | tf_op jit(solution)/shard_map/ppermute | solution.py:336
  24.0 4.4 %attention.3 = (bf16[4,144,128]{2,1,0:T(8,128)(2,1)S(1)}, bf16[4,144,128]{2,1,0:T(8,128)(2,1)S(1)}) custom-call(s32[2,32]{1,0:T(2,128)} %pages_ref.3, s32[2]{0:T(128)} %lengths_ref.3, bf16[288,128]{1,0:T(8,128)(2,1)S(1)} %get-tuple-element.28.refs_0_, bf16[288,128]{1,0:T(8,128)(2,1)S(1)} %collective-permute-done.refs_1_, ...), custom_call_target="tpu_custom_call" | custom-call | flops 20000000000 | bytes 1048576 | tf_op jit(solution)/shard_map/attention/pallas_call | solution.py:373
  28.3 1.0 %collective-permute-start.11 = (bf16[4,144,128]{2,1,0:T(8,128)(2,1)S(1)}, bf16[4,144,128]{2,1,0:T(8,128)(2,1)S(1)}, u32[]{:S(2)}, u32[]{:S(2)}) collective-permute-start(bf16[4,144,128]{2,1,0:T(8,128)(2,1)S(1)} %get-tuple-element.40), channel_id=1, source_target_pairs={{0,4},{4,0},{8,12},{12,8},{16,20},{20,16},{24,28},{28,24},{1,5},{5... | collective-permute-start | bytes 442376 | tf_op jit(solution)/shard_map/ppermute | solution.py:336
  29.4 0.0 collective-permute-done.7.other_ref
  29.4 0.1 merge.2
  29.6 3.3 %collective-permute-start.8 = (bf16[144,128]{1,0:T(8,128)(2,1)S(1)}, bf16[144,128]{1,0:T(8,128)(2,1)S(1)}, u32[]{:S(2)}, u32[]{:S(2)}) collective-permute-start(bf16[144,128]{1,0:T(8,128)(2,1)S(1)} %get-tuple-element.36), channel_id=1, source_target_pairs={{0,24},{4,28},{8,16},{12,20},{16,8},{20,12},{24,0},{28,4},{1,25},{... | collective-permute-start | bytes 110600 | tf_op jit(solution)/shard_map/ppermute | solution.py:336
  32.9 1.1 %collective-permute-start.10 = (bf16[144,128]{1,0:T(8,128)(2,1)S(1)}, bf16[144,128]{1,0:T(8,128)(2,1)S(1)}, u32[]{:S(2)}, u32[]{:S(2)}) collective-permute-start(bf16[144,128]{1,0:T(8,128)(2,1)S(1)} %get-tuple-element.38), channel_id=1, source_target_pairs={{0,8},{4,12},{8,0},{12,4},{16,24},{20,28},{24,16},{28,20},{1,9},{5... | collective-permute-start | bytes 110600 | tf_op jit(solution)/shard_map/ppermute | solution.py:336
  34.0 0.0 collective-permute-done.11.other_ref
  34.0 0.1 merge.3
  34.2 3.3 %collective-permute-start.12 = (bf16[144,128]{1,0:T(8,128)(2,1)S(1)}, bf16[144,128]{1,0:T(8,128)(2,1)S(1)}, u32[]{:S(2)}, u32[]{:S(2)}) collective-permute-start(bf16[144,128]{1,0:T(8,128)(2,1)S(1)} %get-tuple-element.42), channel_id=1, source_target_pairs={{0,24},{4,28},{8,16},{12,20},{16,8},{20,12},{24,0},{28,4},{1,25},{... | collective-permute-start | bytes 110600 | tf_op jit(solution)/shard_map/ppermute | solution.py:336
  37.5 1.1 %collective-permute-start.14 = (bf16[144,128]{1,0:T(8,128)(2,1)S(1)}, bf16[144,128]{1,0:T(8,128)(2,1)S(1)}, u32[]{:S(2)}, u32[]{:S(2)}) collective-permute-start(bf16[144,128]{1,0:T(8,128)(2,1)S(1)} %get-tuple-element.44), channel_id=1, source_target_pairs={{0,8},{4,12},{8,0},{12,4},{16,24},{20,28},{24,16},{28,20},{1,9},{5... | collective-permute-start | bytes 110600 | tf_op jit(solution)/shard_map/ppermute | solution.py:336
  38.6 1.4 %collective-permute-done.12.refs_5_ = bf16[144,128]{1,0:T(8,128)(2,1)S(1)} collective-permute-done((bf16[144,128]{1,0:T(8,128)(2,1)S(1)}, bf16[144,128]{1,0:T(8,128)(2,1)S(1)}, u32[]{:S(2)}, u32[]{:S(2)}) %collective-permute-start.12) | collective-permute-done | bytes 36896 | tf_op jit(solution)/shard_map/ppermute | solution.py:336
  40.0 2.4 %collective-permute-done.13.refs_6_ = bf16[144,128]{1,0:T(8,128)(2,1)S(1)} collective-permute-done((bf16[144,128]{1,0:T(8,128)(2,1)S(1)}, bf16[144,128]{1,0:T(8,128)(2,1)S(1)}, u32[]{:S(2)}, u32[]{:S(2)}) %collective-permute-start.13) | collective-permute-done | bytes 36896 | tf_op jit(solution)/shard_map/ppermute | solution.py:336
  42.4 2.9 %up_and_far_output.1 = (bf16[4,4,896]{2,1,0:T(4,128)(2,1)S(1)}, f32[8,2048]{1,0:T(8,128)S(1)}) custom-call(bf16[144,128]{1,0:T(8,128)(2,1)S(1)} %get-tuple-element.35.refs_0_, bf16[144,128]{1,0:T(8,128)(2,1)S(1)} %collective-permute-done.8.refs_1_, bf16[144,128]{1,0:T(8,128)(2,1)S(1)} %collective-permute-done.9.refs_2_, ...), custom_call_target="tpu_custom_call" | custom-call | flops 20000000000 | bytes 1048576 | tf_op jit(solution)/shard_map/up_and_far_output/pallas_call | solution.py:401
  45.3 0.2 collective-permute-start.15
  45.5 2.1 %near_output.1.own_ref = f32[4,4,896]{2,1,0:T(4,128)S(1)} custom-call(f32[8,2048]{1,0:T(8,128)S(1)} %get-tuple-element.45.values, bf16[2048,7168]{1,0:T(8,128)(2,1)S(1)} %bitcast.5), custom_call_target="tpu_custom_call" | custom-call | flops 20000000000 | bytes 1048576 | tf_op jit(solution)/shard_map/near_output/pallas_call | solution.py:412
  47.7 1.5 %collective-permute-done.15.other_ref = bf16[4,4,896]{2,1,0:T(4,128)(2,1)S(1)} collective-permute-done((bf16[4,4,896]{2,1,0:T(4,128)(2,1)S(1)}, bf16[4,4,896]{2,1,0:T(4,128)(2,1)S(1)}, u32[]{:S(2)}, u32[]{:S(2)}) %collective-permute-start.15) | collective-permute-done | bytes 28704 | tf_op jit(solution)/shard_map/ppermute | solution.py:336
  49.2 2.4 %collective-permute-start.16 = (bf16[4,896]{1,0:T(4,128)(2,1)S(1)}, bf16[4,896]{1,0:T(4,128)(2,1)S(1)}, u32[]{:S(2)}, u32[]{:S(2)}) collective-permute-start(bf16[4,896]{1,0:T(4,128)(2,1)S(1)} %get-tuple-element.48), channel_id=1, source_target_pairs={{0,20},{4,16},{8,28},{12,24},{16,4},{20,0},{24,12},{28,8},{1,21},{... | collective-permute-start | bytes 21512 | tf_op jit(solution)/shard_map/ppermute | solution.py:336
  51.6 0.8 %collective-permute-start.17 = (bf16[4,896]{1,0:T(4,128)(2,1)S(1)}, bf16[4,896]{1,0:T(4,128)(2,1)S(1)}, u32[]{:S(2)}, u32[]{:S(2)}) collective-permute-start(bf16[4,896]{1,0:T(4,128)(2,1)S(1)} %get-tuple-element.49), channel_id=1, source_target_pairs={{0,16},{4,20},{8,24},{12,28},{16,0},{20,4},{24,8},{28,12},{1,17},{... | collective-permute-start | bytes 21512 | tf_op jit(solution)/shard_map/ppermute | solution.py:336
  52.4 1.2 %collective-permute-start.18 = (bf16[4,896]{1,0:T(4,128)(2,1)S(1)}, bf16[4,896]{1,0:T(4,128)(2,1)S(1)}, u32[]{:S(2)}, u32[]{:S(2)}) collective-permute-start(bf16[4,896]{1,0:T(4,128)(2,1)S(1)} %get-tuple-element.50), channel_id=1, source_target_pairs={{0,4},{4,0},{8,12},{12,8},{16,20},{20,16},{24,28},{28,24},{1,5},{5... | collective-permute-start | bytes 21512 | tf_op jit(solution)/shard_map/ppermute | solution.py:336
  53.7 1.0 %collective-permute-done.16.refs_0_ = bf16[4,896]{1,0:T(4,128)(2,1)S(1)} collective-permute-done((bf16[4,896]{1,0:T(4,128)(2,1)S(1)}, bf16[4,896]{1,0:T(4,128)(2,1)S(1)}, u32[]{:S(2)}, u32[]{:S(2)}) %collective-permute-start.16) | collective-permute-done | bytes 7200 | tf_op jit(solution)/shard_map/ppermute | solution.py:336
  54.7 1.5 %collective-permute-done.17.refs_1_ = bf16[4,896]{1,0:T(4,128)(2,1)S(1)} collective-permute-done((bf16[4,896]{1,0:T(4,128)(2,1)S(1)}, bf16[4,896]{1,0:T(4,128)(2,1)S(1)}, u32[]{:S(2)}, u32[]{:S(2)}) %collective-permute-start.17) | collective-permute-done | bytes 7200 | tf_op jit(solution)/shard_map/ppermute | solution.py:336
  56.2 0.0 collective-permute-done.18.refs_2_
  56.2 0.6 %sum_output.1 = bf16[2,2,896]{2,1,0:T(2,128)(2,1)} custom-call(f32[4,896]{1,0:T(4,128)S(1)} %get-tuple-element.47.own_ref, bf16[4,896]{1,0:T(4,128)(2,1)S(1)} %collective-permute-done.16.refs_0_, bf16[4,896]{1,0:T(4,128)(2,1)S(1)} %collective-permute-done.17.refs_1_, bf16[4,896]{1,0:T(4,128)(2,1)S(1)} %collective-permute-done.18.refs_2_), custom_call_target="tpu_custom_call" | custom-call | tf_op jit(solution)/shard_map/sum_output/pallas_call | solution.py:427
  (19 shorter events, 0.1 us)
Async XLA Ops:
  1.8 8.4 %collective-permute-start = (bf16[288,128]{1,0:T(8,128)(2,1)S(1)}, bf16[288,128]{1,0:T(8,128)(2,1)S(1)}, u32[]{:S(2)}, u32[]{:S(2)}) collective-permute-start(bf16[288,128]{1,0:T(8,128)(2,1)S(1)} %get-tuple-element.28.refs_0_), channel_id=1, source_target_pairs={{0,8},{4,12},{8,0},{12,4},{16,24},{20,28},{24,16},{28,20},{1,9},{5... | collective-permute-start | bytes 221192 | tf_op jit(solution)/shard_map/ppermute | solution.py:336
  4.9 7.8 %collective-permute-start.1 = (bf16[288,128]{1,0:T(8,128)(2,1)S(1)}, bf16[288,128]{1,0:T(8,128)(2,1)S(1)}, u32[]{:S(2)}, u32[]{:S(2)}) collective-permute-start(bf16[288,128]{1,0:T(8,128)(2,1)S(1)} %get-tuple-element.28.refs_0_), channel_id=1, source_target_pairs={{0,16},{4,20},{8,24},{12,28},{16,0},{20,4},{24,8},{28,12},{1,17},{... | collective-permute-start | bytes 221192 | tf_op jit(solution)/shard_map/ppermute | solution.py:336
  7.5 6.7 %collective-permute-start.2 = (bf16[288,128]{1,0:T(8,128)(2,1)S(1)}, bf16[288,128]{1,0:T(8,128)(2,1)S(1)}, u32[]{:S(2)}, u32[]{:S(2)}) collective-permute-start(bf16[288,128]{1,0:T(8,128)(2,1)S(1)} %get-tuple-element.28.refs_0_), channel_id=1, source_target_pairs={{0,24},{4,28},{8,16},{12,20},{16,8},{20,12},{24,0},{28,4},{1,25},{... | collective-permute-start | bytes 221192 | tf_op jit(solution)/shard_map/ppermute | solution.py:336
  7.5 11.0 %copy-start = (bf16[2,4096,576]{1,2,0:T(8,128)(2,1)S(1)}, bf16[2,4096,576]{1,2,0:T(8,128)(2,1)}, u32[]{:S(2)}) copy-start(bf16[2,4096,576]{1,2,0:T(8,128)(2,1)} %param.11) | copy-start | bytes 28311556
  8.5 6.8 %collective-permute-start.3 = (bf16[288,128]{1,0:T(8,128)(2,1)S(1)}, bf16[288,128]{1,0:T(8,128)(2,1)S(1)}, u32[]{:S(2)}, u32[]{:S(2)}) collective-permute-start(bf16[288,128]{1,0:T(8,128)(2,1)S(1)} %get-tuple-element.30), channel_id=1, source_target_pairs={{0,4},{4,0},{8,12},{12,8},{16,20},{20,16},{24,28},{28,24},{1,5},{5... | collective-permute-start | bytes 221192 | tf_op jit(solution)/shard_map/ppermute | solution.py:336
  10.2 5.0 %collective-permute-start.4 = (bf16[288,128]{1,0:T(8,128)(2,1)S(1)}, bf16[288,128]{1,0:T(8,128)(2,1)S(1)}, u32[]{:S(2)}, u32[]{:S(2)}) collective-permute-start(bf16[288,128]{1,0:T(8,128)(2,1)S(1)} %collective-permute-done.refs_1_), channel_id=1, source_target_pairs={{0,4},{4,0},{8,12},{12,8},{16,20},{20,16},{24,28},{28,24},{1,5},{5... | collective-permute-start | bytes 221192 | tf_op jit(solution)/shard_map/ppermute | solution.py:336
  12.7 4.4 %collective-permute-start.5 = (bf16[288,128]{1,0:T(8,128)(2,1)S(1)}, bf16[288,128]{1,0:T(8,128)(2,1)S(1)}, u32[]{:S(2)}, u32[]{:S(2)}) collective-permute-start(bf16[288,128]{1,0:T(8,128)(2,1)S(1)} %collective-permute-done.1.refs_2_), channel_id=1, source_target_pairs={{0,4},{4,0},{8,12},{12,8},{16,20},{20,16},{24,28},{28,24},{1,5},{5... | collective-permute-start | bytes 221192 | tf_op jit(solution)/shard_map/ppermute | solution.py:336
  14.2 4.4 %collective-permute-start.6 = (bf16[288,128]{1,0:T(8,128)(2,1)S(1)}, bf16[288,128]{1,0:T(8,128)(2,1)S(1)}, u32[]{:S(2)}, u32[]{:S(2)}) collective-permute-start(bf16[288,128]{1,0:T(8,128)(2,1)S(1)} %collective-permute-done.2.refs_3_), channel_id=1, source_target_pairs={{0,4},{4,0},{8,12},{12,8},{16,20},{20,16},{24,28},{28,24},{1,5},{5... | collective-permute-start | bytes 221192 | tf_op jit(solution)/shard_map/ppermute | solution.py:336
  22.8 19.6 %slice-start = ((s8[29360128]{0:T(1024)(128)(4,1)}), s8[4194304]{0:T(1024)(128)(4,1)S(1)}, s32[]{:S(2)}) async-start(s8[29360128]{0:T(1024)(128)(4,1)} %bitcast.4), calls=%async_computation | async-start | bytes 8388608
  22.8 19.6 %slice-start.1 = ((s8[29360128]{0:T(1024)(128)(4,1)}), s8[4194304]{0:T(1024)(128)(4,1)S(1)}, s32[]{:S(2)}) async-start(s8[29360128]{0:T(1024)(128)(4,1)} %bitcast.4), calls=%async_computation.1 | async-start | bytes 8388608
  22.8 19.6 %slice-start.2 = ((s8[29360128]{0:T(1024)(128)(4,1)}), s8[4194304]{0:T(1024)(128)(4,1)S(1)}, s32[]{:S(2)}) async-start(s8[29360128]{0:T(1024)(128)(4,1)} %bitcast.4), calls=%async_computation.2 | async-start | bytes 8388608
  22.8 19.6 %slice-start.3 = ((s8[29360128]{0:T(1024)(128)(4,1)}), s8[4194304]{0:T(1024)(128)(4,1)S(1)}, s32[]{:S(2)}) async-start(s8[29360128]{0:T(1024)(128)(4,1)} %bitcast.4), calls=%async_computation.3 | async-start | bytes 8388608
  22.8 19.6 %slice-start.4 = ((s8[29360128]{0:T(1024)(128)(4,1)}), s8[4194304]{0:T(1024)(128)(4,1)S(1)}, s32[]{:S(2)}) async-start(s8[29360128]{0:T(1024)(128)(4,1)} %bitcast.4), calls=%async_computation.4 | async-start | bytes 8388608
  22.8 19.6 %slice-start.5 = ((s8[29360128]{0:T(1024)(128)(4,1)}), s8[4194304]{0:T(1024)(128)(4,1)S(1)}, s32[]{:S(2)}) async-start(s8[29360128]{0:T(1024)(128)(4,1)} %bitcast.4), calls=%async_computation.5 | async-start | bytes 8388608
  22.8 19.6 %slice-start.6 = ((s8[29360128]{0:T(1024)(128)(4,1)}), s8[4194304]{0:T(1024)(128)(4,1)S(1)}, s32[]{:S(2)}) async-start(s8[29360128]{0:T(1024)(128)(4,1)} %bitcast.4), calls=%async_computation.6 | async-start | bytes 8388608
  22.9 19.6 %copy-start.1 = (bf16[16,512,128]{2,1,0:T(8,128)(2,1)S(1)}, bf16[16,512,128]{2,1,0:T(8,128)(2,1)}, u32[]{:S(2)}) copy-start(bf16[16,512,128]{2,1,0:T(8,128)(2,1)} %refs_8_.1) | copy-start | bytes 6291460
  22.9 6.5 %collective-permute-start.7 = (bf16[4,144,128]{2,1,0:T(8,128)(2,1)S(1)}, bf16[4,144,128]{2,1,0:T(8,128)(2,1)S(1)}, u32[]{:S(2)}, u32[]{:S(2)}) collective-permute-start(bf16[4,144,128]{2,1,0:T(8,128)(2,1)S(1)} %get-tuple-element.34), channel_id=1, source_target_pairs={{0,4},{4,0},{8,12},{12,8},{16,20},{20,16},{24,28},{28,24},{1,5},{5... | collective-permute-start | bytes 442376 | tf_op jit(solution)/shard_map/ppermute | solution.py:336
  28.3 5.7 %collective-permute-start.11 = (bf16[4,144,128]{2,1,0:T(8,128)(2,1)S(1)}, bf16[4,144,128]{2,1,0:T(8,128)(2,1)S(1)}, u32[]{:S(2)}, u32[]{:S(2)}) collective-permute-start(bf16[4,144,128]{2,1,0:T(8,128)(2,1)S(1)} %get-tuple-element.40), channel_id=1, source_target_pairs={{0,4},{4,0},{8,12},{12,8},{16,20},{20,16},{24,28},{28,24},{1,5},{5... | collective-permute-start | bytes 442376 | tf_op jit(solution)/shard_map/ppermute | solution.py:336
  29.6 7.9 %collective-permute-start.8 = (bf16[144,128]{1,0:T(8,128)(2,1)S(1)}, bf16[144,128]{1,0:T(8,128)(2,1)S(1)}, u32[]{:S(2)}, u32[]{:S(2)}) collective-permute-start(bf16[144,128]{1,0:T(8,128)(2,1)S(1)} %get-tuple-element.36), channel_id=1, source_target_pairs={{0,24},{4,28},{8,16},{12,20},{16,8},{20,12},{24,0},{28,4},{1,25},{... | collective-permute-start | bytes 110600 | tf_op jit(solution)/shard_map/ppermute | solution.py:336
  32.9 5.7 %collective-permute-start.9 = (bf16[144,128]{1,0:T(8,128)(2,1)S(1)}, bf16[144,128]{1,0:T(8,128)(2,1)S(1)}, u32[]{:S(2)}, u32[]{:S(2)}) collective-permute-start(bf16[144,128]{1,0:T(8,128)(2,1)S(1)} %get-tuple-element.37), channel_id=1, source_target_pairs={{0,16},{4,20},{8,24},{12,28},{16,0},{20,4},{24,8},{28,12},{1,17},{... | collective-permute-start | bytes 110600 | tf_op jit(solution)/shard_map/ppermute | solution.py:336
  32.9 5.7 %collective-permute-start.10 = (bf16[144,128]{1,0:T(8,128)(2,1)S(1)}, bf16[144,128]{1,0:T(8,128)(2,1)S(1)}, u32[]{:S(2)}, u32[]{:S(2)}) collective-permute-start(bf16[144,128]{1,0:T(8,128)(2,1)S(1)} %get-tuple-element.38), channel_id=1, source_target_pairs={{0,8},{4,12},{8,0},{12,4},{16,24},{20,28},{24,16},{28,20},{1,9},{5... | collective-permute-start | bytes 110600 | tf_op jit(solution)/shard_map/ppermute | solution.py:336
  34.2 5.8 %collective-permute-start.12 = (bf16[144,128]{1,0:T(8,128)(2,1)S(1)}, bf16[144,128]{1,0:T(8,128)(2,1)S(1)}, u32[]{:S(2)}, u32[]{:S(2)}) collective-permute-start(bf16[144,128]{1,0:T(8,128)(2,1)S(1)} %get-tuple-element.42), channel_id=1, source_target_pairs={{0,24},{4,28},{8,16},{12,20},{16,8},{20,12},{24,0},{28,4},{1,25},{... | collective-permute-start | bytes 110600 | tf_op jit(solution)/shard_map/ppermute | solution.py:336
  37.5 4.9 %collective-permute-start.13 = (bf16[144,128]{1,0:T(8,128)(2,1)S(1)}, bf16[144,128]{1,0:T(8,128)(2,1)S(1)}, u32[]{:S(2)}, u32[]{:S(2)}) collective-permute-start(bf16[144,128]{1,0:T(8,128)(2,1)S(1)} %get-tuple-element.43), channel_id=1, source_target_pairs={{0,16},{4,20},{8,24},{12,28},{16,0},{20,4},{24,8},{28,12},{1,17},{... | collective-permute-start | bytes 110600 | tf_op jit(solution)/shard_map/ppermute | solution.py:336
  37.5 4.9 %collective-permute-start.14 = (bf16[144,128]{1,0:T(8,128)(2,1)S(1)}, bf16[144,128]{1,0:T(8,128)(2,1)S(1)}, u32[]{:S(2)}, u32[]{:S(2)}) collective-permute-start(bf16[144,128]{1,0:T(8,128)(2,1)S(1)} %get-tuple-element.44), channel_id=1, source_target_pairs={{0,8},{4,12},{8,0},{12,4},{16,24},{20,28},{24,16},{28,20},{1,9},{5... | collective-permute-start | bytes 110600 | tf_op jit(solution)/shard_map/ppermute | solution.py:336
  45.3 3.9 %collective-permute-start.15 = (bf16[4,4,896]{2,1,0:T(4,128)(2,1)S(1)}, bf16[4,4,896]{2,1,0:T(4,128)(2,1)S(1)}, u32[]{:S(2)}, u32[]{:S(2)}) collective-permute-start(bf16[4,4,896]{2,1,0:T(4,128)(2,1)S(1)} %get-tuple-element.46), channel_id=1, source_target_pairs={{0,8},{4,12},{8,0},{12,4},{16,24},{20,28},{24,16},{28,20},{1,9},{5... | collective-permute-start | bytes 86024 | tf_op jit(solution)/shard_map/ppermute | solution.py:336
  49.2 5.5 %collective-permute-start.16 = (bf16[4,896]{1,0:T(4,128)(2,1)S(1)}, bf16[4,896]{1,0:T(4,128)(2,1)S(1)}, u32[]{:S(2)}, u32[]{:S(2)}) collective-permute-start(bf16[4,896]{1,0:T(4,128)(2,1)S(1)} %get-tuple-element.48), channel_id=1, source_target_pairs={{0,20},{4,16},{8,28},{12,24},{16,4},{20,0},{24,12},{28,8},{1,21},{... | collective-permute-start | bytes 21512 | tf_op jit(solution)/shard_map/ppermute | solution.py:336
  51.6 4.5 %collective-permute-start.17 = (bf16[4,896]{1,0:T(4,128)(2,1)S(1)}, bf16[4,896]{1,0:T(4,128)(2,1)S(1)}, u32[]{:S(2)}, u32[]{:S(2)}) collective-permute-start(bf16[4,896]{1,0:T(4,128)(2,1)S(1)} %get-tuple-element.49), channel_id=1, source_target_pairs={{0,16},{4,20},{8,24},{12,28},{16,0},{20,4},{24,8},{28,12},{1,17},{... | collective-permute-start | bytes 21512 | tf_op jit(solution)/shard_map/ppermute | solution.py:336
  52.4 3.8 %collective-permute-start.18 = (bf16[4,896]{1,0:T(4,128)(2,1)S(1)}, bf16[4,896]{1,0:T(4,128)(2,1)S(1)}, u32[]{:S(2)}, u32[]{:S(2)}) collective-permute-start(bf16[4,896]{1,0:T(4,128)(2,1)S(1)} %get-tuple-element.50), channel_id=1, source_target_pairs={{0,4},{4,0},{8,12},{12,8},{16,20},{20,16},{24,28},{28,24},{1,5},{5... | collective-permute-start | bytes 21512 | tf_op jit(solution)/shard_map/ppermute | solution.py:336

commit v8 on v4

--- a/solution.py
+++ b/solution.py
@@ -399,7 +399,7 @@
             name="merge",
         )(near, swap(far, 1))
         parts.append(merged[0])
-        parts += [swap(merged[k], 2 * k) for k in reversed(range(1, line))]
+        parts += [swap(merged[k], 2 * k) for k in (line // 2, *range(line // 2 + 1, line), *range(1, line // 2))]
 
     tokens = requests * query_len
     weight = in_vmem(output_weight)

time: 57 us -> 56.9 us (level)
  starting transfers between devices: 26.1 us -> 24.7 us
  waiting for transfers between devices: 13.2 us -> 14.5 us
    ppermute x19, starting transfers between devices: 26.1 us -> 24.7 us  [per_device(): lax.ppermute(value, 'ctx', [(i, i ^ bits) for i in range(ctx)])]
    ppermute x19, waiting for transfers between devices: 13.2 us -> 14.5 us  [per_device(): lax.ppermute(value, 'ctx', [(i, i ^ bits) for i in range(ctx)])]
  transfers between devices with their start and end apart: 19 -> 19, of which waited for: 8 -> 11; matrix products, arithmetic and copies ran while one was open for 0% -> 0% of each run, Pallas kernels for 14% -> 14%
where the time goes in v8:
time: 56.9 us; the launch traced here: 56.7 us
  starting transfers between devices  24.7 us (43%)
  Pallas kernels  17.4 us (31%)
  waiting for transfers between devices  14.5 us (25%)
    ppermute x19, starting transfers between devices, per_device(): lax.ppermute(value, 'ctx', [(i, i ^ bits) for i in range(ctx)])  24.7 us
    ppermute x19, waiting for transfers between devices, per_device(): lax.ppermute(value, 'ctx', [(i, i ^ bits) for i in range(ctx)])  14.5 us
    pallas_call x2, Pallas kernels, per_device(): pl.pallas_call(functools.partial(attention_kernel, ctx=ctx, b=b), in_spec...  8.66 us
    pallas_call x1, Pallas kernels, per_device(): pl.pallas_call(output_kernel, out_shape=[jax.ShapeDtypeStruct((line, toke...  2.88 us
    pallas_call x1, Pallas kernels, per_device(): pl.pallas_call(near_kernel, out_shape=jax.ShapeDtypeStruct((line, tokens,...  2.14 us
    pallas_call x1, Pallas kernels, per_device(): pl.pallas_call(query_kernel, in_specs=[pl.BlockSpec(memory_space=pl.ANY)]...  1.8 us
  transfers between devices with their start and end apart: 19, of which 11 were waited for; matrix products, arithmetic and copies ran while one was open for 0% of the time, Pallas kernels for 14%

profile of v8, /device:TPU:0, one launch (start us, length us, event | category | flops | bytes accessed | tf_op | source)
XLA Modules:
  0.0 56.7 jit_solution(4815885906056976538)
XLA Ops:
  0.0 1.8 %latent_query.1 = (bf16[288,128]{1,0:T(8,128)(2,1)S(1)}, bf16[288,128]{1,0:T(8,128)(2,1)S(1)}) custom-call(bf16[64,192]{1,0:T(8,128)(2,1)} %bitcast.8, bf16[16,128,512]{2,1,0:T(8,128)(2,1)} %absorb_hbm.1), custom_call_target="tpu_custom_call" | custom-call | tf_op jit(solution)/shard_map/latent_query/pallas_call | solution.py:343
  1.8 3.1 %collective-permute-start = (bf16[288,128]{1,0:T(8,128)(2,1)S(1)}, bf16[288,128]{1,0:T(8,128)(2,1)S(1)}, u32[]{:S(2)}, u32[]{:S(2)}) collective-permute-start(bf16[288,128]{1,0:T(8,128)(2,1)S(1)} %get-tuple-element.28.refs_0_), channel_id=1, source_target_pairs={{0,8},{4,12},{8,0},{12,4},{16,24},{20,28},{24,16},{28,20},{1,9},{5... | collective-permute-start | bytes 221192 | tf_op jit(solution)/shard_map/ppermute | solution.py:342
  4.9 2.6 %collective-permute-start.1 = (bf16[288,128]{1,0:T(8,128)(2,1)S(1)}, bf16[288,128]{1,0:T(8,128)(2,1)S(1)}, u32[]{:S(2)}, u32[]{:S(2)}) collective-permute-start(bf16[288,128]{1,0:T(8,128)(2,1)S(1)} %get-tuple-element.28.refs_0_), channel_id=1, source_target_pairs={{0,16},{4,20},{8,24},{12,28},{16,0},{20,4},{24,8},{28,12},{1,17},{... | collective-permute-start | bytes 221192 | tf_op jit(solution)/shard_map/ppermute | solution.py:342
  7.5 1.0 %head_columns.1 = (f32[8,16,128]{2,1,0:T(8,128)S(1)}, f32[8,16,128]{2,1,0:T(8,128)S(1)}, bf16[288,128]{1,0:T(8,128)(2,1)S(1)}) custom-call(f32[1,128]{1,0:T(1,128)} %bitcast.9, f32[1,128]{1,0:T(1,128)} %bitcast.10, bf16[288,128]{1,0:T(8,128)(2,1)S(1)} %get-tuple-element.29.through_ref), custom_call_target="tpu_custom_call", output_to_operand_aliasing={{2}: (2, {})} | custom-call | flops 99999997952 | bytes 1048576 | tf_op jit(solution)/shard_map/head_columns/pallas_call | solution.py:356
  8.5 1.8 %collective-permute-start.3 = (bf16[288,128]{1,0:T(8,128)(2,1)S(1)}, bf16[288,128]{1,0:T(8,128)(2,1)S(1)}, u32[]{:S(2)}, u32[]{:S(2)}) collective-permute-start(bf16[288,128]{1,0:T(8,128)(2,1)S(1)} %get-tuple-element.30), channel_id=1, source_target_pairs={{0,4},{4,0},{8,12},{12,8},{16,20},{20,16},{24,28},{28,24},{1,5},{5... | collective-permute-start | bytes 221192 | tf_op jit(solution)/shard_map/ppermute | solution.py:342
  10.2 0.0 collective-permute-done.refs_1_
  10.2 0.3 collective-permute-start.4
  10.5 2.1 %collective-permute-done.1.refs_2_ = bf16[288,128]{1,0:T(8,128)(2,1)S(1)} collective-permute-done((bf16[288,128]{1,0:T(8,128)(2,1)S(1)}, bf16[288,128]{1,0:T(8,128)(2,1)S(1)}, u32[]{:S(2)}, u32[]{:S(2)}) %collective-permute-start.1) | collective-permute-done | bytes 73760 | tf_op jit(solution)/shard_map/ppermute | solution.py:342
  12.7 1.5 %collective-permute-start.5 = (bf16[288,128]{1,0:T(8,128)(2,1)S(1)}, bf16[288,128]{1,0:T(8,128)(2,1)S(1)}, u32[]{:S(2)}, u32[]{:S(2)}) collective-permute-start(bf16[288,128]{1,0:T(8,128)(2,1)S(1)} %collective-permute-done.1.refs_2_), channel_id=1, source_target_pairs={{0,4},{4,0},{8,12},{12,8},{16,20},{20,16},{24,28},{28,24},{1,5},{5... | collective-permute-start | bytes 221192 | tf_op jit(solution)/shard_map/ppermute | solution.py:342
  14.2 1.1 %collective-permute-start.6 = (bf16[288,128]{1,0:T(8,128)(2,1)S(1)}, bf16[288,128]{1,0:T(8,128)(2,1)S(1)}, u32[]{:S(2)}, u32[]{:S(2)}) collective-permute-start(bf16[288,128]{1,0:T(8,128)(2,1)S(1)} %collective-permute-done.2.refs_3_), channel_id=1, source_target_pairs={{0,4},{4,0},{8,12},{12,8},{16,20},{20,16},{24,28},{28,24},{1,5},{5... | collective-permute-start | bytes 221192 | tf_op jit(solution)/shard_map/ppermute | solution.py:342
  15.2 0.0 collective-permute-done.3.refs_4_
  15.2 0.0 collective-permute-done.4.refs_5_
  15.2 1.8 %collective-permute-done.5.refs_6_ = bf16[288,128]{1,0:T(8,128)(2,1)S(1)} collective-permute-done((bf16[288,128]{1,0:T(8,128)(2,1)S(1)}, bf16[288,128]{1,0:T(8,128)(2,1)S(1)}, u32[]{:S(2)}, u32[]{:S(2)}) %collective-permute-start.5) | collective-permute-done | bytes 73760 | tf_op jit(solution)/shard_map/ppermute | solution.py:342
  17.0 1.5 %collective-permute-done.6.refs_7_ = bf16[288,128]{1,0:T(8,128)(2,1)S(1)} collective-permute-done((bf16[288,128]{1,0:T(8,128)(2,1)S(1)}, bf16[288,128]{1,0:T(8,128)(2,1)S(1)}, u32[]{:S(2)}, u32[]{:S(2)}) %collective-permute-start.6) | collective-permute-done | bytes 73760 | tf_op jit(solution)/shard_map/ppermute | solution.py:342
  18.5 4.3 %attention.2 = (bf16[4,144,128]{2,1,0:T(8,128)(2,1)S(1)}, bf16[4,144,128]{2,1,0:T(8,128)(2,1)S(1)}) custom-call(s32[2,32]{1,0:T(2,128)} %pages_ref.3, s32[2]{0:T(128)} %lengths_ref.3, bf16[288,128]{1,0:T(8,128)(2,1)S(1)} %get-tuple-element.28.refs_0_, bf16[288,128]{1,0:T(8,128)(2,1)S(1)} %collective-permute-done.refs_1_, ...), custom_call_target="tpu_custom_call" | custom-call | flops 20000000000 | bytes 1048576 | tf_op jit(solution)/shard_map/attention/pallas_call | solution.py:379
  22.8 0.0 slice-start
  22.8 0.0 slice-start.1
  22.8 0.0 slice-start.2
  22.8 0.0 slice-start.4
  22.9 0.0 slice-start.5
  22.9 0.0 copy-start.1
  22.9 1.1 %collective-permute-start.7 = (bf16[4,144,128]{2,1,0:T(8,128)(2,1)S(1)}, bf16[4,144,128]{2,1,0:T(8,128)(2,1)S(1)}, u32[]{:S(2)}, u32[]{:S(2)}) collective-permute-start(bf16[4,144,128]{2,1,0:T(8,128)(2,1)S(1)} %get-tuple-element.34), channel_id=1, source_target_pairs={{0,4},{4,0},{8,12},{12,8},{16,20},{20,16},{24,28},{28,24},{1,5},{5... | collective-permute-start | bytes 442376 | tf_op jit(solution)/shard_map/ppermute | solution.py:342
  24.0 4.4 %attention.3 = (bf16[4,144,128]{2,1,0:T(8,128)(2,1)S(1)}, bf16[4,144,128]{2,1,0:T(8,128)(2,1)S(1)}) custom-call(s32[2,32]{1,0:T(2,128)} %pages_ref.3, s32[2]{0:T(128)} %lengths_ref.3, bf16[288,128]{1,0:T(8,128)(2,1)S(1)} %get-tuple-element.28.refs_0_, bf16[288,128]{1,0:T(8,128)(2,1)S(1)} %collective-permute-done.refs_1_, ...), custom_call_target="tpu_custom_call" | custom-call | flops 20000000000 | bytes 1048576 | tf_op jit(solution)/shard_map/attention/pallas_call | solution.py:379
  28.4 1.0 %collective-permute-start.11 = (bf16[4,144,128]{2,1,0:T(8,128)(2,1)S(1)}, bf16[4,144,128]{2,1,0:T(8,128)(2,1)S(1)}, u32[]{:S(2)}, u32[]{:S(2)}) collective-permute-start(bf16[4,144,128]{2,1,0:T(8,128)(2,1)S(1)} %get-tuple-element.40), channel_id=1, source_target_pairs={{0,4},{4,0},{8,12},{12,8},{16,20},{20,16},{24,28},{28,24},{1,5},{5... | collective-permute-start | bytes 442376 | tf_op jit(solution)/shard_map/ppermute | solution.py:342
  29.5 0.1 merge.2
  29.6 1.7 %collective-permute-start.8 = (bf16[144,128]{1,0:T(8,128)(2,1)S(1)}, bf16[144,128]{1,0:T(8,128)(2,1)S(1)}, u32[]{:S(2)}, u32[]{:S(2)}) collective-permute-start(bf16[144,128]{1,0:T(8,128)(2,1)S(1)} %get-tuple-element.36), channel_id=1, source_target_pairs={{0,16},{4,20},{8,24},{12,28},{16,0},{20,4},{24,8},{28,12},{1,17},{... | collective-permute-start | bytes 110600 | tf_op jit(solution)/shard_map/ppermute | solution.py:342
  31.3 1.7 %collective-permute-start.9 = (bf16[144,128]{1,0:T(8,128)(2,1)S(1)}, bf16[144,128]{1,0:T(8,128)(2,1)S(1)}, u32[]{:S(2)}, u32[]{:S(2)}) collective-permute-start(bf16[144,128]{1,0:T(8,128)(2,1)S(1)} %get-tuple-element.37), channel_id=1, source_target_pairs={{0,24},{4,28},{8,16},{12,20},{16,8},{20,12},{24,0},{28,4},{1,25},{... | collective-permute-start | bytes 110600 | tf_op jit(solution)/shard_map/ppermute | solution.py:342
  33.0 0.5 collective-permute-start.10
  33.5 0.1 collective-permute-done.11.other_ref
  33.6 0.1 merge.3
  33.8 2.2 %collective-permute-start.12 = (bf16[144,128]{1,0:T(8,128)(2,1)S(1)}, bf16[144,128]{1,0:T(8,128)(2,1)S(1)}, u32[]{:S(2)}, u32[]{:S(2)}) collective-permute-start(bf16[144,128]{1,0:T(8,128)(2,1)S(1)} %get-tuple-element.42), channel_id=1, source_target_pairs={{0,16},{4,20},{8,24},{12,28},{16,0},{20,4},{24,8},{28,12},{1,17},{... | collective-permute-start | bytes 110600 | tf_op jit(solution)/shard_map/ppermute | solution.py:342
  35.9 1.7 %collective-permute-start.13 = (bf16[144,128]{1,0:T(8,128)(2,1)S(1)}, bf16[144,128]{1,0:T(8,128)(2,1)S(1)}, u32[]{:S(2)}, u32[]{:S(2)}) collective-permute-start(bf16[144,128]{1,0:T(8,128)(2,1)S(1)} %get-tuple-element.43), channel_id=1, source_target_pairs={{0,24},{4,28},{8,16},{12,20},{16,8},{20,12},{24,0},{28,4},{1,25},{... | collective-permute-start | bytes 110600 | tf_op jit(solution)/shard_map/ppermute | solution.py:342
  37.6 0.0 collective-permute-done.8.refs_1_
  37.6 0.0 collective-permute-start.14
  37.6 0.0 collective-permute-done.10.refs_3_
  37.6 1.1 %collective-permute-done.12.refs_5_ = bf16[144,128]{1,0:T(8,128)(2,1)S(1)} collective-permute-done((bf16[144,128]{1,0:T(8,128)(2,1)S(1)}, bf16[144,128]{1,0:T(8,128)(2,1)S(1)}, u32[]{:S(2)}, u32[]{:S(2)}) %collective-permute-start.12) | collective-permute-done | bytes 36896 | tf_op jit(solution)/shard_map/ppermute | solution.py:342
  38.7 3.1 %collective-permute-done.13.refs_6_ = bf16[144,128]{1,0:T(8,128)(2,1)S(1)} collective-permute-done((bf16[144,128]{1,0:T(8,128)(2,1)S(1)}, bf16[144,128]{1,0:T(8,128)(2,1)S(1)}, u32[]{:S(2)}, u32[]{:S(2)}) %collective-permute-start.13) | collective-permute-done | bytes 36896 | tf_op jit(solution)/shard_map/ppermute | solution.py:342
  41.8 0.2 collective-permute-done.14.refs_7_
  42.1 2.9 %up_and_far_output.1 = (bf16[4,4,896]{2,1,0:T(4,128)(2,1)S(1)}, f32[8,2048]{1,0:T(8,128)S(1)}) custom-call(bf16[144,128]{1,0:T(8,128)(2,1)S(1)} %get-tuple-element.35.refs_0_, bf16[144,128]{1,0:T(8,128)(2,1)S(1)} %collective-permute-done.8.refs_1_, bf16[144,128]{1,0:T(8,128)(2,1)S(1)} %collective-permute-done.9.refs_2_, ...), custom_call_target="tpu_custom_call" | custom-call | flops 20000000000 | bytes 1048576 | tf_op jit(solution)/shard_map/up_and_far_output/pallas_call | solution.py:407
  44.9 2.1 %near_output.1.own_ref = f32[4,4,896]{2,1,0:T(4,128)S(1)} custom-call(f32[8,2048]{1,0:T(8,128)S(1)} %get-tuple-element.45.values, bf16[2048,7168]{1,0:T(8,128)(2,1)S(1)} %bitcast.5), custom_call_target="tpu_custom_call" | custom-call | flops 20000000000 | bytes 1048576 | tf_op jit(solution)/shard_map/near_output/pallas_call | solution.py:418
  47.1 1.7 %collective-permute-done.15.other_ref = bf16[4,4,896]{2,1,0:T(4,128)(2,1)S(1)} collective-permute-done((bf16[4,4,896]{2,1,0:T(4,128)(2,1)S(1)}, bf16[4,4,896]{2,1,0:T(4,128)(2,1)S(1)}, u32[]{:S(2)}, u32[]{:S(2)}) %collective-permute-start.15) | collective-permute-done | bytes 28704 | tf_op jit(solution)/shard_map/ppermute | solution.py:342
  48.8 1.8 %collective-permute-start.16 = (bf16[4,896]{1,0:T(4,128)(2,1)S(1)}, bf16[4,896]{1,0:T(4,128)(2,1)S(1)}, u32[]{:S(2)}, u32[]{:S(2)}) collective-permute-start(bf16[4,896]{1,0:T(4,128)(2,1)S(1)} %get-tuple-element.48), channel_id=1, source_target_pairs={{0,20},{4,16},{8,28},{12,24},{16,4},{20,0},{24,12},{28,8},{1,21},{... | collective-permute-start | bytes 21512 | tf_op jit(solution)/shard_map/ppermute | solution.py:342
  50.6 1.9 %collective-permute-start.17 = (bf16[4,896]{1,0:T(4,128)(2,1)S(1)}, bf16[4,896]{1,0:T(4,128)(2,1)S(1)}, u32[]{:S(2)}, u32[]{:S(2)}) collective-permute-start(bf16[4,896]{1,0:T(4,128)(2,1)S(1)} %get-tuple-element.49), channel_id=1, source_target_pairs={{0,16},{4,20},{8,24},{12,28},{16,0},{20,4},{24,8},{28,12},{1,17},{... | collective-permute-start | bytes 21512 | tf_op jit(solution)/shard_map/ppermute | solution.py:342
  52.5 0.8 %collective-permute-start.18 = (bf16[4,896]{1,0:T(4,128)(2,1)S(1)}, bf16[4,896]{1,0:T(4,128)(2,1)S(1)}, u32[]{:S(2)}, u32[]{:S(2)}) collective-permute-start(bf16[4,896]{1,0:T(4,128)(2,1)S(1)} %get-tuple-element.50), channel_id=1, source_target_pairs={{0,4},{4,0},{8,12},{12,8},{16,20},{20,16},{24,28},{28,24},{1,5},{5... | collective-permute-start | bytes 21512 | tf_op jit(solution)/shard_map/ppermute | solution.py:342
  53.3 1.0 %collective-permute-done.16.refs_0_ = bf16[4,896]{1,0:T(4,128)(2,1)S(1)} collective-permute-done((bf16[4,896]{1,0:T(4,128)(2,1)S(1)}, bf16[4,896]{1,0:T(4,128)(2,1)S(1)}, u32[]{:S(2)}, u32[]{:S(2)}) %collective-permute-start.16) | collective-permute-done | bytes 7200 | tf_op jit(solution)/shard_map/ppermute | solution.py:342
  54.3 0.8 %collective-permute-done.17.refs_1_ = bf16[4,896]{1,0:T(4,128)(2,1)S(1)} collective-permute-done((bf16[4,896]{1,0:T(4,128)(2,1)S(1)}, bf16[4,896]{1,0:T(4,128)(2,1)S(1)}, u32[]{:S(2)}, u32[]{:S(2)}) %collective-permute-start.17) | collective-permute-done | bytes 7200 | tf_op jit(solution)/shard_map/ppermute | solution.py:342
  55.1 1.0 %collective-permute-done.18.refs_2_ = bf16[4,896]{1,0:T(4,128)(2,1)S(1)} collective-permute-done((bf16[4,896]{1,0:T(4,128)(2,1)S(1)}, bf16[4,896]{1,0:T(4,128)(2,1)S(1)}, u32[]{:S(2)}, u32[]{:S(2)}) %collective-permute-start.18) | collective-permute-done | bytes 7200 | tf_op jit(solution)/shard_map/ppermute | solution.py:342
  56.1 0.6 %sum_output.1 = bf16[2,2,896]{2,1,0:T(2,128)(2,1)} custom-call(f32[4,896]{1,0:T(4,128)S(1)} %get-tuple-element.47.own_ref, bf16[4,896]{1,0:T(4,128)(2,1)S(1)} %collective-permute-done.16.refs_0_, bf16[4,896]{1,0:T(4,128)(2,1)S(1)} %collective-permute-done.17.refs_1_, bf16[4,896]{1,0:T(4,128)(2,1)S(1)} %collective-permute-done.18.refs_2_), custom_call_target="tpu_custom_call" | custom-call | tf_op jit(solution)/shard_map/sum_output/pallas_call | solution.py:433
  (19 shorter events, 0.1 us)
Async XLA Ops:
  1.8 8.4 %collective-permute-start = (bf16[288,128]{1,0:T(8,128)(2,1)S(1)}, bf16[288,128]{1,0:T(8,128)(2,1)S(1)}, u32[]{:S(2)}, u32[]{:S(2)}) collective-permute-start(bf16[288,128]{1,0:T(8,128)(2,1)S(1)} %get-tuple-element.28.refs_0_), channel_id=1, source_target_pairs={{0,8},{4,12},{8,0},{12,4},{16,24},{20,28},{24,16},{28,20},{1,9},{5... | collective-permute-start | bytes 221192 | tf_op jit(solution)/shard_map/ppermute | solution.py:342
  4.9 7.8 %collective-permute-start.1 = (bf16[288,128]{1,0:T(8,128)(2,1)S(1)}, bf16[288,128]{1,0:T(8,128)(2,1)S(1)}, u32[]{:S(2)}, u32[]{:S(2)}) collective-permute-start(bf16[288,128]{1,0:T(8,128)(2,1)S(1)} %get-tuple-element.28.refs_0_), channel_id=1, source_target_pairs={{0,16},{4,20},{8,24},{12,28},{16,0},{20,4},{24,8},{28,12},{1,17},{... | collective-permute-start | bytes 221192 | tf_op jit(solution)/shard_map/ppermute | solution.py:342
  7.5 6.7 %collective-permute-start.2 = (bf16[288,128]{1,0:T(8,128)(2,1)S(1)}, bf16[288,128]{1,0:T(8,128)(2,1)S(1)}, u32[]{:S(2)}, u32[]{:S(2)}) collective-permute-start(bf16[288,128]{1,0:T(8,128)(2,1)S(1)} %get-tuple-element.28.refs_0_), channel_id=1, source_target_pairs={{0,24},{4,28},{8,16},{12,20},{16,8},{20,12},{24,0},{28,4},{1,25},{... | collective-permute-start | bytes 221192 | tf_op jit(solution)/shard_map/ppermute | solution.py:342
  7.5 11.0 %copy-start = (bf16[2,4096,576]{1,2,0:T(8,128)(2,1)S(1)}, bf16[2,4096,576]{1,2,0:T(8,128)(2,1)}, u32[]{:S(2)}) copy-start(bf16[2,4096,576]{1,2,0:T(8,128)(2,1)} %param.11) | copy-start | bytes 28311556
  8.5 6.8 %collective-permute-start.3 = (bf16[288,128]{1,0:T(8,128)(2,1)S(1)}, bf16[288,128]{1,0:T(8,128)(2,1)S(1)}, u32[]{:S(2)}, u32[]{:S(2)}) collective-permute-start(bf16[288,128]{1,0:T(8,128)(2,1)S(1)} %get-tuple-element.30), channel_id=1, source_target_pairs={{0,4},{4,0},{8,12},{12,8},{16,20},{20,16},{24,28},{28,24},{1,5},{5... | collective-permute-start | bytes 221192 | tf_op jit(solution)/shard_map/ppermute | solution.py:342
  10.2 5.0 %collective-permute-start.4 = (bf16[288,128]{1,0:T(8,128)(2,1)S(1)}, bf16[288,128]{1,0:T(8,128)(2,1)S(1)}, u32[]{:S(2)}, u32[]{:S(2)}) collective-permute-start(bf16[288,128]{1,0:T(8,128)(2,1)S(1)} %collective-permute-done.refs_1_), channel_id=1, source_target_pairs={{0,4},{4,0},{8,12},{12,8},{16,20},{20,16},{24,28},{28,24},{1,5},{5... | collective-permute-start | bytes 221192 | tf_op jit(solution)/shard_map/ppermute | solution.py:342
  12.7 4.4 %collective-permute-start.5 = (bf16[288,128]{1,0:T(8,128)(2,1)S(1)}, bf16[288,128]{1,0:T(8,128)(2,1)S(1)}, u32[]{:S(2)}, u32[]{:S(2)}) collective-permute-start(bf16[288,128]{1,0:T(8,128)(2,1)S(1)} %collective-permute-done.1.refs_2_), channel_id=1, source_target_pairs={{0,4},{4,0},{8,12},{12,8},{16,20},{20,16},{24,28},{28,24},{1,5},{5... | collective-permute-start | bytes 221192 | tf_op jit(solution)/shard_map/ppermute | solution.py:342
  14.2 4.4 %collective-permute-start.6 = (bf16[288,128]{1,0:T(8,128)(2,1)S(1)}, bf16[288,128]{1,0:T(8,128)(2,1)S(1)}, u32[]{:S(2)}, u32[]{:S(2)}) collective-permute-start(bf16[288,128]{1,0:T(8,128)(2,1)S(1)} %collective-permute-done.2.refs_3_), channel_id=1, source_target_pairs={{0,4},{4,0},{8,12},{12,8},{16,20},{20,16},{24,28},{28,24},{1,5},{5... | collective-permute-start | bytes 221192 | tf_op jit(solution)/shard_map/ppermute | solution.py:342
  22.8 19.2 %slice-start = ((s8[29360128]{0:T(1024)(128)(4,1)}), s8[4194304]{0:T(1024)(128)(4,1)S(1)}, s32[]{:S(2)}) async-start(s8[29360128]{0:T(1024)(128)(4,1)} %bitcast.4), calls=%async_computation | async-start | bytes 8388608
  22.8 19.2 %slice-start.1 = ((s8[29360128]{0:T(1024)(128)(4,1)}), s8[4194304]{0:T(1024)(128)(4,1)S(1)}, s32[]{:S(2)}) async-start(s8[29360128]{0:T(1024)(128)(4,1)} %bitcast.4), calls=%async_computation.1 | async-start | bytes 8388608
  22.8 19.2 %slice-start.2 = ((s8[29360128]{0:T(1024)(128)(4,1)}), s8[4194304]{0:T(1024)(128)(4,1)S(1)}, s32[]{:S(2)}) async-start(s8[29360128]{0:T(1024)(128)(4,1)} %bitcast.4), calls=%async_computation.2 | async-start | bytes 8388608
  22.8 19.2 %slice-start.3 = ((s8[29360128]{0:T(1024)(128)(4,1)}), s8[4194304]{0:T(1024)(128)(4,1)S(1)}, s32[]{:S(2)}) async-start(s8[29360128]{0:T(1024)(128)(4,1)} %bitcast.4), calls=%async_computation.3 | async-start | bytes 8388608
  22.8 19.2 %slice-start.4 = ((s8[29360128]{0:T(1024)(128)(4,1)}), s8[4194304]{0:T(1024)(128)(4,1)S(1)}, s32[]{:S(2)}) async-start(s8[29360128]{0:T(1024)(128)(4,1)} %bitcast.4), calls=%async_computation.4 | async-start | bytes 8388608
  22.9 19.2 %slice-start.5 = ((s8[29360128]{0:T(1024)(128)(4,1)}), s8[4194304]{0:T(1024)(128)(4,1)S(1)}, s32[]{:S(2)}) async-start(s8[29360128]{0:T(1024)(128)(4,1)} %bitcast.4), calls=%async_computation.5 | async-start | bytes 8388608
  22.9 19.2 %slice-start.6 = ((s8[29360128]{0:T(1024)(128)(4,1)}), s8[4194304]{0:T(1024)(128)(4,1)S(1)}, s32[]{:S(2)}) async-start(s8[29360128]{0:T(1024)(128)(4,1)} %bitcast.4), calls=%async_computation.6 | async-start | bytes 8388608
  22.9 19.2 %copy-start.1 = (bf16[16,512,128]{2,1,0:T(8,128)(2,1)S(1)}, bf16[16,512,128]{2,1,0:T(8,128)(2,1)}, u32[]{:S(2)}) copy-start(bf16[16,512,128]{2,1,0:T(8,128)(2,1)} %refs_8_.1) | copy-start | bytes 6291460
  22.9 6.6 %collective-permute-start.7 = (bf16[4,144,128]{2,1,0:T(8,128)(2,1)S(1)}, bf16[4,144,128]{2,1,0:T(8,128)(2,1)S(1)}, u32[]{:S(2)}, u32[]{:S(2)}) collective-permute-start(bf16[4,144,128]{2,1,0:T(8,128)(2,1)S(1)} %get-tuple-element.34), channel_id=1, source_target_pairs={{0,4},{4,0},{8,12},{12,8},{16,20},{20,16},{24,28},{28,24},{1,5},{5... | collective-permute-start | bytes 442376 | tf_op jit(solution)/shard_map/ppermute | solution.py:342
  28.4 5.2 %collective-permute-start.11 = (bf16[4,144,128]{2,1,0:T(8,128)(2,1)S(1)}, bf16[4,144,128]{2,1,0:T(8,128)(2,1)S(1)}, u32[]{:S(2)}, u32[]{:S(2)}) collective-permute-start(bf16[4,144,128]{2,1,0:T(8,128)(2,1)S(1)} %get-tuple-element.40), channel_id=1, source_target_pairs={{0,4},{4,0},{8,12},{12,8},{16,20},{20,16},{24,28},{28,24},{1,5},{5... | collective-permute-start | bytes 442376 | tf_op jit(solution)/shard_map/ppermute | solution.py:342
  29.6 8.0 %collective-permute-start.8 = (bf16[144,128]{1,0:T(8,128)(2,1)S(1)}, bf16[144,128]{1,0:T(8,128)(2,1)S(1)}, u32[]{:S(2)}, u32[]{:S(2)}) collective-permute-start(bf16[144,128]{1,0:T(8,128)(2,1)S(1)} %get-tuple-element.36), channel_id=1, source_target_pairs={{0,16},{4,20},{8,24},{12,28},{16,0},{20,4},{24,8},{28,12},{1,17},{... | collective-permute-start | bytes 110600 | tf_op jit(solution)/shard_map/ppermute | solution.py:342
  31.3 6.3 %collective-permute-start.9 = (bf16[144,128]{1,0:T(8,128)(2,1)S(1)}, bf16[144,128]{1,0:T(8,128)(2,1)S(1)}, u32[]{:S(2)}, u32[]{:S(2)}) collective-permute-start(bf16[144,128]{1,0:T(8,128)(2,1)S(1)} %get-tuple-element.37), channel_id=1, source_target_pairs={{0,24},{4,28},{8,16},{12,20},{16,8},{20,12},{24,0},{28,4},{1,25},{... | collective-permute-start | bytes 110600 | tf_op jit(solution)/shard_map/ppermute | solution.py:342
  33.0 4.6 %collective-permute-start.10 = (bf16[144,128]{1,0:T(8,128)(2,1)S(1)}, bf16[144,128]{1,0:T(8,128)(2,1)S(1)}, u32[]{:S(2)}, u32[]{:S(2)}) collective-permute-start(bf16[144,128]{1,0:T(8,128)(2,1)S(1)} %get-tuple-element.38), channel_id=1, source_target_pairs={{0,8},{4,12},{8,0},{12,4},{16,24},{20,28},{24,16},{28,20},{1,9},{5... | collective-permute-start | bytes 110600 | tf_op jit(solution)/shard_map/ppermute | solution.py:342
  33.8 4.9 %collective-permute-start.12 = (bf16[144,128]{1,0:T(8,128)(2,1)S(1)}, bf16[144,128]{1,0:T(8,128)(2,1)S(1)}, u32[]{:S(2)}, u32[]{:S(2)}) collective-permute-start(bf16[144,128]{1,0:T(8,128)(2,1)S(1)} %get-tuple-element.42), channel_id=1, source_target_pairs={{0,16},{4,20},{8,24},{12,28},{16,0},{20,4},{24,8},{28,12},{1,17},{... | collective-permute-start | bytes 110600 | tf_op jit(solution)/shard_map/ppermute | solution.py:342
  35.9 5.9 %collective-permute-start.13 = (bf16[144,128]{1,0:T(8,128)(2,1)S(1)}, bf16[144,128]{1,0:T(8,128)(2,1)S(1)}, u32[]{:S(2)}, u32[]{:S(2)}) collective-permute-start(bf16[144,128]{1,0:T(8,128)(2,1)S(1)} %get-tuple-element.43), channel_id=1, source_target_pairs={{0,24},{4,28},{8,16},{12,20},{16,8},{20,12},{24,0},{28,4},{1,25},{... | collective-permute-start | bytes 110600 | tf_op jit(solution)/shard_map/ppermute | solution.py:342
  37.6 4.4 %collective-permute-start.14 = (bf16[144,128]{1,0:T(8,128)(2,1)S(1)}, bf16[144,128]{1,0:T(8,128)(2,1)S(1)}, u32[]{:S(2)}, u32[]{:S(2)}) collective-permute-start(bf16[144,128]{1,0:T(8,128)(2,1)S(1)} %get-tuple-element.44), channel_id=1, source_target_pairs={{0,8},{4,12},{8,0},{12,4},{16,24},{20,28},{24,16},{28,20},{1,9},{5... | collective-permute-start | bytes 110600 | tf_op jit(solution)/shard_map/ppermute | solution.py:342
  44.9 3.9 %collective-permute-start.15 = (bf16[4,4,896]{2,1,0:T(4,128)(2,1)S(1)}, bf16[4,4,896]{2,1,0:T(4,128)(2,1)S(1)}, u32[]{:S(2)}, u32[]{:S(2)}) collective-permute-start(bf16[4,4,896]{2,1,0:T(4,128)(2,1)S(1)} %get-tuple-element.46), channel_id=1, source_target_pairs={{0,8},{4,12},{8,0},{12,4},{16,24},{20,28},{24,16},{28,20},{1,9},{5... | collective-permute-start | bytes 86024 | tf_op jit(solution)/shard_map/ppermute | solution.py:342
  48.8 5.5 %collective-permute-start.16 = (bf16[4,896]{1,0:T(4,128)(2,1)S(1)}, bf16[4,896]{1,0:T(4,128)(2,1)S(1)}, u32[]{:S(2)}, u32[]{:S(2)}) collective-permute-start(bf16[4,896]{1,0:T(4,128)(2,1)S(1)} %get-tuple-element.48), channel_id=1, source_target_pairs={{0,20},{4,16},{8,28},{12,24},{16,4},{20,0},{24,12},{28,8},{1,21},{... | collective-permute-start | bytes 21512 | tf_op jit(solution)/shard_map/ppermute | solution.py:342
  50.6 4.5 %collective-permute-start.17 = (bf16[4,896]{1,0:T(4,128)(2,1)S(1)}, bf16[4,896]{1,0:T(4,128)(2,1)S(1)}, u32[]{:S(2)}, u32[]{:S(2)}) collective-permute-start(bf16[4,896]{1,0:T(4,128)(2,1)S(1)} %get-tuple-element.49), channel_id=1, source_target_pairs={{0,16},{4,20},{8,24},{12,28},{16,0},{20,4},{24,8},{28,12},{1,17},{... | collective-permute-start | bytes 21512 | tf_op jit(solution)/shard_map/ppermute | solution.py:342
  52.5 3.6 %collective-permute-start.18 = (bf16[4,896]{1,0:T(4,128)(2,1)S(1)}, bf16[4,896]{1,0:T(4,128)(2,1)S(1)}, u32[]{:S(2)}, u32[]{:S(2)}) collective-permute-start(bf16[4,896]{1,0:T(4,128)(2,1)S(1)} %get-tuple-element.50), channel_id=1, source_target_pairs={{0,4},{4,0},{8,12},{12,8},{16,20},{20,16},{24,28},{28,24},{1,5},{5... | collective-permute-start | bytes 21512 | tf_op jit(solution)/shard_map/ppermute | solution.py:342
